TPU v7x, 32 devices: a whole 2x2x4 slice. The times are simulated.
32 devices in a mesh: dp: 4 (over y, x), expert: 8 (over z, core).
Axes of the slice: x: 2, y: 2, z: 4, core: 2. Of those that a mesh axis runs over, the one named last changes fastest.
Arguments:
- tokens: bfloat16 [4096, 1280], P(('dp', 'expert')), may hold values from -6 to 6
- cotangent: bfloat16 [4096, 1280], P(('dp', 'expert')), may hold values from -6 to 6
- routes: int32 [4096, 6], P(('dp', 'expert')), may hold values from 0 to 14, all different within a row; in each aligned block of 128 rows (0 to 127, 128 to 255, ...) at most 64 rows name the same one
- expert_at: int32 [16], replicated, may hold values from 0 to 15, each once
- norm1_gain: float32 [1280], replicated, may hold values from 0.5 to 1.5
- w_query: bfloat16 [1280, 1280], replicated, may hold values from -0.15625 to 0.15625
- w_key: bfloat16 [1280, 1280], replicated, may hold values from -0.15625 to 0.15625
- w_value: bfloat16 [1280, 1280], replicated, may hold values from -0.15625 to 0.15625
- w_out: bfloat16 [1280, 1280], replicated, may hold values from -1 to 1
- norm2_gain: float32 [1280], replicated, may hold values from 0.5 to 1.5
- w_router: bfloat16 [1280, 15], replicated, may hold values from -0.078125 to 0.078125
- shared_gate: bfloat16 [1280, 896], replicated, may hold values from -0.15625 to 0.15625
- shared_up: bfloat16 [1280, 896], replicated, may hold values from -0.15625 to 0.15625
- shared_down: bfloat16 [896, 1280], replicated, may hold values from -0.1875 to 0.1875
- routed_gate: bfloat16 [16, 1280, 896], P('expert'), may hold values from -0.15625 to 0.15625
- routed_up: bfloat16 [16, 1280, 896], P('expert'), may hold values from -0.15625 to 0.15625
- routed_down: bfloat16 [16, 896, 1280], P('expert'), may hold values from -0.875 to 0.875
Outputs:
- output: bfloat16 [4096, 1280], P(('dp', 'expert'))
- grad_tokens: float32 [4096, 1280], P(('dp', 'expert'))
- grad_norm1: float32 [1280], P(('dp', 'expert'))
- grad_query: float32 [1280, 1280], P(('dp', 'expert'))
- grad_key: float32 [1280, 1280], P(('dp', 'expert'))
- grad_value: float32 [1280, 1280], P(('dp', 'expert'))
- grad_out: float32 [1280, 1280], P(('dp', 'expert'))
- grad_norm2: float32 [1280], P(('dp', 'expert'))
- grad_router: float32 [1280, 15], P(('dp', 'expert'))
- grad_shared_gate: float32 [1280, 896], P(('dp', 'expert'))
- grad_shared_up: float32 [1280, 896], P(('dp', 'expert'))
- grad_shared_down: float32 [896, 1280], P(('dp', 'expert'))
- grad_routed_gate: float32 [16, 1280, 896], P('expert', 'dp')
- grad_routed_up: float32 [16, 1280, 896], P('expert', 'dp')
- grad_routed_down: float32 [16, 896, 1280], P('expert', 'dp')
Inputs may be any that keep to these rules, and one draw needn't show every extreme that they name: `routes`: each token names 6 different experts. Among the 128 tokens of one device no expert is named more than 64 times, a bound that some block reaches. `expert_at`: each slot holds one expert; every value appears once, and the slot holding the value 15 is empty.
All inputs are finite; a program needn't handle non-finite values.
Results may differ from a plain program's by a relative error of at most 0.015.
Values may be sent and summed in bfloat16 or wider, within the bound.
No kernel may reach another device: no remote copies, remote signals or barrier semaphores. Data moves between devices by JAX's collectives and lax.ppermute only.
A program may use at most 320 MiB of HBM per device.

v0:
```python
import functools
import math

import jax
import jax.numpy as jnp
import numpy as np
from jax import lax
from jax.experimental import pallas as pl
from jax.experimental.pallas import tpu as pltpu
from jax.sharding import PartitionSpec as P

HEADS = 10
HEAD_DIM = 128
TOP = 6
LANES = 128
epsilon = 1e-06
BF = jnp.bfloat16
F32 = jnp.float32
VMEM_LIMIT = 60 * 2**20
COST = 1


def partner(v, axis, mask):
    n = lax.axis_size(axis)
    return lax.ppermute(v, axis, [(i, i ^ mask) for i in range(n)])


def plus(a, b):
    return (a.astype(F32) + b.astype(F32)).astype(BF)


def along_z(v, pairs):
    return lax.ppermute(v, "expert", [(2 * a + c, 2 * b + c) for a, b in pairs for c in (0, 1)])


def gather_z(v):
    n_z = lax.axis_size("expert") // 2
    return [v] + [along_z(v, [((z - k) % n_z, z) for z in range(n_z)]) for k in range(1, n_z)]


def exchange_z(s):
    n_z = lax.axis_size("expert") // 2
    groups = [[2 * z + c for z in range(n_z)] for c in (0, 1)]
    return lax.all_to_all(s, "expert", 0, 0, tiled=True, axis_index_groups=groups)


def total(blocks):
    out = blocks[0].astype(F32)
    for b in blocks[1:]:
        out = out + b.astype(F32)
    return out


def reduce_here(s):
    return total(list(exchange_z(s)))


def rows_for(d, blocks):
    n_dp, n_ex = lax.axis_size("dp"), lax.axis_size("expert")
    rows = d // (n_dp * n_ex)
    n_z = n_ex // 2
    my_dp, my_core = lax.axis_index("dp"), lax.axis_index("expert") % 2
    at = np.arange(len(blocks) * n_z * rows, dtype=np.int32)
    block_dp = jnp.asarray(np.repeat(np.array(blocks, np.int32), n_z * rows)) ^ my_dp
    block = (block_dp * n_z + jnp.asarray(at // rows % n_z)) * 2 + my_core
    source = block * rows + jnp.asarray(at % rows)
    return (source[:, None] == jnp.arange(d, dtype=jnp.int32)[None, :]).astype(BF)


def dot_nn(a, b):
    return lax.dot_general(a, b, (((1,), (0,)), ((), ())), preferred_element_type=F32)


def dot_nt(a, b):
    return lax.dot_general(a, b, (((1,), (1,)), ((), ())), preferred_element_type=F32)


def dot_tn(a, b):
    return lax.dot_general(a, b, (((0,), (0,)), ((), ())), preferred_element_type=F32)


def picks(routes_t, expert, length, capacity):
    hit = jnp.where(routes_t.astype(F32) == expert.astype(F32), 1.0, 0.0)
    member = jnp.sum(hit, 0, keepdims=True)
    a = lax.broadcasted_iota(jnp.int32, (length, length), 0)
    b = lax.broadcasted_iota(jnp.int32, (length, length), 1)
    earlier = jnp.where(a < b, 1.0, 0.0).astype(BF)
    place = dot_nn(jnp.broadcast_to(member, (16, length)).astype(BF), earlier)[:1]
    row = lax.broadcasted_iota(jnp.int32, (capacity, length), 0).astype(F32)
    return jnp.where((place == row) & (member > 0.5), 1.0, 0.0).astype(BF)


def gates_of(x, router, expert, expert_count):
    logits = dot_nn(x, router)
    lane = lax.broadcasted_iota(jnp.int32, logits.shape, 1)
    logits = jnp.where(lane < expert_count, logits, -1e30)
    terms = jnp.exp(logits - jnp.max(logits, -1, keepdims=True))
    probs = terms / jnp.sum(terms, -1, keepdims=True)
    return jnp.sum(jnp.where(lane == expert, probs, 0.0), -1, keepdims=True)


def whole(shape):
    return pl.BlockSpec(shape, lambda *_: (0,) * len(shape))


def prepare_kernel(ids, early_ref, other_ref, down_ref, pick_ref, dh_ref, dy_ref):
    expert = ids[pl.program_id(0)]
    sources = early_ref.shape[0]
    capacity, length = pick_ref.shape[2:]
    for j, ref in enumerate((early_ref, other_ref)):
        for k in range(sources):
            n = j * sources + k
            pick = picks(ref[k, length : length + 16, :length], expert, length, capacity)
            pick_ref[0, n] = pick
            dy_ref[0, n * capacity : (n + 1) * capacity] = dot_nn(pick, ref[k, :length]).astype(BF)
    dh_ref[0] = dot_nt(dy_ref[0], down_ref[0])


def per_slot(*shape):
    return pl.BlockSpec((1,) + shape, lambda s, *_: (s,) + (0,) * len(shape))


def once(shape):
    return pl.BlockSpec(shape, lambda *_: (0,) * len(shape), pipeline_mode=pl.Buffered(1))


def prepare(ids, early, down, capacity):
    sources, length = early[0].shape[0], early[0].shape[1] - 16
    slots, ff, width = down.shape
    rows = 2 * sources * capacity
    return pl.pallas_call(
        prepare_kernel,
        grid_spec=pltpu.PrefetchScalarGridSpec(
            num_scalar_prefetch=1,
            grid=(slots,),
            in_specs=[once(v.shape) for v in early] + [per_slot(ff, width)],
            out_specs=[
                per_slot(2 * sources, capacity, length),
                per_slot(rows, ff),
                per_slot(rows, width),
            ],
        ),
        out_shape=[
            jax.ShapeDtypeStruct((slots, 2 * sources, capacity, length), BF),
            jax.ShapeDtypeStruct((slots, rows, ff), F32),
            jax.ShapeDtypeStruct((slots, rows, width), BF),
        ],
        compiler_params=pltpu.CompilerParams(vmem_limit_bytes=VMEM_LIMIT),
        cost_estimate=pl.CostEstimate(
            flops=int(COST * (4 * slots * rows * width * (ff + length))),
            bytes_accessed=int(COST * (slots * ff * (width * 2 + rows * 4))),
            transcendentals=0,
        ),
        name="prepare",
    )(ids, *early, down)


def experts_kernel(
    expert_count, ids, ns0_ref, ns1_ref, pick_ref, dh_ref, gate_ref, up_ref, router_ref,
    back0_ref, back1_ref, hid_ref, dg_ref, du_ref, rows_ref, row_gate_ref, d_rows_ref, probs_ref,
):
    s = pl.program_id(0)
    slots, total_sources, capacity, length = pick_ref.shape
    sources, _, width = ns0_ref.shape
    expert = ids[s]
    sides = [(ns0_ref, back0_ref), (ns1_ref, back1_ref)]
    for n in range(total_sources):
        ns = sides[n // sources][0][n % sources]
        rows_ref[0, n * capacity : (n + 1) * capacity] = dot_nn(pick_ref[s, n], ns).astype(BF)
    x = rows_ref[0]
    row_gate = gates_of(x, router_ref[...], expert, expert_count)
    row_gate_ref[0] = jnp.broadcast_to(row_gate, row_gate_ref.shape[1:])
    g = dot_nn(x, gate_ref[0])
    u = dot_nn(x, up_ref[0])
    sig = jax.nn.sigmoid(g)
    act = g * sig
    hid = (act * u).astype(BF)
    hid_ref[0] = hid
    raw = dh_ref[0]
    d_gate = jnp.sum(hid.astype(F32) * raw, -1, keepdims=True)
    dh = raw * row_gate
    dg = (dh * u * sig * (1.0 + g * (1.0 - sig))).astype(BF)
    du = (dh * act).astype(BF)
    dg_ref[0] = dg
    du_ref[0] = du
    d_rows_ref[s] = (dot_nt(dg, gate_ref[0]) + dot_nt(du, up_ref[0])).astype(BF)

    @pl.when(s == 0)
    def _():
        probs_ref[...] = jnp.zeros_like(probs_ref)

    parts = probs_ref.shape[2] // length
    row = lax.broadcasted_iota(jnp.int32, (16, length), 0)
    for n in range(total_sources):
        column = d_gate[n * capacity : (n + 1) * capacity]
        token = jnp.sum(pick_ref[s, n].astype(F32) * column, 0, keepdims=True)
        for b in range(parts):
            probs_ref[n, :, b * length : (b + 1) * length] += jnp.where(
                row == expert - 16 * b, token, 0.0
            )

    @pl.when(s == slots - 1)
    def _():
        wide = parts * length
        for n in range(total_sources):
            back, k = sides[n // sources][1], n % sources
            at = slice(n * capacity, (n + 1) * capacity)
            pick = jnp.concatenate([pick_ref[i, n] for i in range(slots)], 0)
            d_rows = jnp.concatenate([d_rows_ref[i, at] for i in range(slots)], 0)
            back[k, :length] = dot_tn(pick, d_rows).astype(BF)
            back[k, length:, :wide] = probs_ref[n].astype(BF)
            if wide < width:
                back[k, length:, wide:] = jnp.zeros((16, width - wide), BF)


def experts(ids, ns, pick, dh, gate, up, router, expert_count):
    sources, length, width = ns[0].shape
    slots, _, capacity, _ = pick.shape
    ff = gate.shape[2]
    rows = 2 * sources * capacity
    wide = -(-expert_count // 16) * length
    back = (sources, length + 16, width)
    return pl.pallas_call(
        functools.partial(experts_kernel, expert_count),
        grid_spec=pltpu.PrefetchScalarGridSpec(
            num_scalar_prefetch=1,
            grid=(slots,),
            in_specs=[
                once(ns[0].shape),
                once(ns[1].shape),
                once(pick.shape),
                per_slot(rows, ff),
                per_slot(width, ff),
                per_slot(width, ff),
                once(router.shape),
            ],
            out_specs=[
                once(back),
                once(back),
                per_slot(rows, ff),
                per_slot(rows, ff),
                per_slot(rows, ff),
                per_slot(rows, width),
                per_slot(rows, LANES),
            ],
            scratch_shapes=[
                pltpu.VMEM((slots, rows, width), BF),
                pltpu.VMEM((2 * sources, 16, wide), F32),
            ],
        ),
        out_shape=[jax.ShapeDtypeStruct(back, BF)] * 2
        + [jax.ShapeDtypeStruct((slots, rows, ff), BF)] * 3
        + [
            jax.ShapeDtypeStruct((slots, rows, width), BF),
            jax.ShapeDtypeStruct((slots, rows, LANES), F32),
        ],
        compiler_params=pltpu.CompilerParams(vmem_limit_bytes=VMEM_LIMIT),
        cost_estimate=pl.CostEstimate(
            flops=int(COST * (8 * slots * rows * width * ff)),
            bytes_accessed=int(COST * (slots * ff * (width * 4 + rows * 6))),
            transcendentals=slots * rows * ff,
        ),
        name="experts",
    )(ids, *ns, pick, dh, gate, up, router)


def combine_kernel(place, hid_ref, row_gate_ref, pick_ref, down_ref, out_ref, scaled_ref):
    s = pl.program_id(0)
    slots, sources, capacity, length = pick_ref.shape
    result = dot_nn(hid_ref[0], down_ref[0]).astype(BF)
    scaled_ref[s] = (result.astype(F32) * row_gate_ref[0, :, :1]).astype(BF)

    @pl.when(s == slots - 1)
    def _():
        for n in range(sources):
            at = slice(n * capacity, (n + 1) * capacity)
            pick = jnp.concatenate([pick_ref[i, n] for i in range(slots)], 0)
            scaled = jnp.concatenate([scaled_ref[i, at] for i in range(slots)], 0)
            out_ref[place[n]] = dot_tn(pick, scaled).astype(BF)


def combine(place, hid, row_gate, pick, down):
    slots, sources, capacity, length = pick.shape
    _, ff, width = down.shape
    rows = sources * capacity
    return pl.pallas_call(
        combine_kernel,
        grid_spec=pltpu.PrefetchScalarGridSpec(
            num_scalar_prefetch=1,
            grid=(slots,),
            in_specs=[per_slot(rows, ff), per_slot(rows, LANES), once(pick.shape), per_slot(ff, width)],
            out_specs=once((sources, length, width)),
            scratch_shapes=[pltpu.VMEM((slots, rows, width), BF)],
        ),
        out_shape=jax.ShapeDtypeStruct((sources, length, width), BF),
        compiler_params=pltpu.CompilerParams(vmem_limit_bytes=VMEM_LIMIT),
        cost_estimate=pl.CostEstimate(
            flops=int(COST * (4 * slots * rows * width * (ff + length))),
            bytes_accessed=int(COST * (slots * ff * (width * 2 + rows * 2))),
            transcendentals=0,
        ),
        name="combine",
    )(place, hid, row_gate, pick, down)


def routed_grads_kernel(first, mine, x_ref, dg_ref, du_ref, hid_ref, row_gate_ref, dy_ref, *outs):
    send_a, send_b, keep = outs
    d_result = (dy_ref[0].astype(F32) * row_gate_ref[0, :, :1]).astype(BF)
    x = x_ref[0]

    def place(value, size, send, start, kept):
        for q in range(4):
            rel = mine[0] ^ q
            second = jnp.where((rel & (3 ^ first)) == 0, 0, 1)
            for ref, at, there in ((send, start, (rel & first) != 0), (keep, kept, (rel & first) == 0)):

                @pl.when(there)
                def _():
                    for c in range(value.shape[1] // LANES):
                        ref[second, at + c * size : at + (c + 1) * size] = value[
                            q * size : (q + 1) * size, c * LANES : (c + 1) * LANES
                        ].astype(BF)

    width, ff = x.shape[1], dg_ref.shape[2]
    wide, part = width // 4, width // 4 * (ff // LANES)
    place(dot_tn(x, dg_ref[0]), wide, send_a, 0, 0)
    place(dot_tn(x, du_ref[0]), wide, send_a, part, part)
    place(dot_tn(hid_ref[0], d_result), ff // 4, send_b, 0, 2 * part)


def routed_grads(slot, first, mine, x, dg, du, hid, row_gate, dy):
    _, rows, width = dy.shape
    ff = dg.shape[2]
    at = lambda c: pl.BlockSpec((1, rows, c), lambda i, _: (slot, 0, 0))
    part = width * ff // 4 // LANES
    shapes = [(2, n * part, LANES) for n in (2, 1, 3)]
    return pl.pallas_call(
        functools.partial(routed_grads_kernel, first),
        grid_spec=pltpu.PrefetchScalarGridSpec(
            num_scalar_prefetch=1,
            grid=(1,),
            in_specs=[at(width), at(ff), at(ff), at(ff), at(LANES), at(width)],
            out_specs=[whole(shape) for shape in shapes],
        ),
        out_shape=[jax.ShapeDtypeStruct(shape, BF) for shape in shapes],
        compiler_params=pltpu.CompilerParams(vmem_limit_bytes=VMEM_LIMIT),
        cost_estimate=pl.CostEstimate(
            flops=int(COST * (12 * rows * width * ff)),
            bytes_accessed=int(COST * (6 * width * ff + 8 * rows * width)),
            transcendentals=0,
        ),
        name="routed_grads",
    )(mine, x, dg, du, hid, row_gate, dy)


def finish_kernel(slots, *refs):
    outs = refs[4 * slots :]
    for s in range(slots):
        keep, got_a, got_b, last = refs[4 * s : 4 * s + 4]

        @pl.when(pl.program_id(0) == s)
        def _():
            start = 0
            for i, out in enumerate(outs):
                size, columns = out.shape[1:]
                for c in range(columns // LANES):
                    at = slice(start, start + size)
                    skip = got_a.shape[1]
                    got = got_a[0, at] if i < 2 else got_b[0, start - skip : start - skip + size]
                    kept = (keep[0, at].astype(F32) + got.astype(F32)).astype(BF)
                    out[0, :, c * LANES : (c + 1) * LANES] = kept.astype(F32) + last[at].astype(F32)
                    start += size


def finish(pieces, shapes):
    slots = len(pieces)
    front = lambda v: pl.BlockSpec((1,) + v.shape[1:], lambda s: (0, 0, 0), pipeline_mode=pl.Buffered(1))
    return pl.pallas_call(
        functools.partial(finish_kernel, slots),
        grid=(slots,),
        in_specs=[front(v) if v.ndim == 3 else once(v.shape) for piece in pieces for v in piece],
        out_specs=[per_slot(*shape) for shape in shapes],
        out_shape=[jax.ShapeDtypeStruct((slots,) + shape, F32) for shape in shapes],
        compiler_params=pltpu.CompilerParams(vmem_limit_bytes=VMEM_LIMIT),
        name="finish",
    )(*(v for piece in pieces for v in piece))


def rotary(length):
    half = HEAD_DIM // 2
    frequencies = np.exp(np.arange(half, dtype=np.float32) * np.float32(-math.log(10000.0) / half))
    angles = np.arange(length, dtype=np.float32)[:, None] * frequencies.astype(np.float32)[None, :]
    cosine, sine = np.cos(angles), np.sin(angles)
    return (
        np.concatenate([cosine, cosine], 1).astype(np.float32),
        np.concatenate([-sine, sine], 1).astype(np.float32),
    )


def turn(x, cosine, sine):
    return x * cosine + pltpu.roll(x, HEAD_DIM // 2, 1) * sine


def causal_probs(q, k):
    scores = dot_nt(q, k) * (1.0 / math.sqrt(HEAD_DIM))
    row = lax.broadcasted_iota(jnp.int32, scores.shape, 0)
    lane = lax.broadcasted_iota(jnp.int32, scores.shape, 1)
    scores = jnp.where(row >= lane, scores, -1e30)
    terms = jnp.exp(scores - jnp.max(scores, -1, keepdims=True))
    return terms / jnp.sum(terms, -1, keepdims=True)


def unit_of(x):
    scale = lax.rsqrt(jnp.mean(x * x, -1, keepdims=True) + epsilon)
    return x * scale, scale


def attention_kernel(
    x_ref, gain1_ref, gain2_ref, cos_ref, sin_ref, wq_ref, wk_ref, wv_ref, wo_ref,
    q_ref, k_ref, v_ref, att_ref, nf_ref, residual_ref, ns_ref,
):
    i = pl.program_id(0)

    @pl.when(i == 0)
    def _():
        x = x_ref[...].astype(F32)
        nf_ref[...] = (unit_of(x)[0] * gain1_ref[...][None]).astype(BF)
        residual_ref[...] = x

    nf = nf_ref[...]
    q_all, k_all, v_all = dot_nn(nf, wq_ref[...]), dot_nn(nf, wk_ref[...]), dot_nn(nf, wv_ref[...])
    cosine, sine = cos_ref[...], sin_ref[...]
    v_ref[...] = v_all.astype(BF)
    for h in range(q_ref.shape[1] // HEAD_DIM):
        at = slice(h * HEAD_DIM, (h + 1) * HEAD_DIM)
        q = turn(q_all[:, at], cosine, sine).astype(BF)
        k = turn(k_all[:, at], cosine, sine).astype(BF)
        q_ref[:, at] = q
        k_ref[:, at] = k
        att_ref[:, at] = dot_nn(causal_probs(q, k).astype(BF), v_all[:, at].astype(BF)).astype(BF)
    residual_ref[...] += dot_nn(att_ref[...], wo_ref[...])

    @pl.when(i == pl.num_programs(0) - 1)
    def _():
        ns_ref[...] = (unit_of(residual_ref[...])[0] * gain2_ref[...][None]).astype(BF)


def attention(x, gain1, gain2, cosine, sine, wq, wk, wv, wo):
    length, width = x.shape
    step = 2 * HEAD_DIM
    columns = lambda rows: pl.BlockSpec((rows, step), lambda i: (0, i))
    low = jax.ShapeDtypeStruct((length, width), BF)
    return pl.pallas_call(
        attention_kernel,
        grid=(width // step,),
        in_specs=[
            whole((length, width)),
            whole((width,)),
            whole((width,)),
            whole(cosine.shape),
            whole(sine.shape),
            columns(width),
            columns(width),
            columns(width),
            pl.BlockSpec((step, width), lambda i: (i, 0)),
        ],
        out_specs=[columns(length)] * 4 + [whole((length, width))] * 3,
        out_shape=[low] * 5 + [jax.ShapeDtypeStruct((length, width), F32), low],
        compiler_params=pltpu.CompilerParams(vmem_limit_bytes=VMEM_LIMIT),
        cost_estimate=pl.CostEstimate(
            flops=int(COST * 8 * length * width * width), bytes_accessed=int(COST * 8 * width * width), transcendentals=0
        ),
        name="attention",
    )(x, gain1, gain2, cosine, sine, wq, wk, wv, wo)


def backward_kernel(
    expert_count,
    x_ref, dy_ref, residual_ref, ns_ref, shared_ref, router_t_ref, gain1_ref, gain2_ref,
    cos_ref, sin_ref, q_ref, k_ref, v_ref, wq_ref, wk_ref, wv_ref, wo_ref, *refs,
):
    parts = refs[0]
    cat_ref, grad_ref, branch_ref, d_res_ref, acc_ref = refs[1:]
    i = pl.program_id(0)
    length, width = x_ref.shape
    step = wq_ref.shape[1]
    here = pl.multiple_of(i * step, step)
    gains = slice(4 * length, 4 * length + 16)

    @pl.when(i == 0)
    def _():
        back = parts[0, :length].astype(F32)
        tail = parts[0, length:].astype(F32)
        for p in range(1, parts.shape[0]):
            back += parts[p, :length].astype(F32)
            tail += parts[p, length:].astype(F32)
        blocks = router_t_ref.shape[0] // 16
        d_probs = jnp.concatenate([tail[:, b * length : (b + 1) * length] for b in range(blocks)], 0)
        logits = dot_nt(router_t_ref[...], ns_ref[...])
        row = lax.broadcasted_iota(jnp.int32, logits.shape, 0)
        logits = jnp.where(row < expert_count, logits, -1e30)
        terms = jnp.exp(logits - jnp.max(logits, 0, keepdims=True))
        probs = terms / jnp.sum(terms, 0, keepdims=True)
        d_logits = probs * (d_probs - jnp.sum(probs * d_probs, 0, keepdims=True))
        d_logits = jnp.where(row < expert_count, d_logits, 0.0).astype(BF)
        cat_ref[4 * length + 16 :] = jnp.zeros((d_logits.shape[0], width), BF)
        cat_ref[4 * length + 16 :, :length] = d_logits
        d_normed = shared_ref[...] + back + dot_tn(d_logits, router_t_ref[...])
        unit, scale = unit_of(residual_ref[...])
        c = d_normed * gain2_ref[...][None]
        gain_row = jnp.sum(d_normed * unit, 0, keepdims=True)
        which = lax.broadcasted_iota(jnp.int32, (16, width), 0)
        cat_ref[gains] = jnp.where(which == 1, gain_row, 0.0).astype(BF)
        d_res = dy_ref[...].astype(F32) + scale * (c - unit * jnp.mean(c * unit, -1, keepdims=True))
        d_res_ref[...] = d_res
        branch_ref[...] = d_res.astype(BF)
        cat_ref[3 * length : 4 * length] = d_res.astype(BF)
        acc_ref[...] = jnp.zeros_like(acc_ref)

    cosine, sine = cos_ref[...], -sin_ref[...]
    att_scale = 1.0 / math.sqrt(HEAD_DIM)
    d_att_all = dot_nt(branch_ref[...], wo_ref[...]).astype(BF)
    d_q, d_k, d_v = [], [], []
    for h in range(step // HEAD_DIM):
        at = slice(h * HEAD_DIM, (h + 1) * HEAD_DIM)
        q, k, v, d_attended = q_ref[:, at], k_ref[:, at], v_ref[:, at], d_att_all[:, at]
        probs = causal_probs(q, k)
        d_att = dot_nt(d_attended, v)
        d_scores = (probs * (d_att - jnp.sum(probs * d_att, -1, keepdims=True))).astype(BF)
        d_q.append(turn(dot_nn(d_scores, k) * att_scale, cosine, sine).astype(BF))
        d_k.append(turn(dot_tn(d_scores, q) * att_scale, cosine, sine).astype(BF))
        d_v.append(dot_tn(probs.astype(BF), d_attended).astype(BF))
    d_q, d_k, d_v = (jnp.concatenate(v, 1) for v in (d_q, d_k, d_v))
    for n, v in enumerate((d_q, d_k, d_v)):
        cat_ref[n * length : (n + 1) * length, pl.ds(here, step)] = v
    acc_ref[...] += dot_nt(d_q, wq_ref[...]) + dot_nt(d_k, wk_ref[...]) + dot_nt(d_v, wv_ref[...])

    @pl.when(i == pl.num_programs(0) - 1)
    def _():
        unit, scale = unit_of(x_ref[...].astype(F32))
        d_normed = acc_ref[...]
        c = d_normed * gain1_ref[...][None]
        gain_row = jnp.sum(d_normed * unit, 0, keepdims=True)
        which = lax.broadcasted_iota(jnp.int32, (16, width), 0)
        cat_ref[gains] = jnp.where(which == 0, gain_row, cat_ref[gains].astype(F32)).astype(BF)
        grad_ref[...] = d_res_ref[...] + scale * (c - unit * jnp.mean(c * unit, -1, keepdims=True))


def backward(
    x, dy, residual, ns, shared, router_t, gain1, gain2, cosine, sine,
    q, k, v, wq, wk, wv, wo, parts, expert_count,
):
    length, width = x.shape
    step = 2 * HEAD_DIM
    columns = lambda rows: pl.BlockSpec((rows, step), lambda i: (0, i))
    tall = whole((length, width))
    return pl.pallas_call(
        functools.partial(backward_kernel, expert_count),
        grid=(width // step,),
        in_specs=[tall] * 5
        + [whole(router_t.shape), whole((width,)), whole((width,))]
        + [whole(cosine.shape)] * 2
        + [columns(length)] * 3
        + [columns(width)] * 3
        + [pl.BlockSpec((step, width), lambda i: (i, 0))]
        + [whole(parts.shape)],
        out_specs=[
            whole((4 * length + 16 + router_t.shape[0], width)),
            tall,
        ],
        scratch_shapes=[
            pltpu.VMEM((length, width), BF),
            pltpu.VMEM((length, width), F32),
            pltpu.VMEM((length, width), F32),
        ],
        out_shape=[
            jax.ShapeDtypeStruct((4 * length + 16 + router_t.shape[0], width), BF),
            jax.ShapeDtypeStruct((length, width), F32),
        ],
        compiler_params=pltpu.CompilerParams(vmem_limit_bytes=VMEM_LIMIT),
        cost_estimate=pl.CostEstimate(
            flops=int(COST * 8 * length * width * width), bytes_accessed=int(COST * 8 * width * width), transcendentals=0
        ),
        name="backward",
    )(
        x, dy, residual, ns, shared, router_t, gain1, gain2, cosine, sine,
        q, k, v, wq, wk, wv, wo, parts,
    )


def call(kernel, name, outs, *args, flops=1):
    return pl.pallas_call(
        kernel,
        in_specs=[pl.BlockSpec(memory_space=pltpu.VMEM)] * len(args),
        out_specs=[pl.BlockSpec(memory_space=pltpu.VMEM)] * len(outs),
        out_shape=[jax.ShapeDtypeStruct(*o) for o in outs],
        compiler_params=pltpu.CompilerParams(vmem_limit_bytes=VMEM_LIMIT),
        cost_estimate=pl.CostEstimate(flops=flops, bytes_accessed=flops, transcendentals=0),
        name=name,
    )(*args)


def shared_kernel(ns_ref, dy_ref, gate_ref, up_ref, down_ref, cat_ref, result_ref, back_ref):
    ns, dy = ns_ref[...], dy_ref[...]
    width, ff = gate_ref.shape
    g = dot_nn(ns, gate_ref[...])
    u = dot_nn(ns, up_ref[...])
    sig = jax.nn.sigmoid(g)
    act = g * sig
    hid = (act * u).astype(BF)
    dh = dot_nt(dy, down_ref[...])
    dg = (dh * u * sig * (1.0 + g * (1.0 - sig))).astype(BF)
    du = (dh * act).astype(BF)
    result_ref[...] = dot_nn(hid, down_ref[...])
    back_ref[...] = dot_nt(dg, gate_ref[...]) + dot_nt(du, up_ref[...])
    for i, v in enumerate((dg, du, hid)):
        cat_ref[:, i * ff : (i + 1) * ff] = v
    cat_ref[:, 3 * ff : 3 * ff + width] = ns
    cat_ref[:, 3 * ff + width :] = dy


def shared_grads_kernel(ff, width, cat_ref, other_ref, order_d_ref, order_f_ref, su_send, su_keep, sd_send, sd_keep):
    pair = jnp.concatenate([cat_ref[...], other_ref[...]], 0)
    ns_t = dot_nt(order_d_ref[...], pair[:, 3 * ff : 3 * ff + width]).astype(BF)
    hid_t = dot_nt(order_f_ref[...], pair[:, 2 * ff : 3 * ff]).astype(BF)
    su = dot_nn(ns_t, pair[:, : 2 * ff]).astype(BF)
    sd = dot_nn(hid_t, pair[:, 3 * ff + width :]).astype(BF)
    for value, send, keep in ((su, su_send, su_keep), (sd, sd_send, sd_keep)):
        n = send.shape[1]
        for i in range(2):
            send[i] = value[i * n : (i + 1) * n]
            keep[i] = value[(2 + i) * n : (3 + i) * n]


def lefts_kernel(at_ns, mine_ref, other_ref, ns_ref, cat_other_ref, order_a_ref, order_b_ref, a_ref, v_ref, o_ref, r_ref):
    width = ns_ref.shape[1]
    join = lambda *v: jnp.concatenate(v, 0)
    sets = lambda i, j: join(mine_ref[i], other_ref[i], mine_ref[j], other_ref[j])
    a_ref[...] = dot_nt(order_a_ref[...], sets(0, 2)).astype(BF)
    v_ref[...] = dot_nt(order_b_ref[...], sets(0, 3)).astype(BF)
    o_ref[...] = dot_nt(order_b_ref[...], sets(1, 4)).astype(BF)
    ns = join(ns_ref[...], cat_other_ref[:, at_ns : at_ns + width], mine_ref[5], other_ref[5])
    r_ref[...] = dot_nt(order_b_ref[...], ns).astype(BF)


def last_grads_kernel(
    length, mine_ref, other_ref, qx_ref, qxo_ref, by_ref, byo_ref, a_ref, v_ref, o_ref, r_ref, order_b_ref,
    a_send, a_keep, b_send, b_keep,
):
    width = mine_ref.shape[1]
    half = a_send.shape[0]
    join = lambda *v: jnp.concatenate(v, 0)

    def put(value, keep, send, columns):
        keep[:, columns] = value[:half].astype(BF)
        send[:, columns] = value[half:].astype(BF)

    for i in range(2):
        at = slice(i * length, (i + 1) * length)
        tokens = join(mine_ref[at], other_ref[at], qx_ref[at], qxo_ref[at])
        put(dot_nn(a_ref[...], tokens), a_keep, a_send, slice(i * width, (i + 1) * width))
        past = slice((2 + i) * length, (3 + i) * length)
        tokens = join(mine_ref[past], other_ref[past], by_ref[at], byo_ref[at])
        left = (v_ref, o_ref)[i]
        put(dot_nn(left[...], tokens), b_keep, b_send, slice(i * width, (i + 1) * width))
    start = 4 * length
    refs = ((mine_ref, start), (other_ref, start), (by_ref, start - 2 * length), (byo_ref, start - 2 * length))
    gains = sum(ref[i : i + 16].astype(F32) for ref, i in refs).astype(BF)
    logits = jnp.concatenate([ref[i + 16 :, :length] for ref, i in refs], 1)
    small = jnp.concatenate(
        [dot_nt(r_ref[...], logits), dot_nt(order_b_ref[...], gains)], 1
    )
    small = jnp.concatenate([small, jnp.zeros((2 * half, LANES - small.shape[1]), F32)], 1)
    put(small, b_keep, b_send, slice(2 * width, 2 * width + LANES))


def after(value, *earlier):
    return lax.optimization_barrier((value, earlier))[0]


def shards(
    tokens,
    cotangent,
    routes,
    expert_at,
    norm1_gain,
    w_query,
    w_key,
    w_value,
    w_out,
    norm2_gain,
    w_router,
    shared_gate,
    shared_up,
    shared_down,
    routed_gate,
    routed_up,
    routed_down,
):
    length, model_width = tokens.shape
    expert_count = w_router.shape[1]
    slot_dev = routed_gate.shape[0]
    n_ex = lax.axis_size("expert")
    n_dp = lax.axis_size("dp")
    capacity = (length * TOP * 5 // (4 * expert_count) + 7) // 8 * 8
    my_dp, my_ex = lax.axis_index("dp"), lax.axis_index("expert")
    n_z = n_ex // 2
    w = model_width
    rows = w // (n_dp * n_ex)
    over_core = lambda v: partner(v, "expert", 1)
    order_d = rows_for(w, (1, 3, 0, 2))
    order_a, order_b = rows_for(w, (0, 2)), rows_for(w, (0, 1))

    routes_t = jnp.pad(routes.T.astype(BF), ((0, 16 - TOP), (0, 0)), constant_values=-1)
    routes_t = jnp.pad(routes_t, ((0, 0), (0, w - length)))
    early = jnp.concatenate([cotangent, routes_t], 0)
    early = exchange_z(jnp.broadcast_to(early[None], (n_z,) + early.shape))
    early_other = over_core(early)
    cosine, sine = (jnp.asarray(t) for t in rotary(length))
    gain1, gain2 = norm1_gain, norm2_gain
    queries, key_rows, value_rows, attended, normed_first, residual, normed_second = attention(
        tokens, gain1, gain2, cosine, sine, w_query, w_key, w_value, w_out
    )
    ff = shared_gate.shape[1]
    from_shared, shared_result, shared_back = call(
        shared_kernel, "shared",
        [((length, 3 * ff + 2 * w), BF), ((length, w), F32), ((length, w), F32)],
        after(normed_second, early), cotangent, shared_gate, shared_up, shared_down,
    )
    my_z, my_core = my_ex // 2, my_ex % 2
    first_x = partner(normed_first, "dp", 1)
    first_y = partner(jnp.stack([normed_first, attended, normed_second]), "dp", 2)
    ns = gather_z(normed_second)
    ns = jnp.stack(ns)
    ns = jnp.concatenate([lax.dynamic_slice_in_dim(ns, (my_z - z) % n_z, 1) for z in range(n_z)])

    from_other = over_core(from_shared)
    part_d, part_f = w // (2 * n_dp), ff // (2 * n_dp)
    su_send, su_keep, sd_send, sd_keep = call(
        functools.partial(shared_grads_kernel, ff, w), "shared_grads",
        [((2, part_d, 2 * ff), BF)] * 2 + [((2, part_f, w), BF)] * 2,
        from_shared, from_other, order_d, rows_for(ff, (2, 3, 0, 1)),
    )
    su_got, sd_got = partner(su_send, "dp", 1), partner(sd_send, "dp", 2)

    my_expert = lax.dynamic_slice_in_dim(expert_at, my_ex * slot_dev, slot_dev)
    router_wide = jnp.pad(w_router, ((0, 0), (0, LANES - expert_count)))
    pick, dh_raw, dy_rows = prepare(my_expert, (early, early_other), routed_down, capacity)
    ns = after(ns, pick, dh_raw, su_send, first_x, first_y)
    ns_other = over_core(ns)
    back_mine, back_other, hid, dg, du, x_rows, row_gate = experts(
        my_expert, (ns, ns_other), pick, dh_raw, routed_gate, routed_up, router_wide, expert_count
    )
    back_sum = plus(back_mine, over_core(back_other))
    dg = after(dg, back_sum)
    back = exchange_z(back_sum)

    lefts = jnp.concatenate([normed_first[None], attended[None], first_x[None], first_y])
    lefts_other = over_core(lefts)
    left_shape = ((w // 4, 4 * length), BF)
    left_a, left_v, left_o, left_r = call(
        functools.partial(lefts_kernel, 3 * ff), "lefts", [left_shape] * 4,
        lefts, lefts_other, normed_second, from_other, order_a, order_b,
    )
    keeps, gots, waiting = [], [], []
    for slot in range(slot_dev):
        first = 1 if slot % 2 == 0 else 2
        send_a, send_b, keep = routed_grads(
            slot, first, my_dp[None], x_rows, dg, du, hid, row_gate, dy_rows
        )
        keeps.append(keep)
        waiting.append(send_b)
        gots.append([partner(send_a, "dp", first)])

    back = after(back, left_a, waiting)
    high = -(-expert_count // 16) * 16
    router_t = jnp.pad(w_router.T, ((0, high - expert_count), (0, 0)))
    d_cat, grad_inputs = backward(
        tokens, cotangent, residual, normed_second, shared_back, router_t, gain1, gain2, cosine, sine,
        queries, key_rows, value_rows, w_query, w_key, w_value, w_out, back, expert_count,
    )

    cat_other = over_core(d_cat)
    qk_x, b_y = partner(d_cat[: 2 * length], "dp", 1), partner(d_cat[2 * length :], "dp", 2)
    place = np.arange(n_z, dtype=np.int32) * 2
    place = jnp.concatenate([place + my_core, place + 1 - my_core])
    combined = combine(place, after(hid, d_cat), row_gate, pick, routed_down)
    combined = lax.psum_scatter(combined, "expert", scatter_dimension=0, tiled=False)
    qk_x_other, b_y_other = over_core(qk_x), over_core(b_y)
    waiting = after(waiting, gots, qk_x, b_y)
    for slot in range(slot_dev):
        gots[slot].append(partner(waiting[slot], "dp", 1 if slot % 2 == 0 else 2))
    a_send, a_keep, b_send, b_keep = call(
        functools.partial(last_grads_kernel, length), "last_grads",
        [((w // 8, 2 * w), BF)] * 2 + [((w // 8, 2 * w + LANES), BF)] * 2,
        d_cat, cat_other, qk_x, qk_x_other, b_y, b_y_other, left_a, left_v, left_o, left_r, order_b,
    )
    part_a, part_b = plus(a_keep, partner(a_send, "dp", 2)), plus(b_keep, partner(b_send, "dp", 1))
    last = jnp.concatenate([part_a, part_b], -1).reshape(n_z, rows, -1)

    gots, su_got, sd_got, combined = after((gots, su_got, sd_got, combined), last)
    output = (residual + shared_result + combined.astype(F32)).astype(BF)
    pieces = []
    for slot, (keep, (got_a, got_b)) in enumerate(zip(keeps, gots)):
        there = plus(keep[1], jnp.concatenate([got_a[1], got_b[1]]))
        pieces.append((keep, got_a, got_b, partner(there, "dp", 2 if slot % 2 == 0 else 1)))
    grad_rgate, grad_rup, grad_rdown = finish(pieces, [(w // n_dp, ff), (w // n_dp, ff), (ff // n_dp, w)])
    su, sd = plus(su_keep, su_got), plus(sd_keep, sd_got)
    su, sd = plus(su[0], partner(su[1], "dp", 2)), plus(sd[0], partner(sd[1], "dp", 1))
    sd = jnp.pad(sd.reshape(n_z, -1, w), ((0, 0), (0, (w - ff) // (n_dp * n_ex)), (0, 0)))
    grad_shared = reduce_here(jnp.concatenate([su.reshape(n_z, rows, -1), sd], -1))
    last = reduce_here(last)
    return (
        output,
        grad_inputs,
        last[:, 4 * w + high],
        last[:, :w],
        last[:, w : 2 * w],
        last[:, 2 * w : 3 * w],
        last[:, 3 * w : 4 * w],
        last[:, 4 * w + high + 1],
        last[:, 4 * w : 4 * w + expert_count],
        grad_shared[:, :ff],
        grad_shared[:, ff : 2 * ff],
        grad_shared[: ff // (n_dp * n_ex), 2 * ff :],
        grad_rgate,
        grad_rup,
        grad_rdown,
    )


def solution(mesh):
    placed = (
        P(("dp", "expert"), None),
        P(("dp", "expert"), None),
        P(("dp", "expert"), None),
        P(),
        P(),
        P(),
        P(),
        P(),
        P(),
        P(),
        P(),
        P(),
        P(),
        P(),
        P("expert", None, None),
        P("expert", None, None),
        P("expert", None, None),
    )
    return jax.shard_map(
        shards,
        mesh=mesh,
        in_specs=placed,
        out_specs=(
            P(("dp", "expert"), None),
            P(("dp", "expert"), None),
            P(("dp", "expert")),
            P(("dp", "expert"), None),
            P(("dp", "expert"), None),
            P(("dp", "expert"), None),
            P(("dp", "expert"), None),
            P(("dp", "expert")),
            P(("dp", "expert"), None),
            P(("dp", "expert"), None),
            P(("dp", "expert"), None),
            P(("dp", "expert"), None),
            P("expert", "dp", None),
            P("expert", "dp", None),
            P("expert", "dp", None),
        ),
        check_vma=False,
    )
```

profile of v0, /device:TPU:0, one launch (start us, length us, event | category | flops | bytes accessed | tf_op | source)
XLA Modules:
  0.0 436.9 jit_solution(17537143128616673223)
XLA Ops:
  10.1 6.3 %all-to-all-start = ((bf16[4,144,1280]{2,1,0:T(8,128)(2,1)}), bf16[4,144,1280]{2,1,0:T(8,128)(2,1)S(1)}, u32[]{:S(2)}, u32[]{:S(2)}) async-start(bf16[4,144,1280]{2,1,0:T(8,128)(2,1)} %broadcast_in_dim.6), calls=%async_computation | async-start | bytes 2949120 | tf_op jit(solution)/shard_map/all_to_all | solution.py:44
  16.4 11.5 %attention.1 = (bf16[128,1280]{1,0:T(8,128)(2,1)}, bf16[128,1280]{1,0:T(8,128)(2,1)}, bf16[128,1280]{1,0:T(8,128)(2,1)}, bf16[128,1280]{1,0:T(8,128)(2,1)}, bf16...) custom-call(bf16[128,1280]{1,0:T(8,128)(2,1)} %x_ref.3, f32[1280]{0:T(1024)} %gain1_ref.3, ...), custom_call_target="tpu_custom_call" | custom-call | flops 1677721600 | bytes 13107200 | tf_op jit(solution)/shard_map/attention/pallas_call | solution.py:453
  28.0 2.1 collective-permute-start
  30.0 2.4 collective-permute-start.1
  33.9 1.5 fusion.2.order_d_ref
  35.4 31.0 %all-to-all-done.early_ref = bf16[4,144,1280]{2,1,0:T(8,128)(2,1)S(1)} async-done(((bf16[4,144,1280]{2,1,0:T(8,128)(2,1)}), bf16[4,144,1280]{2,1,0:T(8,128)(2,1)S(1)}, u32[]{:S(2)}, u32[]{:S(2)}) %all-to-all-start) | async-done | bytes 1474592 | tf_op jit(solution)/shard_map/all_to_all | solution.py:44
  66.4 7.8 %shared.1 = (bf16[128,5248]{1,0:T(8,128)(2,1)}, f32[128,1280]{1,0:T(8,128)}, f32[128,1280]{1,0:T(8,128)}) custom-call(bf16[128,1280]{1,0:T(8,128)(2,1)} %get-tuple-element.74.ns_ref, bf16[128,1280]{1,0:T(8,128)(2,1)} %dy_ref.3, bf16[1280,896]{1,0:T(8,128)(2,1)} %gate_ref.2, bf16[1280,896]{1,0:T(8,128)(2,1)} %up_ref.2, bf16[896,1280]{1,0:T(8,128)(2,1)} %down_ref.3), custom_call_target="tpu_custom_call" | custom-call | flops 1 | bytes 1 | tf_op jit(solution)/shard_map/shared/pallas_call | solution.py:592
  76.0 2.0 pad_maximum_fusion.4
  78.0 1.5 collective-permute-start.5
  79.5 1.5 collective-permute-start.6
  84.8 5.9 %shared_grads.1 = (bf16[2,160,1792]{2,1,0:T(8,128)(2,1)}, bf16[2,160,1792]{2,1,0:T(8,128)(2,1)}, bf16[2,112,1280]{2,1,0:T(8,128)(2,1)}, bf16[2,112,1280]{2,1,0:T(8,128)(2,1)}) custom-call(bf16[128,5248]{1,0:T(8,128)(2,1)} %get-tuple-element.78.cat_ref, bf16[128,5248]{1,0:T(8,128)(2,1)} %copy-done.6, bf16[640,1280]{1,0:T(8,128)(2,1)} %fusion.2.order_d_ref, ...), custom_call_target="tpu_custom_call" | custom-call | flops 1 | bytes 1 | tf_op jit(solution)/shard_map/shared_grads/pallas_call | solution.py:592
  90.7 11.0 %prepare.1 = (bf16[2,8,64,128]{3,2,1,0:T(8,128)(2,1)}, f32[2,512,896]{2,1,0:T(8,128)}, bf16[2,512,1280]{2,1,0:T(8,128)(2,1)}) custom-call(s32[2]{0:T(128)} %dynamic_slice.15.ids, bf16[4,144,1280]{2,1,0:T(8,128)(2,1)} %copy-done.10, bf16[4,144,1280]{2,1,0:T(8,128)(2,1)} %collective-permute-done.3.other_ref, bf16[2,896,1280]{2,1,0:T(8,128)(2,1)} %down_ref.5), custom_call_target="tpu_custom_call" | custom-call | flops 5368709120 | bytes 8257536 | tf_op jit(solution)/shard_map/prepare/pallas_call | solution.py:131
  101.8 1.9 collective-permute-done.6
  104.8 2.1 collective-permute-done.7.ns1_ref
  106.9 22.2 %experts.1 = (bf16[4,144,1280]{2,1,0:T(8,128)(2,1)}, bf16[4,144,1280]{2,1,0:T(8,128)(2,1)}, bf16[2,512,896]{2,1,0:T(8,128)(2,1)}, bf16[2,512,896]{2,1,0:T(8,128)...) custom-call(s32[2]{0:T(128)} %dynamic_slice.15.ids, ...), custom_call_target="tpu_custom_call" | custom-call | flops 9395240960 | bytes 14680064 | tf_op jit(solution)/shard_map/experts/pallas_call | solution.py:223
  129.2 1.7 pad_maximum_fusion.mine_ref
  132.6 1.5 add_convert_fusion
  134.1 3.7 all-to-all-start.1
  139.4 1.5 fusion.4
  140.9 5.7 %lefts.1 = (bf16[320,512]{1,0:T(8,128)(2,1)}, bf16[320,512]{1,0:T(8,128)(2,1)}, bf16[320,512]{1,0:T(8,128)(2,1)}, bf16[320,512]{1,0:T(8,128)(2,1)}) custom-call(bf16[6,128,1280]{2,1,0:T(8,128)(2,1)} %copy-done.1, bf16[6,128,1280]{2,1,0:T(8,128)(2,1)} %collective-permute-done.11.other_ref, bf16[128,1280]{1,0:T(8,128)(2,1)} %get-tuple-element.74.ns_ref, ...), custom_call_target="tpu_custom_call" | custom-call | flops 1 | bytes 1 | tf_op jit(solution)/shard_map/lefts/pallas_call | solution.py:592
  146.6 11.2 %routed_grads.3 = (bf16[2,4480,128]{2,1,0:T(8,128)(2,1)}, bf16[2,2240,128]{2,1,0:T(8,128)(2,1)}, bf16[2,6720,128]{2,1,0:T(8,128)(2,1)}) custom-call(s32[1]{0:T(128)} %bitcast.1.mine, bf16[2,512,1280]{2,1,0:T(8,128)(2,1)} %get-tuple-element.83.x_ref, bf16[2,512,896]{2,1,0:T(8,128)(2,1)} %get-tuple-element.87.dg_ref, ...), custom_call_target="tpu_custom_call" | custom-call | flops 7046430720 | bytes 12124160 | tf_op jit(solution)/shard_map/routed_grads/pallas_call | solution.py:337
  157.8 11.5 %routed_grads.2 = (bf16[2,4480,128]{2,1,0:T(8,128)(2,1)}, bf16[2,2240,128]{2,1,0:T(8,128)(2,1)}, bf16[2,6720,128]{2,1,0:T(8,128)(2,1)}) custom-call(s32[1]{0:T(128)} %bitcast.1.mine, bf16[2,512,1280]{2,1,0:T(8,128)(2,1)} %get-tuple-element.83.x_ref, bf16[2,512,896]{2,1,0:T(8,128)(2,1)} %get-tuple-element.87.dg_ref, ...), custom_call_target="tpu_custom_call" | custom-call | flops 7046430720 | bytes 12124160 | tf_op jit(solution)/shard_map/routed_grads/pallas_call | solution.py:337
  169.3 4.0 all-to-all-done.1.refs_0_
  174.5 17.7 %backward.1 = (bf16[544,1280]{1,0:T(8,128)(2,1)}, f32[128,1280]{1,0:T(8,128)}) custom-call(bf16[128,1280]{1,0:T(8,128)(2,1)} %x_ref.3, bf16[128,1280]{1,0:T(8,128)(2,1)} %dy_ref.3, f32[128,1280]{1,0:T(8,128)} %get-tuple-element.72.residual_ref, bf16[128,1280]{1,0:T(8,128)(2,1)} %get-tuple-element.74.ns_ref, f32[128,1280]{1,0:T(8,128)} %get-tuple-element.96.shared_ref, ...), custom_call_target="tpu_custom_call" | custom-call | flops 1677721600 | bytes 13107200 | tf_op jit(solution)/shard_map/backward/pallas_call | solution.py:557
  192.1 8.3 %combine.1 = bf16[8,128,1280]{2,1,0:T(8,128)(2,1)} custom-call(s32[8]{0:T(128)} %pad_add_fusion.place, bf16[2,512,896]{2,1,0:T(8,128)(2,1)} %get-tuple-element.106.hid_ref, f32[2,512,128]{2,1,0:T(8,128)} %get-tuple-element.90.row_gate_ref, bf16[2,8,64,128]{3,2,1,0:T(8,128)(2,1)} %get-tuple-element.76.pick_ref, bf16[2,896,1280]{2,1,0:T(8,128)(2,1)} %down_ref.5), custom_call_target="tpu_custom_call" | custom-call | flops 5368709120 | bytes 6422528 | tf_op jit(solution)/shard_map/combine/pallas_call | solution.py:286
  200.5 1.6 collective-permute-start.10
  204.0 1.6 collective-permute-start.12
  205.6 62.0 %collective-permute-done.13.by_ref = bf16[288,1280]{1,0:T(8,128)(2,1)S(1)} collective-permute-done((bf16[288,1280]{1,0:T(8,128)(2,1)S(1)}, bf16[288,1280]{1,0:T(8,128)(2,1)S(1)}, u32[]{:S(2)}, u32[]{:S(2)}) %collective-permute-start.13) | collective-permute-done | bytes 737312 | tf_op jit(solution)/shard_map/ppermute | solution.py:25
  268.4 2.3 collective-permute-done.19.qxo_ref
  272.3 6.6 %last_grads.1 = (bf16[160,2560]{1,0:T(8,128)(2,1)}, bf16[160,2560]{1,0:T(8,128)(2,1)}, bf16[160,2688]{1,0:T(8,128)(2,1)}, bf16[160,2688]{1,0:T(8,128)(2,1)}) custom-call(bf16[544,1280]{1,0:T(8,128)(2,1)} %get-tuple-element.102.mine_ref, bf16[544,1280]{1,0:T(8,128)(2,1)} %copy-done.12, bf16[256,1280]{1,0:T(8,128)(2,1)} %copy-done.22, ...), custom_call_target="tpu_custom_call" | custom-call | flops 1 | bytes 1 | tf_op jit(solution)/shard_map/last_grads/pallas_call | solution.py:592
  278.9 1.5 collective-permute-start.21
  281.0 1.5 collective-permute-start.16
  283.5 16.7 %collective-permute-done.21 = bf16[160,2560]{1,0:T(8,128)(2,1)S(1)} collective-permute-done((bf16[160,2560]{1,0:T(8,128)(2,1)}, bf16[160,2560]{1,0:T(8,128)(2,1)S(1)}, u32[]{:S(2)}, u32[]{:S(2)}) %collective-permute-start.21) | collective-permute-done | bytes 819232 | tf_op jit(solution)/shard_map/ppermute | solution.py:25
  300.2 1.5 collective-permute-start.15
  304.6 4.4 all-to-all-start.2
  309.0 3.6 collective-permute-done.17
  312.6 14.6 %collective-permute-done.16 = bf16[2,160,1792]{2,1,0:T(8,128)(2,1)S(1)} collective-permute-done((bf16[2,160,1792]{2,1,0:T(8,128)(2,1)}, bf16[2,160,1792]{2,1,0:T(8,128)(2,1)S(1)}, u32[]{:S(2)}, u32[]{:S(2)}) %collective-permute-start.16) | collective-permute-done | bytes 1146912 | tf_op jit(solution)/shard_map/ppermute | solution.py:25
  327.2 23.5 %collective-permute-done.14.refs_2_ = bf16[2,2240,128]{2,1,0:T(8,128)(2,1)S(1)} collective-permute-done((bf16[2,2240,128]{2,1,0:T(8,128)(2,1)}, bf16[2,2240,128]{2,1,0:T(8,128)(2,1)S(1)}, u32[]{:S(2)}, u32[]{:S(2)}) %collective-permute-start.14) | collective-permute-done | bytes 1146912 | tf_op jit(solution)/shard_map/ppermute | solution.py:25
  350.7 2.2 slice_bitcast_fusion
  353.8 1.6 fusion
  358.5 1.5 add_convert_fusion.4
  360.0 1.6 collective-permute-start.24
  361.6 1.6 fusion.1
  364.3 36.0 %collective-permute-done.24 = bf16[112,1280]{1,0:T(8,128)(2,1)S(1)} collective-permute-done((bf16[112,1280]{1,0:T(8,128)(2,1)S(1)}, bf16[112,1280]{1,0:T(8,128)(2,1)S(1)}, u32[]{:S(2)}, u32[]{:S(2)}) %collective-permute-start.24) | collective-permute-done | bytes 286752 | tf_op jit(solution)/shard_map/ppermute | solution.py:25
  401.7 3.5 all-to-all-start.3
  405.2 1.7 add_bitcast_fusion
  410.0 7.6 %finish.1 = (f32[2,320,896]{2,1,0:T(8,128)}, f32[2,320,896]{2,1,0:T(8,128)}, f32[2,224,1280]{2,1,0:T(8,128)}) custom-call(bf16[2,6720,128]{2,1,0:T(8,128)(2,1)} %get-tuple-element.120.refs_0_, bf16[2,4480,128]{2,1,0:T(8,128)(2,1)} %collective-permute-done.9.refs_1_, bf16[2,2240,128]{2,1,0:T(8,128)(2,1)} %copy-done.8, ...), custom_call_target="tpu_custom_call" | custom-call | tf_op jit(solution)/shard_map/finish/pallas_call | solution.py:378
  417.7 10.4 %all-to-all-done.3 = bf16[4,40,3072]{2,1,0:T(8,128)(2,1)S(1)} async-done(((bf16[4,40,3072]{2,1,0:T(8,128)(2,1)}), bf16[4,40,3072]{2,1,0:T(8,128)(2,1)S(1)}, u32[]{:S(2)}, u32[]{:S(2)}) %all-to-all-start.3) | async-done | bytes 983072 | tf_op jit(solution)/shard_map/all_to_all | solution.py:44
  (159 shorter events, 35.4 us)
Async XLA Ops:
  10.1 56.3 %all-to-all-start = ((bf16[4,144,1280]{2,1,0:T(8,128)(2,1)}), bf16[4,144,1280]{2,1,0:T(8,128)(2,1)S(1)}, u32[]{:S(2)}, u32[]{:S(2)}) async-start(bf16[4,144,1280]{2,1,0:T(8,128)(2,1)} %broadcast_in_dim.6), calls=%async_computation | async-start | bytes 2949120 | tf_op jit(solution)/shard_map/all_to_all | solution.py:44
  16.4 17.5 %copy-start.28 = (s32[640]{0:T(1024)S(1)}, s32[640]{0:T(1024)}, u32[]{:S(2)}) copy-start(s32[640]{0:T(1024)} %constant.117.clone) | copy-start | bytes 7684
  16.4 17.5 %copy-start.29 = (s32[640]{0:T(1024)S(1)}, s32[640]{0:T(1024)}, u32[]{:S(2)}) copy-start(s32[640]{0:T(1024)} %constant.118.clone) | copy-start | bytes 7684
  16.4 17.5 %copy-start.30 = (s32[640]{0:T(1024)S(1)}, s32[640]{0:T(1024)}, u32[]{:S(2)}) copy-start(s32[640]{0:T(1024)} %constant.119.clone) | copy-start | bytes 7684
  16.4 49.9 %copy-start.35 = (s32[448]{0:T(512)S(1)}, s32[448]{0:T(512)}, u32[]{:S(2)}) copy-start(s32[448]{0:T(512)} %constant.126.clone) | copy-start | bytes 5380
  16.4 49.9 %copy-start.36 = (s32[448]{0:T(512)S(1)}, s32[448]{0:T(512)}, u32[]{:S(2)}) copy-start(s32[448]{0:T(512)} %constant.127.clone) | copy-start | bytes 5380
  16.4 49.9 %copy-start.37 = (s32[448]{0:T(512)S(1)}, s32[448]{0:T(512)}, u32[]{:S(2)}) copy-start(s32[448]{0:T(512)} %constant.128.clone) | copy-start | bytes 5380
  28.0 50.1 %collective-permute-start = (bf16[128,1280]{1,0:T(8,128)(2,1)}, bf16[128,1280]{1,0:T(8,128)(2,1)}, u32[]{:S(2)}, u32[]{:S(2)}) collective-permute-start(bf16[128,1280]{1,0:T(8,128)(2,1)} %get-tuple-element.74.ns_ref), channel_id=1, source_target_pairs={{6,0},{7,1},{0,2},{1,3},{2,4},{3,5},{4,6},{5,7},{14,8},{15,9},{8,1... | collective-permute-start | bytes 983048 | tf_op jit(solution)/shard_map/ppermute | solution.py:33
  30.0 49.5 %collective-permute-start.1 = (bf16[128,1280]{1,0:T(8,128)(2,1)}, bf16[128,1280]{1,0:T(8,128)(2,1)}, u32[]{:S(2)}, u32[]{:S(2)}) collective-permute-start(bf16[128,1280]{1,0:T(8,128)(2,1)} %get-tuple-element.74.ns_ref), channel_id=1, source_target_pairs={{4,0},{5,1},{6,2},{7,3},{0,4},{1,5},{2,6},{3,7},{12,8},{13,9},{14,... | collective-permute-start | bytes 983048 | tf_op jit(solution)/shard_map/ppermute | solution.py:33
  32.4 48.7 %collective-permute-start.2 = (bf16[128,1280]{1,0:T(8,128)(2,1)}, bf16[128,1280]{1,0:T(8,128)(2,1)}, u32[]{:S(2)}, u32[]{:S(2)}) collective-permute-start(bf16[128,1280]{1,0:T(8,128)(2,1)} %get-tuple-element.74.ns_ref), channel_id=1, source_target_pairs={{2,0},{3,1},{4,2},{5,3},{6,4},{7,5},{0,6},{1,7},{10,8},{11,9},{12,... | collective-permute-start | bytes 983048 | tf_op jit(solution)/shard_map/ppermute | solution.py:33
  66.3 7.9 %copy-start.10 = (bf16[4,144,1280]{2,1,0:T(8,128)(2,1)}, bf16[4,144,1280]{2,1,0:T(8,128)(2,1)S(1)}, u32[]{:S(2)}) copy-start(bf16[4,144,1280]{2,1,0:T(8,128)(2,1)S(1)} %all-to-all-done.early_ref) | copy-start | bytes 4423684
  66.4 24.4 %collective-permute-start.3 = (bf16[4,144,1280]{2,1,0:T(8,128)(2,1)S(1)}, bf16[4,144,1280]{2,1,0:T(8,128)(2,1)}, u32[]{:S(2)}, u32[]{:S(2)}) collective-permute-start(bf16[4,144,1280]{2,1,0:T(8,128)(2,1)S(1)} %all-to-all-done.early_ref), channel_id=1, source_target_pairs={{0,1},{1,0},{2,3},{3,2},{4,5},{5,4},{6,7},{7,6},{8,9},{9,8},{10,11... | collective-permute-start | bytes 4423688 | tf_op jit(solution)/shard_map/ppermute | solution.py:25
  66.4 9.0 %copy-start.39 = (s32[16]{0:T(128)S(1)}, s32[16]{0:T(128)}, u32[]{:S(2)}) copy-start(s32[16]{0:T(128)} %param.36) | copy-start | bytes 196
  66.4 9.6 %copy-start = (bf16[128,1280]{1,0:T(8,128)(2,1)S(1)}, bf16[128,1280]{1,0:T(8,128)(2,1)}, u32[]{:S(2)}) copy-start(bf16[128,1280]{1,0:T(8,128)(2,1)} %get-tuple-element.74.ns_ref) | copy-start | bytes 983044
  66.4 9.6 %copy-start.14 = (bf16[128,1280]{1,0:T(8,128)(2,1)S(1)}, bf16[128,1280]{1,0:T(8,128)(2,1)}, u32[]{:S(2)}) copy-start(bf16[128,1280]{1,0:T(8,128)(2,1)} %get-tuple-element.81) | copy-start | bytes 983044
  74.3 9.5 %collective-permute-start.4 = (bf16[128,5248]{1,0:T(8,128)(2,1)}, bf16[128,5248]{1,0:T(8,128)(2,1)S(1)}, u32[]{:S(2)}, u32[]{:S(2)}) collective-permute-start(bf16[128,5248]{1,0:T(8,128)(2,1)} %get-tuple-element.78.cat_ref), channel_id=1, source_target_pairs={{0,1},{1,0},{2,3},{3,2},{4,5},{5,4},{6,7},{7,6},{8,9},{9,8},{10,11... | collective-permute-start | bytes 4030472 | tf_op jit(solution)/shard_map/ppermute | solution.py:25
  78.0 23.7 %collective-permute-start.5 = (bf16[128,1280]{1,0:T(8,128)(2,1)S(1)}, bf16[128,1280]{1,0:T(8,128)(2,1)S(1)}, u32[]{:S(2)}, u32[]{:S(2)}) collective-permute-start(bf16[128,1280]{1,0:T(8,128)(2,1)S(1)} %copy-done.16), channel_id=1, source_target_pairs={{0,8},{8,0},{16,24},{24,16},{1,9},{9,1},{17,25},{25,17},{2,10},{10... | collective-permute-start | bytes 983048 | tf_op jit(solution)/shard_map/ppermute | solution.py:25
  79.5 24.2 %collective-permute-start.6 = (bf16[3,128,1280]{2,1,0:T(8,128)(2,1)}, bf16[3,128,1280]{2,1,0:T(8,128)(2,1)}, u32[]{:S(2)}, u32[]{:S(2)}) collective-permute-start(bf16[3,128,1280]{2,1,0:T(8,128)(2,1)} %pad_maximum_fusion.4), channel_id=1, source_target_pairs={{0,16},{8,24},{16,0},{24,8},{1,17},{9,25},{17,1},{25,9},{2,18},{10... | collective-permute-start | bytes 2949128 | tf_op jit(solution)/shard_map/ppermute | solution.py:25
  90.7 13.0 %copy-start.13 = (bf16[4,128,1280]{2,1,0:T(8,128)(2,1)S(1)}, bf16[4,128,1280]{2,1,0:T(8,128)(2,1)}, u32[]{:S(2)}) copy-start(bf16[4,128,1280]{2,1,0:T(8,128)(2,1)} %pad_maximum_fusion.3.ns0_ref) | copy-start | bytes 3932164
  90.7 13.0 %copy-start.27 = (bf16[1280,15]{0,1:T(8,128)(2,1)S(1)}, bf16[1280,15]{0,1:T(8,128)(2,1)}, u32[]{:S(2)}) copy-start(bf16[1280,15]{0,1:T(8,128)(2,1)} %param.43) | copy-start | bytes 115204
  101.8 27.3 %copy-start.26 = (bf16[128,1280]{1,0:T(8,128)(2,1)}, bf16[128,1280]{1,0:T(8,128)(2,1)S(1)}, u32[]{:S(2)}) copy-start(bf16[128,1280]{1,0:T(8,128)(2,1)S(1)} %collective-permute-done.5) | copy-start | bytes 983044
  103.7 3.2 collective-permute-start.7
  104.8 24.5 %copy-start.15 = (bf16[128,1280]{1,0:T(8,128)(2,1)S(1)}, bf16[128,1280]{1,0:T(8,128)(2,1)}, u32[]{:S(2)}) copy-start(bf16[128,1280]{1,0:T(8,128)(2,1)} %get-tuple-element.81) | copy-start | bytes 983044
  129.0 3.5 collective-permute-start.8
  130.9 9.9 %collective-permute-start.11 = (bf16[6,128,1280]{2,1,0:T(8,128)(2,1)S(1)}, bf16[6,128,1280]{2,1,0:T(8,128)(2,1)}, u32[]{:S(2)}, u32[]{:S(2)}) collective-permute-start(bf16[6,128,1280]{2,1,0:T(8,128)(2,1)S(1)} %pad_maximum_fusion.mine_ref), channel_id=1, source_target_pairs={{0,1},{1,0},{2,3},{3,2},{4,5},{5,4},{6,7},{7,6},{8,9},{9,8},{10,11... | collective-permute-start | bytes 5898248 | tf_op jit(solution)/shard_map/ppermute | solution.py:25
  134.1 39.1 %all-to-all-start.1 = ((bf16[4,144,1280]{2,1,0:T(8,128)(2,1)}), bf16[4,144,1280]{2,1,0:T(8,128)(2,1)S(1)}, u32[]{:S(2)}, u32[]{:S(2)}) async-start(bf16[4,144,1280]{2,1,0:T(8,128)(2,1)} %add_convert_fusion), calls=%async_computation.1 | async-start | bytes 2949120 | tf_op jit(solution)/shard_map/all_to_all | solution.py:44
  137.9 212.8 %reduce-scatter.2.cloned.1.call-start = ((), (), s32[]{:S(2)}) async-start(), calls=%async_computation.5 | async-start | bytes 2949120 | tf_op jit(solution)/shard_map/reduce_scatter | solution.py:788
  200.5 82.0 %collective-permute-start.10 = (bf16[2,4480,128]{2,1,0:T(8,128)(2,1)}, bf16[2,4480,128]{2,1,0:T(8,128)(2,1)}, u32[]{:S(2)}, u32[]{:S(2)}) collective-permute-start(bf16[2,4480,128]{2,1,0:T(8,128)(2,1)} %get-tuple-element.95), channel_id=1, source_target_pairs={{0,16},{8,24},{16,0},{24,8},{1,17},{9,25},{17,1},{25,9},{2,18},{10... | collective-permute-start | bytes 6881288 | tf_op jit(solution)/shard_map/ppermute | solution.py:25
  202.1 65.5 %collective-permute-start.13 = (bf16[288,1280]{1,0:T(8,128)(2,1)S(1)}, bf16[288,1280]{1,0:T(8,128)(2,1)S(1)}, u32[]{:S(2)}, u32[]{:S(2)}) collective-permute-start(bf16[288,1280]{1,0:T(8,128)(2,1)S(1)} %slice.67), channel_id=1, source_target_pairs={{0,16},{8,24},{16,0},{24,8},{1,17},{9,25},{17,1},{25,9},{2,18},{10... | collective-permute-start | bytes 2211848 | tf_op jit(solution)/shard_map/ppermute | solution.py:25
  203.4 79.6 %collective-permute-start.9 = (bf16[2,4480,128]{2,1,0:T(8,128)(2,1)}, bf16[2,4480,128]{2,1,0:T(8,128)(2,1)}, u32[]{:S(2)}, u32[]{:S(2)}) collective-permute-start(bf16[2,4480,128]{2,1,0:T(8,128)(2,1)} %get-tuple-element.92), channel_id=1, source_target_pairs={{0,8},{8,0},{16,24},{24,16},{1,9},{9,1},{17,25},{25,17},{2,10},{10... | collective-permute-start | bytes 6881288 | tf_op jit(solution)/shard_map/ppermute | solution.py:25
  203.9 66.8 %collective-permute-start.18 = (bf16[544,1280]{1,0:T(8,128)(2,1)S(1)}, bf16[544,1280]{1,0:T(8,128)(2,1)S(1)}, u32[]{:S(2)}, u32[]{:S(2)}) collective-permute-start(bf16[544,1280]{1,0:T(8,128)(2,1)S(1)} %copy-done.5), channel_id=1, source_target_pairs={{0,1},{1,0},{2,3},{3,2},{4,5},{5,4},{6,7},{7,6},{8,9},{9,8},{10,11... | collective-permute-start | bytes 4177928 | tf_op jit(solution)/shard_map/ppermute | solution.py:25
  204.0 64.4 %collective-permute-start.12 = (bf16[256,1280]{1,0:T(8,128)(2,1)S(1)}, bf16[256,1280]{1,0:T(8,128)(2,1)S(1)}, u32[]{:S(2)}, u32[]{:S(2)}) collective-permute-start(bf16[256,1280]{1,0:T(8,128)(2,1)S(1)} %slice.66), channel_id=1, source_target_pairs={{0,8},{8,0},{16,24},{24,16},{1,9},{9,1},{17,25},{25,17},{2,10},{10... | collective-permute-start | bytes 1966088 | tf_op jit(solution)/shard_map/ppermute | solution.py:25
  267.6 3.2 collective-permute-start.20
  268.4 2.3 collective-permute-start.19
  278.9 24.2 %copy-start.18 = (bf16[160,2688]{1,0:T(8,128)(2,1)S(1)}, bf16[160,2688]{1,0:T(8,128)(2,1)}, u32[]{:S(2)}) copy-start(bf16[160,2688]{1,0:T(8,128)(2,1)} %get-tuple-element.112) | copy-start | bytes 2580484
  278.9 21.3 %collective-permute-start.21 = (bf16[160,2560]{1,0:T(8,128)(2,1)}, bf16[160,2560]{1,0:T(8,128)(2,1)S(1)}, u32[]{:S(2)}, u32[]{:S(2)}) collective-permute-start(bf16[160,2560]{1,0:T(8,128)(2,1)} %get-tuple-element.111), channel_id=1, source_target_pairs={{0,16},{8,24},{16,0},{24,8},{1,17},{9,25},{17,1},{25,9},{2,18},{10... | collective-permute-start | bytes 2457608 | tf_op jit(solution)/shard_map/ppermute | solution.py:25
  280.4 22.6 %collective-permute-start.22 = (bf16[160,2688]{1,0:T(8,128)(2,1)}, bf16[160,2688]{1,0:T(8,128)(2,1)S(1)}, u32[]{:S(2)}, u32[]{:S(2)}) collective-permute-start(bf16[160,2688]{1,0:T(8,128)(2,1)} %get-tuple-element.113), channel_id=1, source_target_pairs={{0,8},{8,0},{16,24},{24,16},{1,9},{9,1},{17,25},{25,17},{2,10},{10... | collective-permute-start | bytes 2580488 | tf_op jit(solution)/shard_map/ppermute | solution.py:25
  281.0 46.3 %collective-permute-start.16 = (bf16[2,160,1792]{2,1,0:T(8,128)(2,1)}, bf16[2,160,1792]{2,1,0:T(8,128)(2,1)S(1)}, u32[]{:S(2)}, u32[]{:S(2)}) collective-permute-start(bf16[2,160,1792]{2,1,0:T(8,128)(2,1)} %get-tuple-element.79), channel_id=1, source_target_pairs={{0,8},{8,0},{16,24},{24,16},{1,9},{9,1},{17,25},{25,17},{2,10},{10... | collective-permute-start | bytes 3440648 | tf_op jit(solution)/shard_map/ppermute | solution.py:25
  282.5 30.1 %collective-permute-start.17 = (bf16[2,112,1280]{2,1,0:T(8,128)(2,1)}, bf16[2,112,1280]{2,1,0:T(8,128)(2,1)}, u32[]{:S(2)}, u32[]{:S(2)}) collective-permute-start(bf16[2,112,1280]{2,1,0:T(8,128)(2,1)} %get-tuple-element.105), channel_id=1, source_target_pairs={{0,16},{8,24},{16,0},{24,8},{1,17},{9,25},{17,1},{25,9},{2,18},{10... | collective-permute-start | bytes 1720328 | tf_op jit(solution)/shard_map/ppermute | solution.py:25
  283.0 67.7 %collective-permute-start.14 = (bf16[2,2240,128]{2,1,0:T(8,128)(2,1)}, bf16[2,2240,128]{2,1,0:T(8,128)(2,1)S(1)}, u32[]{:S(2)}, u32[]{:S(2)}) collective-permute-start(bf16[2,2240,128]{2,1,0:T(8,128)(2,1)} %get-tuple-element.103), channel_id=1, source_target_pairs={{0,8},{8,0},{16,24},{24,16},{1,9},{9,1},{17,25},{25,17},{2,10},{10... | collective-permute-start | bytes 3440648 | tf_op jit(solution)/shard_map/ppermute | solution.py:25
  300.2 50.5 %collective-permute-start.15 = (bf16[2,2240,128]{2,1,0:T(8,128)(2,1)}, bf16[2,2240,128]{2,1,0:T(8,128)(2,1)S(1)}, u32[]{:S(2)}, u32[]{:S(2)}) collective-permute-start(bf16[2,2240,128]{2,1,0:T(8,128)(2,1)} %get-tuple-element.104), channel_id=1, source_target_pairs={{0,16},{8,24},{16,0},{24,8},{1,17},{9,25},{17,1},{25,9},{2,18},{10... | collective-permute-start | bytes 3440648 | tf_op jit(solution)/shard_map/ppermute | solution.py:25
  304.6 97.0 %all-to-all-start.2 = ((bf16[4,40,5248]{2,1,0:T(8,128)(2,1)}), bf16[4,40,5248]{2,1,0:T(8,128)(2,1)}, u32[]{:S(2)}, u32[]{:S(2)}) async-start(bf16[4,40,5248]{2,1,0:T(8,128)(2,1)} %bitcast.11), calls=%async_computation.3 | async-start | bytes 3358720 | tf_op jit(solution)/shard_map/all_to_all | solution.py:44
  350.7 6.7 %copy-start.8 = (bf16[2,2240,128]{2,1,0:T(8,128)(2,1)}, bf16[2,2240,128]{2,1,0:T(8,128)(2,1)S(1)}, u32[]{:S(2)}) copy-start(bf16[2,2240,128]{2,1,0:T(8,128)(2,1)S(1)} %collective-permute-done.14.refs_2_) | copy-start | bytes 3440644
  355.5 54.6 %collective-permute-start.26 = (bf16[6720,128]{1,0:T(8,128)(2,1)}, bf16[6720,128]{1,0:T(8,128)(2,1)}, u32[]{:S(2)}, u32[]{:S(2)}) collective-permute-start(bf16[6720,128]{1,0:T(8,128)(2,1)} %fusion), channel_id=1, source_target_pairs={{0,8},{8,0},{16,24},{24,16},{1,9},{9,1},{17,25},{25,17},{2,10},{10... | collective-permute-start | bytes 5160968 | tf_op jit(solution)/shard_map/ppermute | solution.py:25
  357.8 42.6 %collective-permute-start.23 = (bf16[160,1792]{1,0:T(8,128)(2,1)S(1)}, bf16[160,1792]{1,0:T(8,128)(2,1)S(1)}, u32[]{:S(2)}, u32[]{:S(2)}) collective-permute-start(bf16[160,1792]{1,0:T(8,128)(2,1)S(1)} %slice_bitcast_fusion.2), channel_id=1, source_target_pairs={{0,16},{8,24},{16,0},{24,8},{1,17},{9,25},{17,1},{25,9},{2,18},{10... | collective-permute-start | bytes 1720328 | tf_op jit(solution)/shard_map/ppermute | solution.py:25
  360.0 40.3 %collective-permute-start.24 = (bf16[112,1280]{1,0:T(8,128)(2,1)S(1)}, bf16[112,1280]{1,0:T(8,128)(2,1)S(1)}, u32[]{:S(2)}, u32[]{:S(2)}) collective-permute-start(bf16[112,1280]{1,0:T(8,128)(2,1)S(1)} %slice_bitcast_fusion.6), channel_id=1, source_target_pairs={{0,8},{8,0},{16,24},{24,16},{1,9},{9,1},{17,25},{25,17},{2,10},{10... | collective-permute-start | bytes 860168 | tf_op jit(solution)/shard_map/ppermute | solution.py:25
  363.2 46.8 %collective-permute-start.25 = (bf16[6720,128]{1,0:T(8,128)(2,1)}, bf16[6720,128]{1,0:T(8,128)(2,1)}, u32[]{:S(2)}, u32[]{:S(2)}) collective-permute-start(bf16[6720,128]{1,0:T(8,128)(2,1)} %fusion.1), channel_id=1, source_target_pairs={{0,16},{8,24},{16,0},{24,8},{1,17},{9,25},{17,1},{25,9},{2,18},{10... | collective-permute-start | bytes 5160968 | tf_op jit(solution)/shard_map/ppermute | solution.py:25
  401.7 26.4 %all-to-all-start.3 = ((bf16[4,40,3072]{2,1,0:T(8,128)(2,1)}), bf16[4,40,3072]{2,1,0:T(8,128)(2,1)S(1)}, u32[]{:S(2)}, u32[]{:S(2)}) async-start(bf16[4,40,3072]{2,1,0:T(8,128)(2,1)} %fusion.8), calls=%async_computation.4 | async-start | bytes 1966080 | tf_op jit(solution)/shard_map/all_to_all | solution.py:44
  (24 other events, 73.3 us)
Sparse Core Ops, SparseCore 0:
  200.6 35.6 reduce-scatter.1
where the time goes:
time: 443 us; the launch traced here: 437 us
  waiting for transfers between devices  210 us (47%)
  Pallas kernels  127 us (29%)
  starting transfers between devices  42.6 us (10%)
  other arithmetic  26.1 us (6%)
  local copies, waits for them, and re-layouts  16 us (4%)
  between operations  15 us (3%)
    ppermute x24, waiting for transfers between devices, partner(): return lax.ppermute(v, axis, [(i, i ^ mask) for i in range(n)])  165 us
    all_to_all x4, waiting for transfers between devices, exchange_z(): lax.all_to_all(s, 'expert', 0, 0, tiled=True, axis_index_groups=groups)  45.4 us
    pallas_call x4, Pallas kernels, call(): pl.pallas_call(kernel, in_specs=[pl.BlockSpec(memory_space=pltpu.VMEM)] *...  26 us
    pallas_call x2, Pallas kernels, routed_grads(): pl.pallas_call(functools.partial(routed_grads_kernel, first), grid_spec=p...  22.7 us
    pallas_call x1, Pallas kernels, experts(): pl.pallas_call(functools.partial(experts_kernel, expert_count), grid_spec...  22.2 us
    ppermute x24, starting transfers between devices, partner(): return lax.ppermute(v, axis, [(i, i ^ mask) for i in range(n)])  18.6 us
    all_to_all x4, starting transfers between devices, exchange_z(): lax.all_to_all(s, 'expert', 0, 0, tiled=True, axis_index_groups=groups)  17.9 us
    pallas_call x1, Pallas kernels, backward(): pl.pallas_call(functools.partial(backward_kernel, expert_count), grid=(wi...  17.7 us
  transfers between devices with their start and end apart: 32, of which 14 were waited for; matrix products, arithmetic and copies ran while one was open for 7% of the time, Pallas kernels for 18%

commit v1 on v0

--- a/solution.py
+++ b/solution.py
@@ -29,15 +29,6 @@
     return (a.astype(F32) + b.astype(F32)).astype(BF)
 
 
-def along_z(v, pairs):
-    return lax.ppermute(v, "expert", [(2 * a + c, 2 * b + c) for a, b in pairs for c in (0, 1)])
-
-
-def gather_z(v):
-    n_z = lax.axis_size("expert") // 2
-    return [v] + [along_z(v, [((z - k) % n_z, z) for z in range(n_z)]) for k in range(1, n_z)]
-
-
 def exchange_z(s):
     n_z = lax.axis_size("expert") // 2
     groups = [[2 * z + c for z in range(n_z)] for c in (0, 1)]
@@ -49,10 +40,6 @@
     for b in blocks[1:]:
         out = out + b.astype(F32)
     return out
-
-
-def reduce_here(s):
-    return total(list(exchange_z(s)))
 
 
 def rows_for(d, blocks):
@@ -147,8 +134,8 @@
         ],
         compiler_params=pltpu.CompilerParams(vmem_limit_bytes=VMEM_LIMIT),
         cost_estimate=pl.CostEstimate(
-            flops=int(COST * (4 * slots * rows * width * (ff + length))),
-            bytes_accessed=int(COST * (slots * ff * (width * 2 + rows * 4))),
+            flops=1,
+            bytes_accessed=1,
             transcendentals=0,
         ),
         name="prepare",
@@ -303,82 +290,113 @@
     )(place, hid, row_gate, pick, down)
 
 
-def routed_grads_kernel(first, mine, x_ref, dg_ref, du_ref, hid_ref, row_gate_ref, dy_ref, *outs):
-    send_a, send_b, keep = outs
-    d_result = (dy_ref[0].astype(F32) * row_gate_ref[0, :, :1]).astype(BF)
-    x = x_ref[0]
-
-    def place(value, size, send, start, kept):
-        for q in range(4):
-            rel = mine[0] ^ q
-            second = jnp.where((rel & (3 ^ first)) == 0, 0, 1)
-            for ref, at, there in ((send, start, (rel & first) != 0), (keep, kept, (rel & first) == 0)):
-
-                @pl.when(there)
-                def _():
-                    for c in range(value.shape[1] // LANES):
-                        ref[second, at + c * size : at + (c + 1) * size] = value[
-                            q * size : (q + 1) * size, c * LANES : (c + 1) * LANES
-                        ].astype(BF)
-
-    width, ff = x.shape[1], dg_ref.shape[2]
-    wide, part = width // 4, width // 4 * (ff // LANES)
-    place(dot_tn(x, dg_ref[0]), wide, send_a, 0, 0)
-    place(dot_tn(x, du_ref[0]), wide, send_a, part, part)
-    place(dot_tn(hid_ref[0], d_result), ff // 4, send_b, 0, 2 * part)
-
-
-def routed_grads(slot, first, mine, x, dg, du, hid, row_gate, dy):
-    _, rows, width = dy.shape
-    ff = dg.shape[2]
-    at = lambda c: pl.BlockSpec((1, rows, c), lambda i, _: (slot, 0, 0))
-    part = width * ff // 4 // LANES
-    shapes = [(2, n * part, LANES) for n in (2, 1, 3)]
+def routed_grads_kernel(
+    expert_count, slot, ids, x_ref, dg_ref, du_ref, hid_ref, row_gate_ref, dy_ref, ns0_ref, ns1_ref, early0_ref, early1_ref,
+    gate_ref, up_ref, down_ref, router_ref, sel_d_ref, sel_f_ref, send_ref, keep_ref, far_x, far_dy,
+):
+    expert = ids[slot]
+    sources, length, width = ns0_ref.shape
+    rows = far_x.shape[0]
+    capacity = rows // (2 * sources)
+    for j, (ns, early) in enumerate(((ns0_ref, early0_ref), (ns1_ref, early1_ref))):
+        for k in range(sources):
+            pick = picks(early[k, length:, :length], expert, length, capacity)
+            at = slice((j * sources + k) * capacity, (j * sources + k + 1) * capacity)
+            far_x[at] = dot_nn(pick, ns[k]).astype(BF)
+            far_dy[at] = dot_nn(pick, early[k, :length]).astype(BF)
+    x = far_x[...]
+    row_gate = gates_of(x, router_ref[...], expert, expert_count)
+    d_far = (far_dy[...].astype(F32) * row_gate).astype(BF)
+    g = dot_nn(x, gate_ref[0])
+    u = dot_nn(x, up_ref[0])
+    sig = jax.nn.sigmoid(g)
+    act = g * sig
+    hid = (act * u).astype(BF)
+    dh = dot_nt(d_far, down_ref[0])
+    dg = (dh * u * sig * (1.0 + g * (1.0 - sig))).astype(BF)
+    du = (dh * act).astype(BF)
+    x_t = dot_nt(sel_d_ref[...], x).astype(BF)
+    x_own = dot_nt(sel_d_ref[...], x_ref[0]).astype(BF)
+    hid_t = dot_nt(sel_f_ref[...], hid).astype(BF)
+    hid_own = dot_nt(sel_f_ref[...], hid_ref[0]).astype(BF)
+    d_own = (dy_ref[0].astype(F32) * row_gate_ref[0, :, :1]).astype(BF)
+    start = 0
+    for value in (
+        dot_nn(x_own, dg_ref[0]) + dot_nn(x_t, dg),
+        dot_nn(x_own, du_ref[0]) + dot_nn(x_t, du),
+        dot_nn(hid_own, d_own) + dot_nn(hid_t, d_far),
+    ):
+        size = value.shape[0] // 2
+        for c in range(value.shape[1] // LANES):
+            columns = value[:, c * LANES : (c + 1) * LANES].astype(BF)
+            send_ref[start : start + size] = columns[:size]
+            keep_ref[start : start + size] = columns[size:]
+            start += size
+
+
+def routed_grads(slot, second, ids, own, far, weights, router, expert_count):
+    gate, up, down = weights
+    _, rows, width = own[0].shape
+    ff = gate.shape[2]
+    mine = lax.axis_index("dp")
+
+    def selector(size):
+        part = size // 4
+        i = np.arange(part, dtype=np.int32)
+        source = jnp.concatenate([(mine ^ second) * part + i, mine * part + i])
+        return (source[:, None] == jnp.arange(size, dtype=jnp.int32)[None, :]).astype(BF)
+
+    at = lambda v: pl.BlockSpec(
+        (1,) + v.shape[1:], lambda i, _: (slot, 0, 0), pipeline_mode=pl.Buffered(1)
+    )
+    shape = (3 * width * ff // 4 // LANES, LANES)
+    rest = far + [router, selector(width), selector(ff)]
+    rest_specs = [once(v.shape) for v in rest]
     return pl.pallas_call(
-        functools.partial(routed_grads_kernel, first),
+        functools.partial(routed_grads_kernel, expert_count, slot),
         grid_spec=pltpu.PrefetchScalarGridSpec(
             num_scalar_prefetch=1,
             grid=(1,),
-            in_specs=[at(width), at(ff), at(ff), at(ff), at(LANES), at(width)],
-            out_specs=[whole(shape) for shape in shapes],
-        ),
-        out_shape=[jax.ShapeDtypeStruct(shape, BF) for shape in shapes],
+            in_specs=[at(v) for v in own]
+            + rest_specs[: len(far)]
+            + [at(v) for v in weights]
+            + rest_specs[len(far) :],
+            out_specs=[once(shape)] * 2,
+            scratch_shapes=[pltpu.VMEM((rows, width), BF)] * 2,
+        ),
+        out_shape=[jax.ShapeDtypeStruct(shape, BF)] * 2,
         compiler_params=pltpu.CompilerParams(vmem_limit_bytes=VMEM_LIMIT),
         cost_estimate=pl.CostEstimate(
-            flops=int(COST * (12 * rows * width * ff)),
-            bytes_accessed=int(COST * (6 * width * ff + 8 * rows * width)),
+            flops=int(COST * (16 * rows * width * ff)),
+            bytes_accessed=int(COST * (12 * width * ff + 16 * rows * width)),
             transcendentals=0,
         ),
         name="routed_grads",
-    )(mine, x, dg, du, hid, row_gate, dy)
+    )(ids, *own, *far, *weights, *rest[len(far) :])
 
 
 def finish_kernel(slots, *refs):
-    outs = refs[4 * slots :]
+    outs = refs[2 * slots :]
     for s in range(slots):
-        keep, got_a, got_b, last = refs[4 * s : 4 * s + 4]
+        keep, got = refs[2 * s], refs[2 * s + 1]
 
         @pl.when(pl.program_id(0) == s)
         def _():
             start = 0
-            for i, out in enumerate(outs):
+            for out in outs:
                 size, columns = out.shape[1:]
                 for c in range(columns // LANES):
                     at = slice(start, start + size)
-                    skip = got_a.shape[1]
-                    got = got_a[0, at] if i < 2 else got_b[0, start - skip : start - skip + size]
-                    kept = (keep[0, at].astype(F32) + got.astype(F32)).astype(BF)
-                    out[0, :, c * LANES : (c + 1) * LANES] = kept.astype(F32) + last[at].astype(F32)
+                    out[0, :, c * LANES : (c + 1) * LANES] = keep[at].astype(F32) + got[at].astype(F32)
                     start += size
 
 
 def finish(pieces, shapes):
     slots = len(pieces)
-    front = lambda v: pl.BlockSpec((1,) + v.shape[1:], lambda s: (0, 0, 0), pipeline_mode=pl.Buffered(1))
     return pl.pallas_call(
         functools.partial(finish_kernel, slots),
         grid=(slots,),
-        in_specs=[front(v) if v.ndim == 3 else once(v.shape) for piece in pieces for v in piece],
+        in_specs=[once(v.shape) for piece in pieces for v in piece],
         out_specs=[per_slot(*shape) for shape in shapes],
         out_shape=[jax.ShapeDtypeStruct((slots,) + shape, F32) for shape in shapes],
         compiler_params=pltpu.CompilerParams(vmem_limit_bytes=VMEM_LIMIT),
@@ -632,19 +650,15 @@
             keep[i] = value[(2 + i) * n : (3 + i) * n]
 
 
-def lefts_kernel(at_ns, mine_ref, other_ref, ns_ref, cat_other_ref, order_a_ref, order_b_ref, a_ref, v_ref, o_ref, r_ref):
-    width = ns_ref.shape[1]
-    join = lambda *v: jnp.concatenate(v, 0)
-    sets = lambda i, j: join(mine_ref[i], other_ref[i], mine_ref[j], other_ref[j])
+def lefts_kernel(mine_ref, other_ref, order_a_ref, order_b_ref, a_ref, v_ref, o_ref):
+    sets = lambda i, j: jnp.concatenate([mine_ref[i], other_ref[i], mine_ref[j], other_ref[j]], 0)
     a_ref[...] = dot_nt(order_a_ref[...], sets(0, 2)).astype(BF)
     v_ref[...] = dot_nt(order_b_ref[...], sets(0, 3)).astype(BF)
     o_ref[...] = dot_nt(order_b_ref[...], sets(1, 4)).astype(BF)
-    ns = join(ns_ref[...], cat_other_ref[:, at_ns : at_ns + width], mine_ref[5], other_ref[5])
-    r_ref[...] = dot_nt(order_b_ref[...], ns).astype(BF)
 
 
 def last_grads_kernel(
-    length, mine_ref, other_ref, qx_ref, qxo_ref, by_ref, byo_ref, a_ref, v_ref, o_ref, r_ref, order_b_ref,
+    length, mine_ref, other_ref, qx_ref, qxo_ref, by_ref, byo_ref, a_ref, v_ref, o_ref, ns_ref, order_b_ref,
     a_send, a_keep, b_send, b_keep,
 ):
     width = mine_ref.shape[1]
@@ -667,8 +681,9 @@
     refs = ((mine_ref, start), (other_ref, start), (by_ref, start - 2 * length), (byo_ref, start - 2 * length))
     gains = sum(ref[i : i + 16].astype(F32) for ref, i in refs).astype(BF)
     logits = jnp.concatenate([ref[i + 16 :, :length] for ref, i in refs], 1)
+    left_r = dot_nt(order_b_ref[...], ns_ref[...]).astype(BF)
     small = jnp.concatenate(
-        [dot_nt(r_ref[...], logits), dot_nt(order_b_ref[...], gains)], 1
+        [dot_nt(left_r, logits), dot_nt(order_b_ref[...], gains)], 1
     )
     small = jnp.concatenate([small, jnp.zeros((2 * half, LANES - small.shape[1]), F32)], 1)
     put(small, b_keep, b_send, slice(2 * width, 2 * width + LANES))
@@ -713,9 +728,8 @@
 
     routes_t = jnp.pad(routes.T.astype(BF), ((0, 16 - TOP), (0, 0)), constant_values=-1)
     routes_t = jnp.pad(routes_t, ((0, 0), (0, w - length)))
-    early = jnp.concatenate([cotangent, routes_t], 0)
-    early = exchange_z(jnp.broadcast_to(early[None], (n_z,) + early.shape))
-    early_other = over_core(early)
+    spread = lambda v: exchange_z(jnp.broadcast_to(v[None], (n_z,) + v.shape))
+    early = spread(jnp.concatenate([cotangent, routes_t], 0))
     cosine, sine = (jnp.asarray(t) for t in rotary(length))
     gain1, gain2 = norm1_gain, norm2_gain
     queries, key_rows, value_rows, attended, normed_first, residual, normed_second = attention(
@@ -725,15 +739,12 @@
     from_shared, shared_result, shared_back = call(
         shared_kernel, "shared",
         [((length, 3 * ff + 2 * w), BF), ((length, w), F32), ((length, w), F32)],
-        after(normed_second, early), cotangent, shared_gate, shared_up, shared_down,
+        normed_second, cotangent, shared_gate, shared_up, shared_down,
     )
     my_z, my_core = my_ex // 2, my_ex % 2
     first_x = partner(normed_first, "dp", 1)
-    first_y = partner(jnp.stack([normed_first, attended, normed_second]), "dp", 2)
-    ns = gather_z(normed_second)
-    ns = jnp.stack(ns)
-    ns = jnp.concatenate([lax.dynamic_slice_in_dim(ns, (my_z - z) % n_z, 1) for z in range(n_z)])
-
+    first_y = partner(jnp.stack([normed_first, attended]), "dp", 2)
+    ns = spread(after(normed_second, early, from_shared))
     from_other = over_core(from_shared)
     part_d, part_f = w // (2 * n_dp), ff // (2 * n_dp)
     su_send, su_keep, sd_send, sd_keep = call(
@@ -742,37 +753,32 @@
         from_shared, from_other, order_d, rows_for(ff, (2, 3, 0, 1)),
     )
     su_got, sd_got = partner(su_send, "dp", 1), partner(sd_send, "dp", 2)
+    early_other = over_core(early)
+    early_x, early_y = partner(early, "dp", 1), partner(early, "dp", 2)
 
     my_expert = lax.dynamic_slice_in_dim(expert_at, my_ex * slot_dev, slot_dev)
     router_wide = jnp.pad(w_router, ((0, 0), (0, LANES - expert_count)))
     pick, dh_raw, dy_rows = prepare(my_expert, (early, early_other), routed_down, capacity)
-    ns = after(ns, pick, dh_raw, su_send, first_x, first_y)
+    ns = after(ns, pick, dh_raw, early_x, early_y, su_send)
     ns_other = over_core(ns)
+    ns_x, ns_y = partner(ns, "dp", 1), partner(ns, "dp", 2)
     back_mine, back_other, hid, dg, du, x_rows, row_gate = experts(
         my_expert, (ns, ns_other), pick, dh_raw, routed_gate, routed_up, router_wide, expert_count
     )
     back_sum = plus(back_mine, over_core(back_other))
-    dg = after(dg, back_sum)
     back = exchange_z(back_sum)
 
     lefts = jnp.concatenate([normed_first[None], attended[None], first_x[None], first_y])
     lefts_other = over_core(lefts)
     left_shape = ((w // 4, 4 * length), BF)
-    left_a, left_v, left_o, left_r = call(
-        functools.partial(lefts_kernel, 3 * ff), "lefts", [left_shape] * 4,
-        lefts, lefts_other, normed_second, from_other, order_a, order_b,
-    )
-    keeps, gots, waiting = [], [], []
-    for slot in range(slot_dev):
-        first = 1 if slot % 2 == 0 else 2
-        send_a, send_b, keep = routed_grads(
-            slot, first, my_dp[None], x_rows, dg, du, hid, row_gate, dy_rows
-        )
-        keeps.append(keep)
-        waiting.append(send_b)
-        gots.append([partner(send_a, "dp", first)])
-
-    back = after(back, left_a, waiting)
+    left_a, left_v, left_o = call(
+        lefts_kernel, "lefts", [left_shape] * 3, lefts, lefts_other, order_a, order_b,
+    )
+    place = np.arange(n_z, dtype=np.int32) * 2
+    place = jnp.concatenate([place + my_core, place + 1 - my_core])
+    combined_rows = combine(place, after(hid, back_sum), row_gate, pick, routed_down)
+    back = after(back, combined_rows, left_a, su_got, sd_got)
+    combined = lax.psum_scatter(combined_rows, "expert", scatter_dimension=0, tiled=False)
     high = -(-expert_count // 16) * 16
     router_t = jnp.pad(w_router.T, ((0, high - expert_count), (0, 0)))
     d_cat, grad_inputs = backward(
@@ -780,36 +786,50 @@
         queries, key_rows, value_rows, w_query, w_key, w_value, w_out, back, expert_count,
     )
 
+    d_cat = after(d_cat, ns_x, ns_y)
     cat_other = over_core(d_cat)
+    su, sd = plus(su_keep, su_got), plus(sd_keep, sd_got)
+    su_last, sd_last = partner(after(su[1], d_cat), "dp", 2), partner(after(sd[1], d_cat), "dp", 1)
+    su, sd = plus(su[0], su_last), plus(sd[0], sd_last)
     qk_x, b_y = partner(d_cat[: 2 * length], "dp", 1), partner(d_cat[2 * length :], "dp", 2)
-    place = np.arange(n_z, dtype=np.int32) * 2
-    place = jnp.concatenate([place + my_core, place + 1 - my_core])
-    combined = combine(place, after(hid, d_cat), row_gate, pick, routed_down)
-    combined = lax.psum_scatter(combined, "expert", scatter_dimension=0, tiled=False)
+    far_x = [ns_x, over_core(after(ns_x, d_cat)), early_x, over_core(early_x)]
+    far_y = [ns_y, over_core(after(ns_y, d_cat)), early_y, over_core(early_y)]
+
+    def slot_grads(slot, last_dg):
+        return routed_grads(
+            slot, 2 if slot % 2 == 0 else 1, my_expert, [x_rows, last_dg, du, hid, row_gate, dy_rows],
+            far_x if slot % 2 == 0 else far_y, [routed_gate, routed_up, routed_down], router_wide, expert_count,
+        )
+
+    routed = [slot_grads(0, after(dg, d_cat))]
+    qk_x, b_y = after((qk_x, b_y), routed[0])
     qk_x_other, b_y_other = over_core(qk_x), over_core(b_y)
-    waiting = after(waiting, gots, qk_x, b_y)
-    for slot in range(slot_dev):
-        gots[slot].append(partner(waiting[slot], "dp", 1 if slot % 2 == 0 else 2))
+    here = lambda v: lax.dynamic_index_in_dim(v, my_z, 0, keepdims=False)
+    ns_sets = jnp.concatenate(
+        [normed_second, from_other[:, 3 * ff : 3 * ff + w], here(far_y[0]), here(far_y[1])], 0
+    )
     a_send, a_keep, b_send, b_keep = call(
         functools.partial(last_grads_kernel, length), "last_grads",
         [((w // 8, 2 * w), BF)] * 2 + [((w // 8, 2 * w + LANES), BF)] * 2,
-        d_cat, cat_other, qk_x, qk_x_other, b_y, b_y_other, left_a, left_v, left_o, left_r, order_b,
-    )
-    part_a, part_b = plus(a_keep, partner(a_send, "dp", 2)), plus(b_keep, partner(b_send, "dp", 1))
-    last = jnp.concatenate([part_a, part_b], -1).reshape(n_z, rows, -1)
-
-    gots, su_got, sd_got, combined = after((gots, su_got, sd_got, combined), last)
+        d_cat, cat_other, qk_x, qk_x_other, b_y, b_y_other, left_a, left_v, left_o, ns_sets, order_b,
+    )
+    a_got, b_got = partner(a_send, "dp", 2), partner(b_send, "dp", 1)
+
+    routed += [slot_grads(slot, after(dg, a_send)) for slot in range(1, slot_dev)]
+    pieces = [
+        (keep, partner(after(send, a_send), "dp", 2 if slot % 2 == 0 else 1))
+        for slot, (send, keep) in enumerate(routed)
+    ]
+    a_got = after(a_got, routed)
+    last = jnp.concatenate([plus(a_keep, a_got), plus(b_keep, b_got)], -1).reshape(n_z, rows, -1)
+
+    sd = jnp.pad(sd.reshape(n_z, -1, w), ((0, 0), (0, (w - ff) // (n_dp * n_ex)), (0, 0)))
+    grad_shared = exchange_z(after(jnp.concatenate([su.reshape(n_z, rows, -1), sd], -1), d_cat))
+    last = exchange_z(after(last, grad_shared))
+    grad_shared, combined = after((grad_shared, combined), last)
+    last, grad_shared = total(list(last)), total(list(grad_shared))
     output = (residual + shared_result + combined.astype(F32)).astype(BF)
-    pieces = []
-    for slot, (keep, (got_a, got_b)) in enumerate(zip(keeps, gots)):
-        there = plus(keep[1], jnp.concatenate([got_a[1], got_b[1]]))
-        pieces.append((keep, got_a, got_b, partner(there, "dp", 2 if slot % 2 == 0 else 1)))
     grad_rgate, grad_rup, grad_rdown = finish(pieces, [(w // n_dp, ff), (w // n_dp, ff), (ff // n_dp, w)])
-    su, sd = plus(su_keep, su_got), plus(sd_keep, sd_got)
-    su, sd = plus(su[0], partner(su[1], "dp", 2)), plus(sd[0], partner(sd[1], "dp", 1))
-    sd = jnp.pad(sd.reshape(n_z, -1, w), ((0, 0), (0, (w - ff) // (n_dp * n_ex)), (0, 0)))
-    grad_shared = reduce_here(jnp.concatenate([su.reshape(n_z, rows, -1), sd], -1))
-    last = reduce_here(last)
     return (
         output,
         grad_inputs,

time: 443 us -> 345 us (0.78)
  waiting for transfers between devices: 210 us -> 84.3 us
  Pallas kernels: 127 us -> 148 us
    ppermute x24 -> x28, waiting for transfers between devices: 165 us -> 68 us  [partner(): return lax.ppermute(v, axis, [(i, i ^ mask) for i in range(n)])]
    all_to_all x4 -> x5, waiting for transfers between devices: 45.4 us -> 16.3 us  [exchange_z(): lax.all_to_all(s, 'expert', 0, 0, tiled=True, axis_index_groups=groups)]
    pallas_call x2, Pallas kernels: 22.7 us -> 45.5 us  [routed_grads(): pl.pallas_call(functools.partial(routed_grads_kernel, expert_count, slot)...]
    all_to_all x4 -> x5, starting transfers between devices: 17.9 us -> 24.9 us  [exchange_z(): lax.all_to_all(s, 'expert', 0, 0, tiled=True, axis_index_groups=groups)]
    ppermute x3 -> x0, starting transfers between devices: 5.9 us -> none  [along_z(): lax.ppermute(v, 'expert', [(2 * a + c, 2 * b + c) for a, b in pairs for c...]
    convert_element_type x0 -> x4, other arithmetic: none -> 5.45 us  [selector(): (source[:, None] == jnp.arange(size, dtype=jnp.int32)[None, :]).astype(BF)]
    ppermute x24 -> x28, starting transfers between devices: 18.6 us -> 19.2 us  [partner(): return lax.ppermute(v, axis, [(i, i ^ mask) for i in range(n)])]
  transfers between devices with their start and end apart: 32 -> 34, of which waited for: 14 -> 10; matrix products, arithmetic and copies ran while one was open for 7% -> 11% of each run, Pallas kernels for 18% -> 44%
where the time goes in v1:
time: 345 us; the launch traced here: 340 us
  Pallas kernels  148 us (43%)
  waiting for transfers between devices  84.3 us (24%)
  starting transfers between devices  44.1 us (13%)
  other arithmetic  28.3 us (8%)
  local copies, waits for them, and re-layouts  20.3 us (6%)
  between operations  14.7 us (4%)
    ppermute x28, waiting for transfers between devices, partner(): return lax.ppermute(v, axis, [(i, i ^ mask) for i in range(n)])  68 us
    pallas_call x2, Pallas kernels, routed_grads(): pl.pallas_call(functools.partial(routed_grads_kernel, expert_count, slot)...  45.5 us
    pallas_call x4, Pallas kernels, call(): pl.pallas_call(kernel, in_specs=[pl.BlockSpec(memory_space=pltpu.VMEM)] *...  25.5 us
    all_to_all x5, starting transfers between devices, exchange_z(): lax.all_to_all(s, 'expert', 0, 0, tiled=True, axis_index_groups=groups)  24.9 us
    pallas_call x1, Pallas kernels, experts(): pl.pallas_call(functools.partial(experts_kernel, expert_count), grid_spec...  22.4 us
    ppermute x28, starting transfers between devices, partner(): return lax.ppermute(v, axis, [(i, i ^ mask) for i in range(n)])  19.2 us
    pallas_call x1, Pallas kernels, backward(): pl.pallas_call(functools.partial(backward_kernel, expert_count), grid=(wi...  18.2 us
    all_to_all x5, waiting for transfers between devices, exchange_z(): lax.all_to_all(s, 'expert', 0, 0, tiled=True, axis_index_groups=groups)  16.3 us
  transfers between devices with their start and end apart: 34, of which 10 were waited for; matrix products, arithmetic and copies ran while one was open for 11% of the time, Pallas kernels for 44%

profile of v1, /device:TPU:0, one launch (start us, length us, event | category | flops | bytes accessed | tf_op | source)
XLA Modules:
  0.0 339.8 jit_solution(14681662578981934152)
XLA Ops:
  8.9 1.2 broadcast_in_dim.10
  10.1 6.3 %all-to-all-start = ((bf16[4,144,1280]{2,1,0:T(8,128)(2,1)}), bf16[4,144,1280]{2,1,0:T(8,128)(2,1)S(1)}, u32[]{:S(2)}, u32[]{:S(2)}) async-start(bf16[4,144,1280]{2,1,0:T(8,128)(2,1)} %broadcast_in_dim.10), calls=%async_computation | async-start | bytes 2949120 | tf_op jit(solution)/shard_map/all_to_all | solution.py:35
  16.4 11.5 %attention.1 = (bf16[128,1280]{1,0:T(8,128)(2,1)}, bf16[128,1280]{1,0:T(8,128)(2,1)}, bf16[128,1280]{1,0:T(8,128)(2,1)}, bf16[128,1280]{1,0:T(8,128)(2,1)}, bf16...) custom-call(bf16[128,1280]{1,0:T(8,128)(2,1)} %x_ref.3, f32[1280]{0:T(1024)} %gain1_ref.3, ...), custom_call_target="tpu_custom_call" | custom-call | flops 1677721600 | bytes 13107200 | tf_op jit(solution)/shard_map/attention/pallas_call | solution.py:471
  28.0 7.4 %shared.1 = (bf16[128,5248]{1,0:T(8,128)(2,1)}, f32[128,1280]{1,0:T(8,128)}, f32[128,1280]{1,0:T(8,128)}) custom-call(bf16[128,1280]{1,0:T(8,128)(2,1)} %get-tuple-element.85.ns_ref, bf16[128,1280]{1,0:T(8,128)(2,1)} %dy_ref.3, bf16[1280,896]{1,0:T(8,128)(2,1)} %gate_ref.4, bf16[1280,896]{1,0:T(8,128)(2,1)} %up_ref.4, bf16[896,1280]{1,0:T(8,128)(2,1)} %down_ref.5), custom_call_target="tpu_custom_call" | custom-call | flops 1 | bytes 1 | tf_op jit(solution)/shard_map/shared/pallas_call | solution.py:610
  35.4 1.5 collective-permute-start.7
  38.4 1.8 pad.23.router_ref
  40.2 11.1 %all-to-all-done.early_ref = bf16[4,144,1280]{2,1,0:T(8,128)(2,1)S(1)} async-done(((bf16[4,144,1280]{2,1,0:T(8,128)(2,1)}), bf16[4,144,1280]{2,1,0:T(8,128)(2,1)S(1)}, u32[]{:S(2)}, u32[]{:S(2)}) %all-to-all-start) | async-done | bytes 1474592 | tf_op jit(solution)/shard_map/all_to_all | solution.py:35
  51.3 1.3 broadcast_in_dim.11
  52.6 4.7 %all-to-all-start.1 = ((bf16[4,128,1280]{2,1,0:T(8,128)(2,1)}), bf16[4,128,1280]{2,1,0:T(8,128)(2,1)}, u32[]{:S(2)}, u32[]{:S(2)}) async-start(bf16[4,128,1280]{2,1,0:T(8,128)(2,1)} %broadcast_in_dim.11), calls=%async_computation.1 | async-start | bytes 2621440 | tf_op jit(solution)/shard_map/all_to_all | solution.py:35
  58.5 1.5 collective-permute-start.3
  60.0 1.5 collective-permute-start.4
  61.6 1.9 pad_maximum_fusion.3
  64.5 1.5 fusion.order_d_ref
  67.1 6.0 %shared_grads.1 = (bf16[2,160,1792]{2,1,0:T(8,128)(2,1)}, bf16[2,160,1792]{2,1,0:T(8,128)(2,1)}, bf16[2,112,1280]{2,1,0:T(8,128)(2,1)}, bf16[2,112,1280]{2,1,0:T(8,128)(2,1)}) custom-call(bf16[128,5248]{1,0:T(8,128)(2,1)} %get-tuple-element.78.cat_ref, bf16[128,5248]{1,0:T(8,128)(2,1)} %copy-done.9, bf16[640,1280]{1,0:T(8,128)(2,1)} %fusion.order_d_ref, ...), custom_call_target="tpu_custom_call" | custom-call | flops 1 | bytes 1 | tf_op jit(solution)/shard_map/shared_grads/pallas_call | solution.py:610
  73.2 10.7 %prepare.1 = (bf16[2,8,64,128]{3,2,1,0:T(8,128)(2,1)}, f32[2,512,896]{2,1,0:T(8,128)}, bf16[2,512,1280]{2,1,0:T(8,128)(2,1)}) custom-call(s32[2]{0:T(128)} %dynamic_slice.10.ids, bf16[4,144,1280]{2,1,0:T(8,128)(2,1)} %copy-done.2, bf16[4,144,1280]{2,1,0:T(8,128)(2,1)} %collective-permute-done.2.other_ref, bf16[2,896,1280]{2,1,0:T(8,128)(2,1)} %down_ref.9), custom_call_target="tpu_custom_call" | custom-call | flops 1 | bytes 1 | tf_op jit(solution)/shard_map/prepare/pallas_call | solution.py:118
  83.8 9.5 %collective-permute-done.3.early0_ref = bf16[4,144,1280]{2,1,0:T(8,128)(2,1)} collective-permute-done((bf16[4,144,1280]{2,1,0:T(8,128)(2,1)S(1)}, bf16[4,144,1280]{2,1,0:T(8,128)(2,1)}, u32[]{:S(2)}, u32[]{:S(2)}) %collective-permute-start.3) | collective-permute-done | bytes 1474592 | tf_op jit(solution)/shard_map/ppermute | solution.py:25
  93.3 1.9 collective-permute-done.4.early0_ref
  95.3 1.6 fusion.1.sel_d_ref
  96.9 1.6 fusion.2.sel_d_ref
  99.6 22.4 %experts.1 = (bf16[4,144,1280]{2,1,0:T(8,128)(2,1)}, bf16[4,144,1280]{2,1,0:T(8,128)(2,1)}, bf16[2,512,896]{2,1,0:T(8,128)(2,1)}, bf16[2,512,896]{2,1,0:T(8,128)...) custom-call(s32[2]{0:T(128)} %dynamic_slice.10.ids, ...), custom_call_target="tpu_custom_call" | custom-call | flops 9395240960 | bytes 14680064 | tf_op jit(solution)/shard_map/experts/pallas_call | solution.py:210
  126.1 1.6 pad_maximum_fusion.1.mine_ref
  128.3 1.5 collective-permute-start.10
  129.8 1.5 add_convert_fusion
  131.4 5.2 %all-to-all-start.2 = ((bf16[4,144,1280]{2,1,0:T(8,128)(2,1)}), bf16[4,144,1280]{2,1,0:T(8,128)(2,1)S(1)}, u32[]{:S(2)}, u32[]{:S(2)}) async-start(bf16[4,144,1280]{2,1,0:T(8,128)(2,1)} %add_convert_fusion), calls=%async_computation.2 | async-start | bytes 2949120 | tf_op jit(solution)/shard_map/all_to_all | solution.py:35
  137.8 5.9 %collective-permute-done.10 = bf16[2,112,1280]{2,1,0:T(8,128)(2,1)} collective-permute-done((bf16[2,112,1280]{2,1,0:T(8,128)(2,1)}, bf16[2,112,1280]{2,1,0:T(8,128)(2,1)}, u32[]{:S(2)}, u32[]{:S(2)}) %collective-permute-start.10) | collective-permute-done | bytes 573472 | tf_op jit(solution)/shard_map/ppermute | solution.py:25
  143.7 1.4 add_convert_fusion.4
  145.0 1.6 collective-permute-start.11
  146.6 1.5 collective-permute-start.12
  148.9 4.6 %lefts.1 = (bf16[320,512]{1,0:T(8,128)(2,1)}, bf16[320,512]{1,0:T(8,128)(2,1)}, bf16[320,512]{1,0:T(8,128)(2,1)}) custom-call(bf16[5,128,1280]{2,1,0:T(8,128)(2,1)} %copy-done, bf16[5,128,1280]{2,1,0:T(8,128)(2,1)} %collective-permute-done.9.other_ref, bf16[320,1280]{1,0:T(8,128)(2,1)} %fusion.4.order_a_ref, bf16[320,1280]{1,0:T(8,128)(2,1)} %fusion.5.order_b_ref), custom_call_target="tpu_custom_call" | custom-call | flops 1 | bytes 1 | tf_op jit(solution)/shard_map/lefts/pallas_call | solution.py:610
  153.4 2.7 collective-permute-done.1
  156.2 1.9 add_convert_fusion.1
  158.1 8.2 %combine.1 = bf16[8,128,1280]{2,1,0:T(8,128)(2,1)} custom-call(s32[8]{0:T(128)} %pad_add_fusion.4.place, bf16[2,512,896]{2,1,0:T(8,128)(2,1)} %get-tuple-element.92.hid_ref, f32[2,512,128]{2,1,0:T(8,128)} %get-tuple-element.93.row_gate_ref, bf16[2,8,64,128]{3,2,1,0:T(8,128)(2,1)} %get-tuple-element.86.pick_ref, bf16[2,896,1280]{2,1,0:T(8,128)(2,1)} %down_ref.9), custom_call_target="tpu_custom_call" | custom-call | flops 5368709120 | bytes 6422528 | tf_op jit(solution)/shard_map/combine/pallas_call | solution.py:273
  166.3 5.2 %all-to-all-done.2.refs_0_ = bf16[4,144,1280]{2,1,0:T(8,128)(2,1)S(1)} async-done(((bf16[4,144,1280]{2,1,0:T(8,128)(2,1)}), bf16[4,144,1280]{2,1,0:T(8,128)(2,1)S(1)}, u32[]{:S(2)}, u32[]{:S(2)}) %all-to-all-start.2) | async-done | bytes 1474592 | tf_op jit(solution)/shard_map/all_to_all | solution.py:35
  172.6 18.2 %backward.1 = (bf16[544,1280]{1,0:T(8,128)(2,1)}, f32[128,1280]{1,0:T(8,128)}) custom-call(bf16[128,1280]{1,0:T(8,128)(2,1)} %x_ref.3, bf16[128,1280]{1,0:T(8,128)(2,1)} %dy_ref.3, f32[128,1280]{1,0:T(8,128)} %get-tuple-element.75.residual_ref, bf16[128,1280]{1,0:T(8,128)(2,1)} %get-tuple-element.85.ns_ref, f32[128,1280]{1,0:T(8,128)} %get-tuple-element.81.shared_ref, ...), custom_call_target="tpu_custom_call" | custom-call | flops 1677721600 | bytes 13107200 | tf_op jit(solution)/shard_map/backward/pallas_call | solution.py:575
  190.8 1.6 collective-permute-start.14
  197.1 1.8 collective-permute-done.14
  200.7 8.2 %collective-permute-done.13 = bf16[160,1792]{1,0:T(8,128)(2,1)} collective-permute-done((bf16[160,1792]{1,0:T(8,128)(2,1)}, bf16[160,1792]{1,0:T(8,128)(2,1)}, u32[]{:S(2)}, u32[]{:S(2)}) %collective-permute-start.13) | collective-permute-done | bytes 573472 | tf_op jit(solution)/shard_map/ppermute | solution.py:25
  211.2 22.7 %routed_grads.2 = (bf16[6720,128]{1,0:T(8,128)(2,1)}, bf16[6720,128]{1,0:T(8,128)(2,1)}) custom-call(s32[2]{0:T(128)} %dynamic_slice.10.ids, bf16[2,512,1280]{2,1,0:T(8,128)(2,1)} %get-tuple-element.105.x_ref, bf16[2,512,896]{2,1,0:T(8,128)(2,1)} %get-tuple-element.120.dg_ref, bf16[2,512,896]{2,1,0:T(8,128)(2,1)} %get-tuple-element.108.du_ref, ...), custom_call_target="tpu_custom_call" | custom-call | flops 9395240960 | bytes 24248320 | tf_op jit(solution)/shard_map/routed_grads/pallas_call | solution.py:355
  234.5 1.2 fusion.10
  235.7 3.6 %all-to-all-start.3 = ((bf16[4,40,3072]{2,1,0:T(8,128)(2,1)}), bf16[4,40,3072]{2,1,0:T(8,128)(2,1)S(1)}, u32[]{:S(2)}, u32[]{:S(2)}) async-start(bf16[4,40,3072]{2,1,0:T(8,128)(2,1)} %fusion.10), calls=%async_computation.3 | async-start | bytes 1966080 | tf_op jit(solution)/shard_map/all_to_all | solution.py:35
  241.6 7.5 %last_grads.1 = (bf16[160,2560]{1,0:T(8,128)(2,1)}, bf16[160,2560]{1,0:T(8,128)(2,1)}, bf16[160,2688]{1,0:T(8,128)(2,1)}, bf16[160,2688]{1,0:T(8,128)(2,1)}) custom-call(bf16[544,1280]{1,0:T(8,128)(2,1)} %get-tuple-element.100.mine_ref, bf16[544,1280]{1,0:T(8,128)(2,1)} %collective-permute-done.15.other_ref, ...), custom_call_target="tpu_custom_call" | custom-call | flops 1 | bytes 1 | tf_op jit(solution)/shard_map/last_grads/pallas_call | solution.py:610
  249.2 1.5 collective-permute-start.23
  250.7 1.5 collective-permute-start.25
  252.2 22.8 %routed_grads.3 = (bf16[6720,128]{1,0:T(8,128)(2,1)}, bf16[6720,128]{1,0:T(8,128)(2,1)}) custom-call(s32[2]{0:T(128)} %dynamic_slice.10.ids, bf16[2,512,1280]{2,1,0:T(8,128)(2,1)} %get-tuple-element.105.x_ref, bf16[2,512,896]{2,1,0:T(8,128)(2,1)} %get-tuple-element.120.dg_ref, bf16[2,512,896]{2,1,0:T(8,128)(2,1)} %get-tuple-element.108.du_ref, ...), custom_call_target="tpu_custom_call" | custom-call | flops 9395240960 | bytes 24248320 | tf_op jit(solution)/shard_map/routed_grads/pallas_call | solution.py:355
  276.3 1.3 pad_maximum_fusion
  277.6 5.0 %all-to-all-start.4 = ((bf16[4,40,5248]{2,1,0:T(8,128)(2,1)}), bf16[4,40,5248]{2,1,0:T(8,128)(2,1)S(1)}, u32[]{:S(2)}, u32[]{:S(2)}) async-start(bf16[4,40,5248]{2,1,0:T(8,128)(2,1)} %bitcast.13), calls=%async_computation.5 | async-start | bytes 3358720 | tf_op jit(solution)/shard_map/all_to_all | solution.py:35
  283.7 37.7 %collective-permute-done.26.refs_1_ = bf16[6720,128]{1,0:T(8,128)(2,1)} collective-permute-done((bf16[6720,128]{1,0:T(8,128)(2,1)}, bf16[6720,128]{1,0:T(8,128)(2,1)}, u32[]{:S(2)}, u32[]{:S(2)}) %collective-permute-start.26) | collective-permute-done | bytes 1720352 | tf_op jit(solution)/shard_map/ppermute | solution.py:25
  321.6 6.2 %finish.1 = (f32[2,320,896]{2,1,0:T(8,128)}, f32[2,320,896]{2,1,0:T(8,128)}, f32[2,224,1280]{2,1,0:T(8,128)}) custom-call(bf16[6720,128]{1,0:T(8,128)(2,1)} %get-tuple-element.112.refs_0_, bf16[6720,128]{1,0:T(8,128)(2,1)} %collective-permute-done.26.refs_1_, bf16[6720,128]{1,0:T(8,128)(2,1)} %get-tuple-element.122.refs_2_, ...), custom_call_target="tpu_custom_call" | custom-call | tf_op jit(solution)/shard_map/finish/pallas_call | solution.py:396
  (151 shorter events, 34.8 us)
Async XLA Ops:
  10.1 41.2 %all-to-all-start = ((bf16[4,144,1280]{2,1,0:T(8,128)(2,1)}), bf16[4,144,1280]{2,1,0:T(8,128)(2,1)S(1)}, u32[]{:S(2)}, u32[]{:S(2)}) async-start(bf16[4,144,1280]{2,1,0:T(8,128)(2,1)} %broadcast_in_dim.10), calls=%async_computation | async-start | bytes 2949120 | tf_op jit(solution)/shard_map/all_to_all | solution.py:35
  27.9 8.9 %copy-start.16 = (bf16[1280,15]{0,1:T(8,128)(2,1)S(1)}, bf16[1280,15]{0,1:T(8,128)(2,1)}, u32[]{:S(2)}) copy-start(bf16[1280,15]{0,1:T(8,128)(2,1)} %param.47) | copy-start | bytes 115204
  27.9 9.9 %copy-start.29 = (s32[16]{0:T(128)S(1)}, s32[16]{0:T(128)}, u32[]{:S(2)}) copy-start(s32[16]{0:T(128)} %param.40) | copy-start | bytes 196
  27.9 12.2 %copy-start.17 = (s32[640]{0:T(1024)S(1)}, s32[640]{0:T(1024)}, u32[]{:S(2)}) copy-start(s32[640]{0:T(1024)} %constant.106.clone) | copy-start | bytes 7684
  28.0 12.2 %copy-start.18 = (s32[640]{0:T(1024)S(1)}, s32[640]{0:T(1024)}, u32[]{:S(2)}) copy-start(s32[640]{0:T(1024)} %constant.105.clone) | copy-start | bytes 7684
  28.0 12.2 %copy-start.19 = (s32[640]{0:T(1024)S(1)}, s32[640]{0:T(1024)}, u32[]{:S(2)}) copy-start(s32[640]{0:T(1024)} %constant.104.clone) | copy-start | bytes 7684
  28.0 23.3 %copy-start.4 = (bf16[128,1280]{1,0:T(8,128)(2,1)S(1)}, bf16[128,1280]{1,0:T(8,128)(2,1)}, u32[]{:S(2)}) copy-start(bf16[128,1280]{1,0:T(8,128)(2,1)} %get-tuple-element.85.ns_ref) | copy-start | bytes 983044
  35.4 30.7 %collective-permute-start = (bf16[128,5248]{1,0:T(8,128)(2,1)}, bf16[128,5248]{1,0:T(8,128)(2,1)S(1)}, u32[]{:S(2)}, u32[]{:S(2)}) collective-permute-start(bf16[128,5248]{1,0:T(8,128)(2,1)} %get-tuple-element.78.cat_ref), channel_id=1, source_target_pairs={{0,1},{1,0},{2,3},{3,2},{4,5},{5,4},{6,7},{7,6},{8,9},{9,8},{10,11... | collective-permute-start | bytes 4030472 | tf_op jit(solution)/shard_map/ppermute | solution.py:25
  35.4 90.7 %collective-permute-start.7 = (bf16[128,1280]{1,0:T(8,128)(2,1)}, bf16[128,1280]{1,0:T(8,128)(2,1)}, u32[]{:S(2)}, u32[]{:S(2)}) collective-permute-start(bf16[128,1280]{1,0:T(8,128)(2,1)} %get-tuple-element.94), channel_id=1, source_target_pairs={{0,8},{8,0},{16,24},{24,16},{1,9},{9,1},{17,25},{25,17},{2,10},{10... | collective-permute-start | bytes 983048 | tf_op jit(solution)/shard_map/ppermute | solution.py:25
  51.3 8.7 %copy-start.2 = (bf16[4,144,1280]{2,1,0:T(8,128)(2,1)}, bf16[4,144,1280]{2,1,0:T(8,128)(2,1)S(1)}, u32[]{:S(2)}) copy-start(bf16[4,144,1280]{2,1,0:T(8,128)(2,1)S(1)} %all-to-all-done.early_ref) | copy-start | bytes 4423684
  52.5 9.0 %copy-start.20 = (s32[320]{0:T(512)S(1)}, s32[320]{0:T(512)}, u32[]{:S(2)}) copy-start(s32[320]{0:T(512)} %constant.109.clone) | copy-start | bytes 3844
  52.5 9.0 %copy-start.21 = (s32[320]{0:T(512)S(1)}, s32[320]{0:T(512)}, u32[]{:S(2)}) copy-start(s32[320]{0:T(512)} %constant.108.clone) | copy-start | bytes 3844
  52.6 9.0 %copy-start.22 = (s32[320]{0:T(512)S(1)}, s32[320]{0:T(512)}, u32[]{:S(2)}) copy-start(s32[320]{0:T(512)} %constant.110.clone) | copy-start | bytes 3844
  52.6 8.9 %copy-start.23 = (s32[320]{0:T(512)S(1)}, s32[320]{0:T(512)}, u32[]{:S(2)}) copy-start(s32[320]{0:T(512)} %constant.107.clone) | copy-start | bytes 3844
  52.6 9.0 %copy-start.11 = (bf16[128,1280]{1,0:T(8,128)(2,1)S(1)}, bf16[128,1280]{1,0:T(8,128)(2,1)}, u32[]{:S(2)}) copy-start(bf16[128,1280]{1,0:T(8,128)(2,1)} %get-tuple-element.95) | copy-start | bytes 983044
  52.6 42.6 %all-to-all-start.1 = ((bf16[4,128,1280]{2,1,0:T(8,128)(2,1)}), bf16[4,128,1280]{2,1,0:T(8,128)(2,1)}, u32[]{:S(2)}, u32[]{:S(2)}) async-start(bf16[4,128,1280]{2,1,0:T(8,128)(2,1)} %broadcast_in_dim.11), calls=%async_computation.1 | async-start | bytes 2621440 | tf_op jit(solution)/shard_map/all_to_all | solution.py:35
  58.5 14.7 %collective-permute-start.2 = (bf16[4,144,1280]{2,1,0:T(8,128)(2,1)S(1)}, bf16[4,144,1280]{2,1,0:T(8,128)(2,1)}, u32[]{:S(2)}, u32[]{:S(2)}) collective-permute-start(bf16[4,144,1280]{2,1,0:T(8,128)(2,1)S(1)} %all-to-all-done.early_ref), channel_id=1, source_target_pairs={{0,1},{1,0},{2,3},{3,2},{4,5},{5,4},{6,7},{7,6},{8,9},{9,8},{10,11... | collective-permute-start | bytes 4423688 | tf_op jit(solution)/shard_map/ppermute | solution.py:25
  58.5 34.8 %collective-permute-start.3 = (bf16[4,144,1280]{2,1,0:T(8,128)(2,1)S(1)}, bf16[4,144,1280]{2,1,0:T(8,128)(2,1)}, u32[]{:S(2)}, u32[]{:S(2)}) collective-permute-start(bf16[4,144,1280]{2,1,0:T(8,128)(2,1)S(1)} %all-to-all-done.early_ref), channel_id=1, source_target_pairs={{0,8},{8,0},{16,24},{24,16},{1,9},{9,1},{17,25},{25,17},{2,10},{10... | collective-permute-start | bytes 4423688 | tf_op jit(solution)/shard_map/ppermute | solution.py:25
  60.0 35.2 %collective-permute-start.4 = (bf16[4,144,1280]{2,1,0:T(8,128)(2,1)S(1)}, bf16[4,144,1280]{2,1,0:T(8,128)(2,1)}, u32[]{:S(2)}, u32[]{:S(2)}) collective-permute-start(bf16[4,144,1280]{2,1,0:T(8,128)(2,1)S(1)} %all-to-all-done.early_ref), channel_id=1, source_target_pairs={{0,16},{8,24},{16,0},{24,8},{1,17},{9,25},{17,1},{25,9},{2,18},{10... | collective-permute-start | bytes 4423688 | tf_op jit(solution)/shard_map/ppermute | solution.py:25
  66.0 60.0 %collective-permute-start.8 = (bf16[2,128,1280]{2,1,0:T(8,128)(2,1)}, bf16[2,128,1280]{2,1,0:T(8,128)(2,1)}, u32[]{:S(2)}, u32[]{:S(2)}) collective-permute-start(bf16[2,128,1280]{2,1,0:T(8,128)(2,1)} %pad_maximum_fusion.3), channel_id=1, source_target_pairs={{0,16},{8,24},{16,0},{24,8},{1,17},{9,25},{17,1},{25,9},{2,18},{10... | collective-permute-start | bytes 1966088 | tf_op jit(solution)/shard_map/ppermute | solution.py:25
  95.2 3.3 collective-permute-start.5
  122.0 7.8 %collective-permute-start.6 = (bf16[4,144,1280]{2,1,0:T(8,128)(2,1)}, bf16[4,144,1280]{2,1,0:T(8,128)(2,1)S(1)}, u32[]{:S(2)}, u32[]{:S(2)}) collective-permute-start(bf16[4,144,1280]{2,1,0:T(8,128)(2,1)} %get-tuple-element.90), channel_id=1, source_target_pairs={{0,1},{1,0},{2,3},{3,2},{4,5},{5,4},{6,7},{7,6},{8,9},{9,8},{10,11... | collective-permute-start | bytes 4423688 | tf_op jit(solution)/shard_map/ppermute | solution.py:25
  127.6 21.2 %collective-permute-start.9 = (bf16[5,128,1280]{2,1,0:T(8,128)(2,1)S(1)}, bf16[5,128,1280]{2,1,0:T(8,128)(2,1)}, u32[]{:S(2)}, u32[]{:S(2)}) collective-permute-start(bf16[5,128,1280]{2,1,0:T(8,128)(2,1)S(1)} %pad_maximum_fusion.1.mine_ref), channel_id=1, source_target_pairs={{0,1},{1,0},{2,3},{3,2},{4,5},{5,4},{6,7},{7,6},{8,9},{9,8},{10,11... | collective-permute-start | bytes 4915208 | tf_op jit(solution)/shard_map/ppermute | solution.py:25
  127.7 28.4 %collective-permute-start.1 = (bf16[2,160,1792]{2,1,0:T(8,128)(2,1)}, bf16[2,160,1792]{2,1,0:T(8,128)(2,1)}, u32[]{:S(2)}, u32[]{:S(2)}) collective-permute-start(bf16[2,160,1792]{2,1,0:T(8,128)(2,1)} %get-tuple-element.80), channel_id=1, source_target_pairs={{0,8},{8,0},{16,24},{24,16},{1,9},{9,1},{17,25},{25,17},{2,10},{10... | collective-permute-start | bytes 3440648 | tf_op jit(solution)/shard_map/ppermute | solution.py:25
  128.3 15.4 %collective-permute-start.10 = (bf16[2,112,1280]{2,1,0:T(8,128)(2,1)}, bf16[2,112,1280]{2,1,0:T(8,128)(2,1)}, u32[]{:S(2)}, u32[]{:S(2)}) collective-permute-start(bf16[2,112,1280]{2,1,0:T(8,128)(2,1)} %get-tuple-element.97), channel_id=1, source_target_pairs={{0,16},{8,24},{16,0},{24,8},{1,17},{9,25},{17,1},{25,9},{2,18},{10... | collective-permute-start | bytes 1720328 | tf_op jit(solution)/shard_map/ppermute | solution.py:25
  131.4 5.2 %copy-start.27 = (s32[4]{0:T(128)S(1)}, s32[4]{0:T(128)}, u32[]{:S(2)}) copy-start(s32[4]{0:T(128)} %constant.117.clone) | copy-start | bytes 52
  131.4 40.1 %all-to-all-start.2 = ((bf16[4,144,1280]{2,1,0:T(8,128)(2,1)}), bf16[4,144,1280]{2,1,0:T(8,128)(2,1)S(1)}, u32[]{:S(2)}, u32[]{:S(2)}) async-start(bf16[4,144,1280]{2,1,0:T(8,128)(2,1)} %add_convert_fusion), calls=%async_computation.2 | async-start | bytes 2949120 | tf_op jit(solution)/shard_map/all_to_all | solution.py:35
  136.6 193.1 %reduce-scatter.2.cloned.1.call-start = ((), (), s32[]{:S(2)}) async-start(), calls=%async_computation.6 | async-start | bytes 2949120 | tf_op jit(solution)/shard_map/reduce_scatter | solution.py:781
  145.0 45.7 %collective-permute-start.11 = (bf16[4,128,1280]{2,1,0:T(8,128)(2,1)}, bf16[4,128,1280]{2,1,0:T(8,128)(2,1)}, u32[]{:S(2)}, u32[]{:S(2)}) collective-permute-start(bf16[4,128,1280]{2,1,0:T(8,128)(2,1)} %all-to-all-done.1.ns0_ref), channel_id=1, source_target_pairs={{0,8},{8,0},{16,24},{24,16},{1,9},{9,1},{17,25},{25,17},{2,10},{10... | collective-permute-start | bytes 3932168 | tf_op jit(solution)/shard_map/ppermute | solution.py:25
  146.6 44.1 %collective-permute-start.12 = (bf16[4,128,1280]{2,1,0:T(8,128)(2,1)}, bf16[4,128,1280]{2,1,0:T(8,128)(2,1)}, u32[]{:S(2)}, u32[]{:S(2)}) collective-permute-start(bf16[4,128,1280]{2,1,0:T(8,128)(2,1)} %all-to-all-done.1.ns0_ref), channel_id=1, source_target_pairs={{0,16},{8,24},{16,0},{24,8},{1,17},{9,25},{17,1},{25,9},{2,18},{10... | collective-permute-start | bytes 3932168 | tf_op jit(solution)/shard_map/ppermute | solution.py:25
  158.0 52.1 %collective-permute-start.19 = (bf16[4,144,1280]{2,1,0:T(8,128)(2,1)}, bf16[4,144,1280]{2,1,0:T(8,128)(2,1)}, u32[]{:S(2)}, u32[]{:S(2)}) collective-permute-start(bf16[4,144,1280]{2,1,0:T(8,128)(2,1)} %collective-permute-done.3.early0_ref), channel_id=1, source_target_pairs={{0,1},{1,0},{2,3},{3,2},{4,5},{5,4},{6,7},{7,6},{8,9},{9,8},{10,11... | collective-permute-start | bytes 4423688 | tf_op jit(solution)/shard_map/ppermute | solution.py:25
  190.8 8.1 %collective-permute-start.14 = (bf16[112,1280]{1,0:T(8,128)(2,1)}, bf16[112,1280]{1,0:T(8,128)(2,1)S(1)}, u32[]{:S(2)}, u32[]{:S(2)}) collective-permute-start(bf16[112,1280]{1,0:T(8,128)(2,1)} %slice_bitcast_fusion.2), channel_id=1, source_target_pairs={{0,8},{8,0},{16,24},{24,16},{1,9},{9,1},{17,25},{25,17},{2,10},{10... | collective-permute-start | bytes 860168 | tf_op jit(solution)/shard_map/ppermute | solution.py:25
  192.3 18.4 %collective-permute-start.18 = (bf16[4,128,1280]{2,1,0:T(8,128)(2,1)}, bf16[4,128,1280]{2,1,0:T(8,128)(2,1)}, u32[]{:S(2)}, u32[]{:S(2)}) collective-permute-start(bf16[4,128,1280]{2,1,0:T(8,128)(2,1)} %collective-permute-done.11.ns0_ref), channel_id=1, source_target_pairs={{0,1},{1,0},{2,3},{3,2},{4,5},{5,4},{6,7},{7,6},{8,9},{9,8},{10,11... | collective-permute-start | bytes 3932168 | tf_op jit(solution)/shard_map/ppermute | solution.py:25
  193.2 59.0 %collective-permute-start.24 = (bf16[4,144,1280]{2,1,0:T(8,128)(2,1)}, bf16[4,144,1280]{2,1,0:T(8,128)(2,1)}, u32[]{:S(2)}, u32[]{:S(2)}) collective-permute-start(bf16[4,144,1280]{2,1,0:T(8,128)(2,1)} %collective-permute-done.4.early0_ref), channel_id=1, source_target_pairs={{0,1},{1,0},{2,3},{3,2},{4,5},{5,4},{6,7},{7,6},{8,9},{9,8},{10,11... | collective-permute-start | bytes 4423688 | tf_op jit(solution)/shard_map/ppermute | solution.py:25
  193.7 15.2 %collective-permute-start.13 = (bf16[160,1792]{1,0:T(8,128)(2,1)}, bf16[160,1792]{1,0:T(8,128)(2,1)}, u32[]{:S(2)}, u32[]{:S(2)}) collective-permute-start(bf16[160,1792]{1,0:T(8,128)(2,1)} %slice_bitcast_fusion), channel_id=1, source_target_pairs={{0,16},{8,24},{16,0},{24,8},{1,17},{9,25},{17,1},{25,9},{2,18},{10... | collective-permute-start | bytes 1720328 | tf_op jit(solution)/shard_map/ppermute | solution.py:25
  198.9 42.7 %collective-permute-start.15 = (bf16[544,1280]{1,0:T(8,128)(2,1)S(1)}, bf16[544,1280]{1,0:T(8,128)(2,1)}, u32[]{:S(2)}, u32[]{:S(2)}) collective-permute-start(bf16[544,1280]{1,0:T(8,128)(2,1)S(1)} %copy-done.3), channel_id=1, source_target_pairs={{0,1},{1,0},{2,3},{3,2},{4,5},{5,4},{6,7},{7,6},{8,9},{9,8},{10,11... | collective-permute-start | bytes 4177928 | tf_op jit(solution)/shard_map/ppermute | solution.py:25
  208.9 30.5 %collective-permute-start.22 = (bf16[4,128,1280]{2,1,0:T(8,128)(2,1)}, bf16[4,128,1280]{2,1,0:T(8,128)(2,1)}, u32[]{:S(2)}, u32[]{:S(2)}) collective-permute-start(bf16[4,128,1280]{2,1,0:T(8,128)(2,1)} %collective-permute-done.12.ns0_ref), channel_id=1, source_target_pairs={{0,1},{1,0},{2,3},{3,2},{4,5},{5,4},{6,7},{7,6},{8,9},{9,8},{10,11... | collective-permute-start | bytes 3932168 | tf_op jit(solution)/shard_map/ppermute | solution.py:25
  210.1 23.8 %collective-permute-start.16 = (bf16[256,1280]{1,0:T(8,128)(2,1)}, bf16[256,1280]{1,0:T(8,128)(2,1)}, u32[]{:S(2)}, u32[]{:S(2)}) collective-permute-start(bf16[256,1280]{1,0:T(8,128)(2,1)} %slice.55), channel_id=1, source_target_pairs={{0,8},{8,0},{16,24},{24,16},{1,9},{9,1},{17,25},{25,17},{2,10},{10... | collective-permute-start | bytes 1966088 | tf_op jit(solution)/shard_map/ppermute | solution.py:25
  210.7 23.2 %collective-permute-start.17 = (bf16[288,1280]{1,0:T(8,128)(2,1)}, bf16[288,1280]{1,0:T(8,128)(2,1)}, u32[]{:S(2)}, u32[]{:S(2)}) collective-permute-start(bf16[288,1280]{1,0:T(8,128)(2,1)} %slice.56), channel_id=1, source_target_pairs={{0,16},{8,24},{16,0},{24,8},{1,17},{9,25},{17,1},{25,9},{2,18},{10... | collective-permute-start | bytes 2211848 | tf_op jit(solution)/shard_map/ppermute | solution.py:25
  233.9 7.7 %collective-permute-start.20 = (bf16[256,1280]{1,0:T(8,128)(2,1)}, bf16[256,1280]{1,0:T(8,128)(2,1)}, u32[]{:S(2)}, u32[]{:S(2)}) collective-permute-start(bf16[256,1280]{1,0:T(8,128)(2,1)} %collective-permute-done.16.qx_ref), channel_id=1, source_target_pairs={{0,1},{1,0},{2,3},{3,2},{4,5},{5,4},{6,7},{7,6},{8,9},{9,8},{10,11... | collective-permute-start | bytes 1966088 | tf_op jit(solution)/shard_map/ppermute | solution.py:25
  234.0 7.6 %collective-permute-start.21 = (bf16[288,1280]{1,0:T(8,128)(2,1)}, bf16[288,1280]{1,0:T(8,128)(2,1)}, u32[]{:S(2)}, u32[]{:S(2)}) collective-permute-start(bf16[288,1280]{1,0:T(8,128)(2,1)} %collective-permute-done.17.by_ref), channel_id=1, source_target_pairs={{0,1},{1,0},{2,3},{3,2},{4,5},{5,4},{6,7},{7,6},{8,9},{9,8},{10,11... | collective-permute-start | bytes 2211848 | tf_op jit(solution)/shard_map/ppermute | solution.py:25
  235.7 41.9 %all-to-all-start.3 = ((bf16[4,40,3072]{2,1,0:T(8,128)(2,1)}), bf16[4,40,3072]{2,1,0:T(8,128)(2,1)S(1)}, u32[]{:S(2)}, u32[]{:S(2)}) async-start(bf16[4,40,3072]{2,1,0:T(8,128)(2,1)} %fusion.10), calls=%async_computation.3 | async-start | bytes 1966080 | tf_op jit(solution)/shard_map/all_to_all | solution.py:35
  249.2 25.8 %collective-permute-start.23 = (bf16[160,2560]{1,0:T(8,128)(2,1)}, bf16[160,2560]{1,0:T(8,128)(2,1)S(1)}, u32[]{:S(2)}, u32[]{:S(2)}) collective-permute-start(bf16[160,2560]{1,0:T(8,128)(2,1)} %get-tuple-element.119), channel_id=1, source_target_pairs={{0,16},{8,24},{16,0},{24,8},{1,17},{9,25},{17,1},{25,9},{2,18},{10... | collective-permute-start | bytes 2457608 | tf_op jit(solution)/shard_map/ppermute | solution.py:25
  250.7 24.3 %copy-start.13 = (bf16[160,2560]{1,0:T(8,128)(2,1)S(1)}, bf16[160,2560]{1,0:T(8,128)(2,1)}, u32[]{:S(2)}) copy-start(bf16[160,2560]{1,0:T(8,128)(2,1)} %get-tuple-element.118) | copy-start | bytes 2457604
  250.7 24.5 %collective-permute-start.25 = (bf16[160,2688]{1,0:T(8,128)(2,1)}, bf16[160,2688]{1,0:T(8,128)(2,1)S(1)}, u32[]{:S(2)}, u32[]{:S(2)}) collective-permute-start(bf16[160,2688]{1,0:T(8,128)(2,1)} %get-tuple-element.125), channel_id=1, source_target_pairs={{0,8},{8,0},{16,24},{24,16},{1,9},{9,1},{17,25},{25,17},{2,10},{10... | collective-permute-start | bytes 2580488 | tf_op jit(solution)/shard_map/ppermute | solution.py:25
  277.6 50.2 %all-to-all-start.4 = ((bf16[4,40,5248]{2,1,0:T(8,128)(2,1)}), bf16[4,40,5248]{2,1,0:T(8,128)(2,1)S(1)}, u32[]{:S(2)}, u32[]{:S(2)}) async-start(bf16[4,40,5248]{2,1,0:T(8,128)(2,1)} %bitcast.13), calls=%async_computation.5 | async-start | bytes 3358720 | tf_op jit(solution)/shard_map/all_to_all | solution.py:35
  282.7 38.7 %collective-permute-start.26 = (bf16[6720,128]{1,0:T(8,128)(2,1)}, bf16[6720,128]{1,0:T(8,128)(2,1)}, u32[]{:S(2)}, u32[]{:S(2)}) collective-permute-start(bf16[6720,128]{1,0:T(8,128)(2,1)} %get-tuple-element.130), channel_id=1, source_target_pairs={{0,16},{8,24},{16,0},{24,8},{1,17},{9,25},{17,1},{25,9},{2,18},{10... | collective-permute-start | bytes 5160968 | tf_op jit(solution)/shard_map/ppermute | solution.py:25
  283.2 38.5 %collective-permute-start.27 = (bf16[6720,128]{1,0:T(8,128)(2,1)}, bf16[6720,128]{1,0:T(8,128)(2,1)}, u32[]{:S(2)}, u32[]{:S(2)}) collective-permute-start(bf16[6720,128]{1,0:T(8,128)(2,1)} %get-tuple-element.131), channel_id=1, source_target_pairs={{0,8},{8,0},{16,24},{24,16},{1,9},{9,1},{17,25},{25,17},{2,10},{10... | collective-permute-start | bytes 5160968 | tf_op jit(solution)/shard_map/ppermute | solution.py:25
  (17 other events, 52.7 us)
Sparse Core Ops, SparseCore 0:
  195.4 35.5 reduce-scatter.1

commit v2 on v1

--- a/solution.py
+++ b/solution.py
@@ -251,7 +251,7 @@
     )(ids, *ns, pick, dh, gate, up, router)
 
 
-def combine_kernel(place, hid_ref, row_gate_ref, pick_ref, down_ref, out_ref, scaled_ref):
+def combine_kernel(hid_ref, row_gate_ref, pick_ref, down_ref, mine_ref, other_ref, scaled_ref):
     s = pl.program_id(0)
     slots, sources, capacity, length = pick_ref.shape
     result = dot_nn(hid_ref[0], down_ref[0]).astype(BF)
@@ -263,23 +263,22 @@
             at = slice(n * capacity, (n + 1) * capacity)
             pick = jnp.concatenate([pick_ref[i, n] for i in range(slots)], 0)
             scaled = jnp.concatenate([scaled_ref[i, at] for i in range(slots)], 0)
-            out_ref[place[n]] = dot_tn(pick, scaled).astype(BF)
-
-
-def combine(place, hid, row_gate, pick, down):
+            out = (mine_ref, other_ref)[n // (sources // 2)]
+            out[n % (sources // 2)] = dot_tn(pick, scaled).astype(BF)
+
+
+def combine(hid, row_gate, pick, down):
     slots, sources, capacity, length = pick.shape
     _, ff, width = down.shape
     rows = sources * capacity
+    out = (sources // 2, length, width)
     return pl.pallas_call(
         combine_kernel,
-        grid_spec=pltpu.PrefetchScalarGridSpec(
-            num_scalar_prefetch=1,
-            grid=(slots,),
-            in_specs=[per_slot(rows, ff), per_slot(rows, LANES), once(pick.shape), per_slot(ff, width)],
-            out_specs=once((sources, length, width)),
-            scratch_shapes=[pltpu.VMEM((slots, rows, width), BF)],
-        ),
-        out_shape=jax.ShapeDtypeStruct((sources, length, width), BF),
+        grid=(slots,),
+        in_specs=[per_slot(rows, ff), per_slot(rows, LANES), once(pick.shape), per_slot(ff, width)],
+        out_specs=[once(out)] * 2,
+        scratch_shapes=[pltpu.VMEM((slots, rows, width), BF)],
+        out_shape=[jax.ShapeDtypeStruct(out, BF)] * 2,
         compiler_params=pltpu.CompilerParams(vmem_limit_bytes=VMEM_LIMIT),
         cost_estimate=pl.CostEstimate(
             flops=int(COST * (4 * slots * rows * width * (ff + length))),
@@ -287,7 +286,14 @@
             transcendentals=0,
         ),
         name="combine",
-    )(place, hid, row_gate, pick, down)
+    )(hid, row_gate, pick, down)
+
+
+def keep_rows(size, second):
+    mine = lax.axis_index("dp")
+    i = np.arange(size // 4, dtype=np.int32)
+    source = jnp.concatenate([(mine ^ second) * (size // 4) + i, mine * (size // 4) + i])
+    return (source[:, None] == jnp.arange(size, dtype=jnp.int32)[None, :]).astype(BF)
 
 
 def routed_grads_kernel(
@@ -334,23 +340,15 @@
             start += size
 
 
-def routed_grads(slot, second, ids, own, far, weights, router, expert_count):
+def routed_grads(slot, selectors, ids, own, far, weights, router, expert_count):
     gate, up, down = weights
     _, rows, width = own[0].shape
     ff = gate.shape[2]
-    mine = lax.axis_index("dp")
-
-    def selector(size):
-        part = size // 4
-        i = np.arange(part, dtype=np.int32)
-        source = jnp.concatenate([(mine ^ second) * part + i, mine * part + i])
-        return (source[:, None] == jnp.arange(size, dtype=jnp.int32)[None, :]).astype(BF)
-
     at = lambda v: pl.BlockSpec(
         (1,) + v.shape[1:], lambda i, _: (slot, 0, 0), pipeline_mode=pl.Buffered(1)
     )
     shape = (3 * width * ff // 4 // LANES, LANES)
-    rest = far + [router, selector(width), selector(ff)]
+    rest = far + [router, *selectors]
     rest_specs = [once(v.shape) for v in rest]
     return pl.pallas_call(
         functools.partial(routed_grads_kernel, expert_count, slot),
@@ -606,14 +604,15 @@
     )
 
 
-def call(kernel, name, outs, *args, flops=1):
+def call(kernel, name, outs, *args, scalars=0):
     return pl.pallas_call(
         kernel,
-        in_specs=[pl.BlockSpec(memory_space=pltpu.VMEM)] * len(args),
+        in_specs=[pl.BlockSpec(memory_space=pltpu.SMEM)] * scalars
+        + [pl.BlockSpec(memory_space=pltpu.VMEM)] * (len(args) - scalars),
         out_specs=[pl.BlockSpec(memory_space=pltpu.VMEM)] * len(outs),
         out_shape=[jax.ShapeDtypeStruct(*o) for o in outs],
         compiler_params=pltpu.CompilerParams(vmem_limit_bytes=VMEM_LIMIT),
-        cost_estimate=pl.CostEstimate(flops=flops, bytes_accessed=flops, transcendentals=0),
+        cost_estimate=pl.CostEstimate(flops=1, bytes_accessed=1, transcendentals=0),
         name=name,
     )(*args)
 
@@ -658,7 +657,8 @@
 
 
 def last_grads_kernel(
-    length, mine_ref, other_ref, qx_ref, qxo_ref, by_ref, byo_ref, a_ref, v_ref, o_ref, ns_ref, order_b_ref,
+    length, at_ns, z_ref, mine_ref, other_ref, qx_ref, qxo_ref, by_ref, byo_ref, a_ref, v_ref, o_ref,
+    ns_ref, cat_other_ref, ns_y_ref, ns_yo_ref, order_b_ref,
     a_send, a_keep, b_send, b_keep,
 ):
     width = mine_ref.shape[1]
@@ -681,7 +681,10 @@
     refs = ((mine_ref, start), (other_ref, start), (by_ref, start - 2 * length), (byo_ref, start - 2 * length))
     gains = sum(ref[i : i + 16].astype(F32) for ref, i in refs).astype(BF)
     logits = jnp.concatenate([ref[i + 16 :, :length] for ref, i in refs], 1)
-    left_r = dot_nt(order_b_ref[...], ns_ref[...]).astype(BF)
+    ns = join(
+        ns_ref[...], cat_other_ref[:, at_ns : at_ns + width], ns_y_ref[z_ref[0]], ns_yo_ref[z_ref[0]]
+    )
+    left_r = dot_nt(order_b_ref[...], ns).astype(BF)
     small = jnp.concatenate(
         [dot_nt(left_r, logits), dot_nt(order_b_ref[...], gains)], 1
     )
@@ -723,7 +726,7 @@
     w = model_width
     rows = w // (n_dp * n_ex)
     over_core = lambda v: partner(v, "expert", 1)
-    order_d = rows_for(w, (1, 3, 0, 2))
+    order_d = rows_for(w, (2, 3, 0, 1))
     order_a, order_b = rows_for(w, (0, 2)), rows_for(w, (0, 1))
 
     routes_t = jnp.pad(routes.T.astype(BF), ((0, 16 - TOP), (0, 0)), constant_values=-1)
@@ -741,18 +744,17 @@
         [((length, 3 * ff + 2 * w), BF), ((length, w), F32), ((length, w), F32)],
         normed_second, cotangent, shared_gate, shared_up, shared_down,
     )
-    my_z, my_core = my_ex // 2, my_ex % 2
+    my_z = my_ex // 2
     first_x = partner(normed_first, "dp", 1)
     first_y = partner(jnp.stack([normed_first, attended]), "dp", 2)
-    ns = spread(after(normed_second, early, from_shared))
+    ns = spread(after(normed_second, early, from_shared, first_x, first_y))
     from_other = over_core(from_shared)
     part_d, part_f = w // (2 * n_dp), ff // (2 * n_dp)
     su_send, su_keep, sd_send, sd_keep = call(
         functools.partial(shared_grads_kernel, ff, w), "shared_grads",
         [((2, part_d, 2 * ff), BF)] * 2 + [((2, part_f, w), BF)] * 2,
-        from_shared, from_other, order_d, rows_for(ff, (2, 3, 0, 1)),
-    )
-    su_got, sd_got = partner(su_send, "dp", 1), partner(sd_send, "dp", 2)
+        from_shared, from_other, order_d, rows_for(ff, (1, 3, 0, 2)),
+    )
     early_other = over_core(early)
     early_x, early_y = partner(early, "dp", 1), partner(early, "dp", 2)
 
@@ -761,24 +763,33 @@
     pick, dh_raw, dy_rows = prepare(my_expert, (early, early_other), routed_down, capacity)
     ns = after(ns, pick, dh_raw, early_x, early_y, su_send)
     ns_other = over_core(ns)
-    ns_x, ns_y = partner(ns, "dp", 1), partner(ns, "dp", 2)
     back_mine, back_other, hid, dg, du, x_rows, row_gate = experts(
         my_expert, (ns, ns_other), pick, dh_raw, routed_gate, routed_up, router_wide, expert_count
     )
     back_sum = plus(back_mine, over_core(back_other))
     back = exchange_z(back_sum)
+    ns_far, su_send, sd_send, early_x, early_y = after((ns, su_send, sd_send, early_x, early_y), back_sum)
+    early_x_other, early_y_other = over_core(early_x), over_core(early_y)
+    su_got, sd_got = partner(su_send, "dp", 2), partner(sd_send, "dp", 1)
+    ns_far = after(ns_far, su_got)
+    ns_x, ns_y = partner(ns_far, "dp", 1), partner(ns_far, "dp", 2)
+    su, sd = plus(su_keep, su_got), plus(sd_keep, sd_got)
+    su_last, sd_last = partner(su[1], "dp", 1), partner(sd[1], "dp", 2)
+    su, sd = plus(su[0], su_last), plus(sd[0], sd_last)
 
     lefts = jnp.concatenate([normed_first[None], attended[None], first_x[None], first_y])
+    lefts = after(lefts, back_sum)
     lefts_other = over_core(lefts)
     left_shape = ((w // 4, 4 * length), BF)
     left_a, left_v, left_o = call(
         lefts_kernel, "lefts", [left_shape] * 3, lefts, lefts_other, order_a, order_b,
     )
-    place = np.arange(n_z, dtype=np.int32) * 2
-    place = jnp.concatenate([place + my_core, place + 1 - my_core])
-    combined_rows = combine(place, after(hid, back_sum), row_gate, pick, routed_down)
-    back = after(back, combined_rows, left_a, su_got, sd_got)
-    combined = lax.psum_scatter(combined_rows, "expert", scatter_dimension=0, tiled=False)
+    combined_mine, combined_other = combine(after(hid, early_x_other, early_y_other), row_gate, pick, routed_down)
+    combined = plus(combined_mine, over_core(combined_other))
+    selectors = [(keep_rows(w, q), keep_rows(ff, q)) for q in (2, 1)]
+    back = after(back, combined, left_a, selectors)
+    combined = exchange_z(after(combined, back))
+
     high = -(-expert_count // 16) * 16
     router_t = jnp.pad(w_router.T, ((0, high - expert_count), (0, 0)))
     d_cat, grad_inputs = backward(
@@ -786,32 +797,29 @@
         queries, key_rows, value_rows, w_query, w_key, w_value, w_out, back, expert_count,
     )
 
-    d_cat = after(d_cat, ns_x, ns_y)
-    cat_other = over_core(d_cat)
-    su, sd = plus(su_keep, su_got), plus(sd_keep, sd_got)
-    su_last, sd_last = partner(after(su[1], d_cat), "dp", 2), partner(after(sd[1], d_cat), "dp", 1)
-    su, sd = plus(su[0], su_last), plus(sd[0], sd_last)
-    qk_x, b_y = partner(d_cat[: 2 * length], "dp", 1), partner(d_cat[2 * length :], "dp", 2)
-    far_x = [ns_x, over_core(after(ns_x, d_cat)), early_x, over_core(early_x)]
-    far_y = [ns_y, over_core(after(ns_y, d_cat)), early_y, over_core(early_y)]
+    d_out = d_cat
+    qk_x, b_y = partner(d_out[: 2 * length], "dp", 1), partner(d_out[2 * length :], "dp", 2)
+    far_x = [ns_x, over_core(after(ns_x, d_cat)), early_x, early_x_other]
+
+    far_y = [ns_y, over_core(after(ns_y, d_cat)), early_y, early_y_other]
+    far = [far_x, far_y]
 
     def slot_grads(slot, last_dg):
         return routed_grads(
-            slot, 2 if slot % 2 == 0 else 1, my_expert, [x_rows, last_dg, du, hid, row_gate, dy_rows],
-            far_x if slot % 2 == 0 else far_y, [routed_gate, routed_up, routed_down], router_wide, expert_count,
+            slot, selectors[slot % 2], my_expert, [x_rows, last_dg, du, hid, row_gate, dy_rows],
+            far[slot % 2], [routed_gate, routed_up, routed_down], router_wide, expert_count,
         )
 
-    routed = [slot_grads(0, after(dg, d_cat))]
-    qk_x, b_y = after((qk_x, b_y), routed[0])
+    routed = [slot_grads(0, after(dg, d_cat, far_y[1]))]
+    d_cat, qk_x, b_y = after((d_cat, qk_x, b_y), routed[0], su_last, sd_last)
+
+    cat_other = over_core(d_cat)
     qk_x_other, b_y_other = over_core(qk_x), over_core(b_y)
-    here = lambda v: lax.dynamic_index_in_dim(v, my_z, 0, keepdims=False)
-    ns_sets = jnp.concatenate(
-        [normed_second, from_other[:, 3 * ff : 3 * ff + w], here(far_y[0]), here(far_y[1])], 0
-    )
     a_send, a_keep, b_send, b_keep = call(
-        functools.partial(last_grads_kernel, length), "last_grads",
+        functools.partial(last_grads_kernel, length, 3 * ff), "last_grads",
         [((w // 8, 2 * w), BF)] * 2 + [((w // 8, 2 * w + LANES), BF)] * 2,
-        d_cat, cat_other, qk_x, qk_x_other, b_y, b_y_other, left_a, left_v, left_o, ns_sets, order_b,
+        my_z[None], d_cat, cat_other, qk_x, qk_x_other, b_y, b_y_other, left_a, left_v, left_o,
+        normed_second, from_other, far_y[0], far_y[1], order_b, scalars=1,
     )
     a_got, b_got = partner(a_send, "dp", 2), partner(b_send, "dp", 1)
 
@@ -824,11 +832,11 @@
     last = jnp.concatenate([plus(a_keep, a_got), plus(b_keep, b_got)], -1).reshape(n_z, rows, -1)
 
     sd = jnp.pad(sd.reshape(n_z, -1, w), ((0, 0), (0, (w - ff) // (n_dp * n_ex)), (0, 0)))
-    grad_shared = exchange_z(after(jnp.concatenate([su.reshape(n_z, rows, -1), sd], -1), d_cat))
+    grad_shared = exchange_z(after(jnp.concatenate([su.reshape(n_z, rows, -1), sd], -1), combined))
     last = exchange_z(after(last, grad_shared))
     grad_shared, combined = after((grad_shared, combined), last)
     last, grad_shared = total(list(last)), total(list(grad_shared))
-    output = (residual + shared_result + combined.astype(F32)).astype(BF)
+    output = (residual + shared_result + total(list(combined))).astype(BF)
     grad_rgate, grad_rup, grad_rdown = finish(pieces, [(w // n_dp, ff), (w // n_dp, ff), (ff // n_dp, w)])
     return (
         output,

time: 345 us -> 331 us (0.959)
  between operations: 14.7 us -> 1.27 us
  starting transfers between devices: 44.1 us -> 52.3 us
  waiting for transfers between devices: 84.3 us -> 76.7 us
    all_to_all x5 -> x6, waiting for transfers between devices: 16.3 us -> 7.33 us  [exchange_z(): lax.all_to_all(s, 'expert', 0, 0, tiled=True, axis_index_groups=groups)]
    all_to_all x5 -> x6, starting transfers between devices: 24.9 us -> 30.3 us  [exchange_z(): lax.all_to_all(s, 'expert', 0, 0, tiled=True, axis_index_groups=groups)]
    convert_element_type x7 -> x8, other arithmetic: 7.17 us -> 11.9 us  [plus(): return (a.astype(F32) + b.astype(F32)).astype(BF)]
    ppermute x28 -> x29, starting transfers between devices: 19.2 us -> 22.1 us  [partner(): return lax.ppermute(v, axis, [(i, i ^ mask) for i in range(n)])]
    ppermute x28 -> x29, waiting for transfers between devices: 68 us -> 69.4 us  [partner(): return lax.ppermute(v, axis, [(i, i ^ mask) for i in range(n)])]
  transfers between devices with their start and end apart: 34 -> 35, of which waited for: 10 -> 12; matrix products, arithmetic and copies ran while one was open for 11% -> 10% of each run, Pallas kernels for 44% -> 39%
where the time goes in v2:
time: 331 us; the launch traced here: 326 us
  Pallas kernels  148 us (45%)
  waiting for transfers between devices  76.7 us (23%)
  starting transfers between devices  52.3 us (16%)
  other arithmetic  30.2 us (9%)
  local copies, waits for them, and re-layouts  17.3 us (5%)
    ppermute x29, waiting for transfers between devices, partner(): return lax.ppermute(v, axis, [(i, i ^ mask) for i in range(n)])  69.4 us
    pallas_call x2, Pallas kernels, routed_grads(): pl.pallas_call(functools.partial(routed_grads_kernel, expert_count, slot)...  45.6 us
    all_to_all x6, starting transfers between devices, exchange_z(): lax.all_to_all(s, 'expert', 0, 0, tiled=True, axis_index_groups=groups)  30.3 us
    pallas_call x4, Pallas kernels, call(): pl.pallas_call(kernel, in_specs=[pl.BlockSpec(memory_space=pltpu.SMEM)] *...  26.6 us
    pallas_call x1, Pallas kernels, experts(): pl.pallas_call(functools.partial(experts_kernel, expert_count), grid_spec...  22.3 us
    ppermute x29, starting transfers between devices, partner(): return lax.ppermute(v, axis, [(i, i ^ mask) for i in range(n)])  22.1 us
    pallas_call x1, Pallas kernels, backward(): pl.pallas_call(functools.partial(backward_kernel, expert_count), grid=(wi...  17.7 us
    convert_element_type x8, other arithmetic, plus(): return (a.astype(F32) + b.astype(F32)).astype(BF)  11.9 us
  transfers between devices with their start and end apart: 35, of which 12 were waited for; matrix products, arithmetic and copies ran while one was open for 10% of the time, Pallas kernels for 39%

profile of v2, /device:TPU:0, one launch (start us, length us, event | category | flops | bytes accessed | tf_op | source)
XLA Modules:
  0.0 326.0 jit_solution(781003437558913814)
XLA Ops:
  2.3 1.2 broadcast_in_dim.8
  3.5 6.3 %all-to-all-start = ((bf16[4,144,1280]{2,1,0:T(8,128)(2,1)}), bf16[4,144,1280]{2,1,0:T(8,128)(2,1)S(1)}, u32[]{:S(2)}, u32[]{:S(2)}) async-start(bf16[4,144,1280]{2,1,0:T(8,128)(2,1)} %broadcast_in_dim.8), calls=%async_computation | async-start | bytes 2949120 | tf_op jit(solution)/shard_map/all_to_all | solution.py:35
  9.9 11.4 %attention.1 = (bf16[128,1280]{1,0:T(8,128)(2,1)}, bf16[128,1280]{1,0:T(8,128)(2,1)}, bf16[128,1280]{1,0:T(8,128)(2,1)}, bf16[128,1280]{1,0:T(8,128)(2,1)}, bf16...) custom-call(bf16[128,1280]{1,0:T(8,128)(2,1)} %x_ref.3, f32[1280]{0:T(1024)} %gain1_ref.3, ...), custom_call_target="tpu_custom_call" | custom-call | flops 1677721600 | bytes 13107200 | tf_op jit(solution)/shard_map/attention/pallas_call | solution.py:469
  22.5 1.6 collective-permute-start.2
  24.0 1.5 collective-permute-start.1
  25.5 7.4 %shared.1 = (bf16[128,5248]{1,0:T(8,128)(2,1)}, f32[128,1280]{1,0:T(8,128)}, f32[128,1280]{1,0:T(8,128)}) custom-call(bf16[128,1280]{1,0:T(8,128)(2,1)} %get-tuple-element.90.ns_ref, bf16[128,1280]{1,0:T(8,128)(2,1)} %dy_ref.3, bf16[1280,896]{1,0:T(8,128)(2,1)} %gate_ref.4, bf16[1280,896]{1,0:T(8,128)(2,1)} %up_ref.4, bf16[896,1280]{1,0:T(8,128)(2,1)} %down_ref.5), custom_call_target="tpu_custom_call" | custom-call | flops 1 | bytes 1 | tf_op jit(solution)/shard_map/shared/pallas_call | solution.py:608
  33.1 5.6 %collective-permute-done.2 = bf16[2,128,1280]{2,1,0:T(8,128)(2,1)S(1)} collective-permute-done((bf16[2,128,1280]{2,1,0:T(8,128)(2,1)S(1)}, bf16[2,128,1280]{2,1,0:T(8,128)(2,1)S(1)}, u32[]{:S(2)}, u32[]{:S(2)}) %collective-permute-start.2) | collective-permute-done | bytes 655392 | tf_op jit(solution)/shard_map/ppermute | solution.py:25
  38.7 6.0 %all-to-all-done.early_ref = bf16[4,144,1280]{2,1,0:T(8,128)(2,1)S(1)} async-done(((bf16[4,144,1280]{2,1,0:T(8,128)(2,1)}), bf16[4,144,1280]{2,1,0:T(8,128)(2,1)S(1)}, u32[]{:S(2)}, u32[]{:S(2)}) %all-to-all-start) | async-done | bytes 1474592 | tf_op jit(solution)/shard_map/all_to_all | solution.py:35
  44.7 1.3 broadcast_in_dim.9
  46.1 5.0 %all-to-all-start.1 = ((bf16[4,128,1280]{2,1,0:T(8,128)(2,1)}), bf16[4,128,1280]{2,1,0:T(8,128)(2,1)}, u32[]{:S(2)}, u32[]{:S(2)}) async-start(bf16[4,128,1280]{2,1,0:T(8,128)(2,1)} %broadcast_in_dim.9), calls=%async_computation.1 | async-start | bytes 2621440 | tf_op jit(solution)/shard_map/all_to_all | solution.py:35
  51.1 1.6 collective-permute-start.5
  52.7 1.5 collective-permute-start.4
  56.0 1.5 fusion.order_d_ref
  58.6 6.0 %shared_grads.1 = (bf16[2,160,1792]{2,1,0:T(8,128)(2,1)}, bf16[2,160,1792]{2,1,0:T(8,128)(2,1)}, bf16[2,112,1280]{2,1,0:T(8,128)(2,1)}, bf16[2,112,1280]{2,1,0:T(8,128)(2,1)}) custom-call(bf16[128,5248]{1,0:T(8,128)(2,1)} %get-tuple-element.86.cat_ref, bf16[128,5248]{1,0:T(8,128)(2,1)} %copy-done.4, bf16[640,1280]{1,0:T(8,128)(2,1)} %fusion.order_d_ref, ...), custom_call_target="tpu_custom_call" | custom-call | flops 1 | bytes 1 | tf_op jit(solution)/shard_map/shared_grads/pallas_call | solution.py:608
  64.6 10.8 %prepare.1 = (bf16[2,8,64,128]{3,2,1,0:T(8,128)(2,1)}, f32[2,512,896]{2,1,0:T(8,128)}, bf16[2,512,1280]{2,1,0:T(8,128)(2,1)}) custom-call(s32[2]{0:T(128)} %dynamic_slice.3.ids, bf16[4,144,1280]{2,1,0:T(8,128)(2,1)} %copy-done.2, bf16[4,144,1280]{2,1,0:T(8,128)(2,1)} %collective-permute-done.3.other_ref, bf16[2,896,1280]{2,1,0:T(8,128)(2,1)} %down_ref.9), custom_call_target="tpu_custom_call" | custom-call | flops 1 | bytes 1 | tf_op jit(solution)/shard_map/prepare/pallas_call | solution.py:118
  75.5 10.5 %collective-permute-done.5.early0_ref = bf16[4,144,1280]{2,1,0:T(8,128)(2,1)} collective-permute-done((bf16[4,144,1280]{2,1,0:T(8,128)(2,1)S(1)}, bf16[4,144,1280]{2,1,0:T(8,128)(2,1)}, u32[]{:S(2)}, u32[]{:S(2)}) %collective-permute-start.5) | collective-permute-done | bytes 1474592 | tf_op jit(solution)/shard_map/ppermute | solution.py:25
  85.9 1.2 collective-permute-done.4.early0_ref
  88.2 2.2 collective-permute-done.6.ns1_ref
  91.5 22.3 %experts.1 = (bf16[4,144,1280]{2,1,0:T(8,128)(2,1)}, bf16[4,144,1280]{2,1,0:T(8,128)(2,1)}, bf16[2,512,896]{2,1,0:T(8,128)(2,1)}, bf16[2,512,896]{2,1,0:T(8,128)...) custom-call(s32[2]{0:T(128)} %dynamic_slice.3.ids, ...), custom_call_target="tpu_custom_call" | custom-call | flops 9395240960 | bytes 14680064 | tf_op jit(solution)/shard_map/experts/pallas_call | solution.py:210
  117.4 1.5 add_convert_fusion
  119.5 1.6 fusion.2.sel_d_ref
  121.1 1.5 fusion.1.sel_d_ref
  123.3 5.1 %all-to-all-start.2 = ((bf16[4,144,1280]{2,1,0:T(8,128)(2,1)}), bf16[4,144,1280]{2,1,0:T(8,128)(2,1)S(1)}, u32[]{:S(2)}, u32[]{:S(2)}) async-start(bf16[4,144,1280]{2,1,0:T(8,128)(2,1)} %add_convert_fusion), calls=%async_computation.2 | async-start | bytes 2949120 | tf_op jit(solution)/shard_map/all_to_all | solution.py:35
  128.4 7.6 %combine.1 = (bf16[4,128,1280]{2,1,0:T(8,128)(2,1)}, bf16[4,128,1280]{2,1,0:T(8,128)(2,1)}) custom-call(bf16[2,512,896]{2,1,0:T(8,128)(2,1)} %get-tuple-element.104.hid_ref, f32[2,512,128]{2,1,0:T(8,128)} %get-tuple-element.105.row_gate_ref, bf16[2,8,64,128]{3,2,1,0:T(8,128)(2,1)} %get-tuple-element.91.pick_ref, bf16[2,896,1280]{2,1,0:T(8,128)(2,1)} %down_ref.9), custom_call_target="tpu_custom_call" | custom-call | flops 5368709120 | bytes 6422528 | tf_op jit(solution)/shard_map/combine/pallas_call | solution.py:275
  136.5 1.6 collective-permute-start.10
  139.3 10.9 %collective-permute-done.8 = bf16[2,160,1792]{2,1,0:T(8,128)(2,1)} collective-permute-done((bf16[2,160,1792]{2,1,0:T(8,128)(2,1)}, bf16[2,160,1792]{2,1,0:T(8,128)(2,1)}, u32[]{:S(2)}, u32[]{:S(2)}) %collective-permute-start.8) | collective-permute-done | bytes 1146912 | tf_op jit(solution)/shard_map/ppermute | solution.py:25
  150.2 1.5 collective-permute-start.20
  154.9 4.7 %lefts.1 = (bf16[320,512]{1,0:T(8,128)(2,1)}, bf16[320,512]{1,0:T(8,128)(2,1)}, bf16[320,512]{1,0:T(8,128)(2,1)}) custom-call(bf16[5,128,1280]{2,1,0:T(8,128)(2,1)} %copy-done, bf16[5,128,1280]{2,1,0:T(8,128)(2,1)} %collective-permute-done.15.other_ref, bf16[320,1280]{1,0:T(8,128)(2,1)} %fusion.4.order_a_ref, bf16[320,1280]{1,0:T(8,128)(2,1)} %fusion.5.order_b_ref), custom_call_target="tpu_custom_call" | custom-call | flops 1 | bytes 1 | tf_op jit(solution)/shard_map/lefts/pallas_call | solution.py:608
  159.6 2.7 add_convert_fusion.1
  164.4 17.7 %backward.1 = (bf16[544,1280]{1,0:T(8,128)(2,1)}, f32[128,1280]{1,0:T(8,128)}) custom-call(bf16[128,1280]{1,0:T(8,128)(2,1)} %x_ref.3, bf16[128,1280]{1,0:T(8,128)(2,1)} %dy_ref.3, f32[128,1280]{1,0:T(8,128)} %get-tuple-element.83.residual_ref, bf16[128,1280]{1,0:T(8,128)(2,1)} %get-tuple-element.90.ns_ref, f32[128,1280]{1,0:T(8,128)} %get-tuple-element.113.shared_ref, ...), custom_call_target="tpu_custom_call" | custom-call | flops 1677721600 | bytes 13107200 | tf_op jit(solution)/shard_map/backward/pallas_call | solution.py:573
  183.4 1.5 collective-permute-start.11
  184.9 2.0 add_convert_fusion.2
  188.8 1.5 collective-permute-start.9
  192.1 3.8 %all-to-all-start.3 = ((bf16[4,128,1280]{2,1,0:T(8,128)(2,1)}), bf16[4,128,1280]{2,1,0:T(8,128)(2,1)S(1)}, u32[]{:S(2)}, u32[]{:S(2)}) async-start(bf16[4,128,1280]{2,1,0:T(8,128)(2,1)} %add_convert_fusion.1), calls=%async_computation.3 | async-start | bytes 2621440 | tf_op jit(solution)/shard_map/all_to_all | solution.py:35
  195.8 1.2 collective-permute-start.16
  198.0 22.7 %routed_grads.2 = (bf16[6720,128]{1,0:T(8,128)(2,1)}, bf16[6720,128]{1,0:T(8,128)(2,1)}) custom-call(s32[2]{0:T(128)} %dynamic_slice.3.ids, bf16[2,512,1280]{2,1,0:T(8,128)(2,1)} %get-tuple-element.118.x_ref, bf16[2,512,896]{2,1,0:T(8,128)(2,1)} %get-tuple-element.136.dg_ref, bf16[2,512,896]{2,1,0:T(8,128)(2,1)} %get-tuple-element.124.du_ref, ...), custom_call_target="tpu_custom_call" | custom-call | flops 9395240960 | bytes 24248320 | tf_op jit(solution)/shard_map/routed_grads/pallas_call | solution.py:353
  220.8 1.7 fusion.12
  224.2 1.4 fusion.9
  227.1 5.1 %all-to-all-start.4 = ((bf16[4,40,3072]{2,1,0:T(8,128)(2,1)}), bf16[4,40,3072]{2,1,0:T(8,128)(2,1)}, u32[]{:S(2)}, u32[]{:S(2)}) async-start(bf16[4,40,3072]{2,1,0:T(8,128)(2,1)} %fusion.10), calls=%async_computation.4 | async-start | bytes 1966080 | tf_op jit(solution)/shard_map/all_to_all | solution.py:35
  232.2 8.5 %last_grads.1 = (bf16[160,2560]{1,0:T(8,128)(2,1)}, bf16[160,2560]{1,0:T(8,128)(2,1)}, bf16[160,2688]{1,0:T(8,128)(2,1)}, bf16[160,2688]{1,0:T(8,128)(2,1)}) custom-call(s32[1]{0:T(128)} %bitcast.9.z_ref, bf16[544,1280]{1,0:T(8,128)(2,1)} %get-tuple-element.129.mine_ref, bf16[544,1280]{1,0:T(8,128)(2,1)} %collective-permute-done.22.other_ref, ...), custom_call_target="tpu_custom_call" | custom-call | flops 1 | bytes 1 | tf_op jit(solution)/shard_map/last_grads/pallas_call | solution.py:608
  242.6 22.9 %routed_grads.3 = (bf16[6720,128]{1,0:T(8,128)(2,1)}, bf16[6720,128]{1,0:T(8,128)(2,1)}) custom-call(s32[2]{0:T(128)} %dynamic_slice.3.ids, bf16[2,512,1280]{2,1,0:T(8,128)(2,1)} %get-tuple-element.118.x_ref, bf16[2,512,896]{2,1,0:T(8,128)(2,1)} %get-tuple-element.136.dg_ref, bf16[2,512,896]{2,1,0:T(8,128)(2,1)} %get-tuple-element.124.du_ref, ...), custom_call_target="tpu_custom_call" | custom-call | flops 9395240960 | bytes 24248320 | tf_op jit(solution)/shard_map/routed_grads/pallas_call | solution.py:353
  265.5 1.5 add_convert_fusion.4
  267.2 1.3 pad_maximum_fusion
  268.5 5.1 %all-to-all-start.5 = ((bf16[4,40,5248]{2,1,0:T(8,128)(2,1)}), bf16[4,40,5248]{2,1,0:T(8,128)(2,1)S(1)}, u32[]{:S(2)}, u32[]{:S(2)}) async-start(bf16[4,40,5248]{2,1,0:T(8,128)(2,1)} %bitcast.11), calls=%async_computation.5 | async-start | bytes 3358720 | tf_op jit(solution)/shard_map/all_to_all | solution.py:35
  273.6 1.2 collective-permute-start.28
  275.7 36.7 %collective-permute-done.28.refs_3_ = bf16[6720,128]{1,0:T(8,128)(2,1)} collective-permute-done((bf16[6720,128]{1,0:T(8,128)(2,1)}, bf16[6720,128]{1,0:T(8,128)(2,1)}, u32[]{:S(2)}, u32[]{:S(2)}) %collective-permute-start.28) | collective-permute-done | bytes 1720352 | tf_op jit(solution)/shard_map/ppermute | solution.py:25
  313.3 6.2 %finish.1 = (f32[2,320,896]{2,1,0:T(8,128)}, f32[2,320,896]{2,1,0:T(8,128)}, f32[2,224,1280]{2,1,0:T(8,128)}) custom-call(bf16[6720,128]{1,0:T(8,128)(2,1)} %get-tuple-element.128.refs_0_, bf16[6720,128]{1,0:T(8,128)(2,1)} %collective-permute-done.27.refs_1_, bf16[6720,128]{1,0:T(8,128)(2,1)} %get-tuple-element.138.refs_2_, ...), custom_call_target="tpu_custom_call" | custom-call | tf_op jit(solution)/shard_map/finish/pallas_call | solution.py:394
  319.5 1.4 add_bitcast_fusion.1
  (152 shorter events, 38.0 us)
Async XLA Ops:
  3.5 41.2 %all-to-all-start = ((bf16[4,144,1280]{2,1,0:T(8,128)(2,1)}), bf16[4,144,1280]{2,1,0:T(8,128)(2,1)S(1)}, u32[]{:S(2)}, u32[]{:S(2)}) async-start(bf16[4,144,1280]{2,1,0:T(8,128)(2,1)} %broadcast_in_dim.8), calls=%async_computation | async-start | bytes 2949120 | tf_op jit(solution)/shard_map/all_to_all | solution.py:35
  22.5 16.3 %collective-permute-start.2 = (bf16[2,128,1280]{2,1,0:T(8,128)(2,1)S(1)}, bf16[2,128,1280]{2,1,0:T(8,128)(2,1)S(1)}, u32[]{:S(2)}, u32[]{:S(2)}) collective-permute-start(bf16[2,128,1280]{2,1,0:T(8,128)(2,1)S(1)} %pad_maximum_fusion.2), channel_id=1, source_target_pairs={{0,16},{8,24},{16,0},{24,8},{1,17},{9,25},{17,1},{25,9},{2,18},{10... | collective-permute-start | bytes 1966088 | tf_op jit(solution)/shard_map/ppermute | solution.py:25
  24.0 9.1 %collective-permute-start.1 = (bf16[128,1280]{1,0:T(8,128)(2,1)}, bf16[128,1280]{1,0:T(8,128)(2,1)S(1)}, u32[]{:S(2)}, u32[]{:S(2)}) collective-permute-start(bf16[128,1280]{1,0:T(8,128)(2,1)} %get-tuple-element.88), channel_id=1, source_target_pairs={{0,8},{8,0},{16,24},{24,16},{1,9},{9,1},{17,25},{25,17},{2,10},{10... | collective-permute-start | bytes 983048 | tf_op jit(solution)/shard_map/ppermute | solution.py:25
  25.5 19.2 %copy-start.5 = (bf16[128,1280]{1,0:T(8,128)(2,1)S(1)}, bf16[128,1280]{1,0:T(8,128)(2,1)}, u32[]{:S(2)}) copy-start(bf16[128,1280]{1,0:T(8,128)(2,1)} %get-tuple-element.90.ns_ref) | copy-start | bytes 983044
  46.0 8.8 %copy-start.20 = (s32[640]{0:T(1024)S(1)}, s32[640]{0:T(1024)}, u32[]{:S(2)}) copy-start(s32[640]{0:T(1024)} %constant.93.clone) | copy-start | bytes 7684
  46.0 8.8 %copy-start.21 = (s32[640]{0:T(1024)S(1)}, s32[640]{0:T(1024)}, u32[]{:S(2)}) copy-start(s32[640]{0:T(1024)} %constant.92.clone) | copy-start | bytes 7684
  46.0 8.8 %copy-start.22 = (s32[640]{0:T(1024)S(1)}, s32[640]{0:T(1024)}, u32[]{:S(2)}) copy-start(s32[640]{0:T(1024)} %constant.91.clone) | copy-start | bytes 7684
  46.1 41.1 %all-to-all-start.1 = ((bf16[4,128,1280]{2,1,0:T(8,128)(2,1)}), bf16[4,128,1280]{2,1,0:T(8,128)(2,1)}, u32[]{:S(2)}, u32[]{:S(2)}) async-start(bf16[4,128,1280]{2,1,0:T(8,128)(2,1)} %broadcast_in_dim.9), calls=%async_computation.1 | async-start | bytes 2621440 | tf_op jit(solution)/shard_map/all_to_all | solution.py:35
  51.0 13.6 %collective-permute-start.3 = (bf16[4,144,1280]{2,1,0:T(8,128)(2,1)S(1)}, bf16[4,144,1280]{2,1,0:T(8,128)(2,1)}, u32[]{:S(2)}, u32[]{:S(2)}) collective-permute-start(bf16[4,144,1280]{2,1,0:T(8,128)(2,1)S(1)} %all-to-all-done.early_ref), channel_id=1, source_target_pairs={{0,1},{1,0},{2,3},{3,2},{4,5},{5,4},{6,7},{7,6},{8,9},{9,8},{10,11... | collective-permute-start | bytes 4423688 | tf_op jit(solution)/shard_map/ppermute | solution.py:25
  51.1 34.8 %collective-permute-start.5 = (bf16[4,144,1280]{2,1,0:T(8,128)(2,1)S(1)}, bf16[4,144,1280]{2,1,0:T(8,128)(2,1)}, u32[]{:S(2)}, u32[]{:S(2)}) collective-permute-start(bf16[4,144,1280]{2,1,0:T(8,128)(2,1)S(1)} %all-to-all-done.early_ref), channel_id=1, source_target_pairs={{0,16},{8,24},{16,0},{24,8},{1,17},{9,25},{17,1},{25,9},{2,18},{10... | collective-permute-start | bytes 4423688 | tf_op jit(solution)/shard_map/ppermute | solution.py:25
  52.7 34.5 %collective-permute-start.4 = (bf16[4,144,1280]{2,1,0:T(8,128)(2,1)S(1)}, bf16[4,144,1280]{2,1,0:T(8,128)(2,1)}, u32[]{:S(2)}, u32[]{:S(2)}) collective-permute-start(bf16[4,144,1280]{2,1,0:T(8,128)(2,1)S(1)} %all-to-all-done.early_ref), channel_id=1, source_target_pairs={{0,8},{8,0},{16,24},{24,16},{1,9},{9,1},{17,25},{25,17},{2,10},{10... | collective-permute-start | bytes 4423688 | tf_op jit(solution)/shard_map/ppermute | solution.py:25
  54.2 3.3 %collective-permute-start = (bf16[128,5248]{1,0:T(8,128)(2,1)}, bf16[128,5248]{1,0:T(8,128)(2,1)S(1)}, u32[]{:S(2)}, u32[]{:S(2)}) collective-permute-start(bf16[128,5248]{1,0:T(8,128)(2,1)} %get-tuple-element.86.cat_ref), channel_id=1, source_target_pairs={{0,1},{1,0},{2,3},{3,2},{4,5},{5,4},{6,7},{7,6},{8,9},{9,8},{10,11... | collective-permute-start | bytes 4030472 | tf_op jit(solution)/shard_map/ppermute | solution.py:25
  64.6 22.6 %copy-start.19 = (bf16[1280,15]{0,1:T(8,128)(2,1)S(1)}, bf16[1280,15]{0,1:T(8,128)(2,1)}, u32[]{:S(2)}) copy-start(bf16[1280,15]{0,1:T(8,128)(2,1)} %param.45) | copy-start | bytes 115204
  87.2 3.2 collective-permute-start.6
  88.2 25.8 %copy-start.23 = (s32[320]{0:T(512)S(1)}, s32[320]{0:T(512)}, u32[]{:S(2)}) copy-start(s32[320]{0:T(512)} %constant.97.clone) | copy-start | bytes 3844
  88.2 25.8 %copy-start.24 = (s32[320]{0:T(512)S(1)}, s32[320]{0:T(512)}, u32[]{:S(2)}) copy-start(s32[320]{0:T(512)} %constant.96.clone) | copy-start | bytes 3844
  88.2 25.8 %copy-start.25 = (s32[320]{0:T(512)S(1)}, s32[320]{0:T(512)}, u32[]{:S(2)}) copy-start(s32[320]{0:T(512)} %constant.95.clone) | copy-start | bytes 3844
  88.2 25.8 %copy-start.26 = (s32[320]{0:T(512)S(1)}, s32[320]{0:T(512)}, u32[]{:S(2)}) copy-start(s32[320]{0:T(512)} %constant.94.clone) | copy-start | bytes 3844
  113.8 3.5 %collective-permute-start.7 = (bf16[4,144,1280]{2,1,0:T(8,128)(2,1)}, bf16[4,144,1280]{2,1,0:T(8,128)(2,1)S(1)}, u32[]{:S(2)}, u32[]{:S(2)}) collective-permute-start(bf16[4,144,1280]{2,1,0:T(8,128)(2,1)} %get-tuple-element.97), channel_id=1, source_target_pairs={{0,1},{1,0},{2,3},{3,2},{4,5},{5,4},{6,7},{7,6},{8,9},{9,8},{10,11... | collective-permute-start | bytes 4423688 | tf_op jit(solution)/shard_map/ppermute | solution.py:25
  118.9 9.5 %collective-permute-start.12 = (bf16[4,144,1280]{2,1,0:T(8,128)(2,1)}, bf16[4,144,1280]{2,1,0:T(8,128)(2,1)}, u32[]{:S(2)}, u32[]{:S(2)}) collective-permute-start(bf16[4,144,1280]{2,1,0:T(8,128)(2,1)} %collective-permute-done.4.early0_ref), channel_id=1, source_target_pairs={{0,1},{1,0},{2,3},{3,2},{4,5},{5,4},{6,7},{7,6},{8,9},{9,8},{10,11... | collective-permute-start | bytes 4423688 | tf_op jit(solution)/shard_map/ppermute | solution.py:25
  119.0 9.3 %collective-permute-start.13 = (bf16[4,144,1280]{2,1,0:T(8,128)(2,1)}, bf16[4,144,1280]{2,1,0:T(8,128)(2,1)}, u32[]{:S(2)}, u32[]{:S(2)}) collective-permute-start(bf16[4,144,1280]{2,1,0:T(8,128)(2,1)} %collective-permute-done.5.early0_ref), channel_id=1, source_target_pairs={{0,1},{1,0},{2,3},{3,2},{4,5},{5,4},{6,7},{7,6},{8,9},{9,8},{10,11... | collective-permute-start | bytes 4423688 | tf_op jit(solution)/shard_map/ppermute | solution.py:25
  122.6 27.6 %collective-permute-start.8 = (bf16[2,160,1792]{2,1,0:T(8,128)(2,1)}, bf16[2,160,1792]{2,1,0:T(8,128)(2,1)}, u32[]{:S(2)}, u32[]{:S(2)}) collective-permute-start(bf16[2,160,1792]{2,1,0:T(8,128)(2,1)} %get-tuple-element.98), channel_id=1, source_target_pairs={{0,16},{8,24},{16,0},{24,8},{1,17},{9,25},{17,1},{25,9},{2,18},{10... | collective-permute-start | bytes 3440648 | tf_op jit(solution)/shard_map/ppermute | solution.py:25
  123.3 12.7 %copy-start = (bf16[5,128,1280]{2,1,0:T(8,128)(2,1)}, bf16[5,128,1280]{2,1,0:T(8,128)(2,1)S(1)}, u32[]{:S(2)}) copy-start(bf16[5,128,1280]{2,1,0:T(8,128)(2,1)S(1)} %pad_maximum_fusion.1.mine_ref) | copy-start | bytes 4915204
  123.3 39.9 %all-to-all-start.2 = ((bf16[4,144,1280]{2,1,0:T(8,128)(2,1)}), bf16[4,144,1280]{2,1,0:T(8,128)(2,1)S(1)}, u32[]{:S(2)}, u32[]{:S(2)}) async-start(bf16[4,144,1280]{2,1,0:T(8,128)(2,1)} %add_convert_fusion), calls=%async_computation.2 | async-start | bytes 2949120 | tf_op jit(solution)/shard_map/all_to_all | solution.py:35
  128.3 26.5 %collective-permute-start.15 = (bf16[5,128,1280]{2,1,0:T(8,128)(2,1)S(1)}, bf16[5,128,1280]{2,1,0:T(8,128)(2,1)}, u32[]{:S(2)}, u32[]{:S(2)}) collective-permute-start(bf16[5,128,1280]{2,1,0:T(8,128)(2,1)S(1)} %pad_maximum_fusion.1.mine_ref), channel_id=1, source_target_pairs={{0,1},{1,0},{2,3},{3,2},{4,5},{5,4},{6,7},{7,6},{8,9},{9,8},{10,11... | collective-permute-start | bytes 4915208 | tf_op jit(solution)/shard_map/ppermute | solution.py:25
  135.9 18.0 %copy-start.18 = (bf16[2,112,1280]{2,1,0:T(8,128)(2,1)S(1)}, bf16[2,112,1280]{2,1,0:T(8,128)(2,1)}, u32[]{:S(2)}) copy-start(bf16[2,112,1280]{2,1,0:T(8,128)(2,1)} %get-tuple-element.99) | copy-start | bytes 1720324
  135.9 23.7 %collective-permute-start.14 = (bf16[4,128,1280]{2,1,0:T(8,128)(2,1)}, bf16[4,128,1280]{2,1,0:T(8,128)(2,1)}, u32[]{:S(2)}, u32[]{:S(2)}) collective-permute-start(bf16[4,128,1280]{2,1,0:T(8,128)(2,1)} %get-tuple-element.107), channel_id=1, source_target_pairs={{0,1},{1,0},{2,3},{3,2},{4,5},{5,4},{6,7},{7,6},{8,9},{9,8},{10,11... | collective-permute-start | bytes 3932168 | tf_op jit(solution)/shard_map/ppermute | solution.py:25
  136.5 17.4 %collective-permute-start.10 = (bf16[2,112,1280]{2,1,0:T(8,128)(2,1)S(1)}, bf16[2,112,1280]{2,1,0:T(8,128)(2,1)S(1)}, u32[]{:S(2)}, u32[]{:S(2)}) collective-permute-start(bf16[2,112,1280]{2,1,0:T(8,128)(2,1)S(1)} %copy-done.31), channel_id=1, source_target_pairs={{0,8},{8,0},{16,24},{24,16},{1,9},{9,1},{17,25},{25,17},{2,10},{10... | collective-permute-start | bytes 1720328 | tf_op jit(solution)/shard_map/ppermute | solution.py:25
  150.2 31.9 %collective-permute-start.20 = (bf16[4,128,1280]{2,1,0:T(8,128)(2,1)}, bf16[4,128,1280]{2,1,0:T(8,128)(2,1)}, u32[]{:S(2)}, u32[]{:S(2)}) collective-permute-start(bf16[4,128,1280]{2,1,0:T(8,128)(2,1)} %all-to-all-done.1.ns0_ref), channel_id=1, source_target_pairs={{0,8},{8,0},{16,24},{24,16},{1,9},{9,1},{17,25},{25,17},{2,10},{10... | collective-permute-start | bytes 3932168 | tf_op jit(solution)/shard_map/ppermute | solution.py:25
  151.7 30.4 %collective-permute-start.18 = (bf16[4,128,1280]{2,1,0:T(8,128)(2,1)}, bf16[4,128,1280]{2,1,0:T(8,128)(2,1)}, u32[]{:S(2)}, u32[]{:S(2)}) collective-permute-start(bf16[4,128,1280]{2,1,0:T(8,128)(2,1)} %all-to-all-done.1.ns0_ref), channel_id=1, source_target_pairs={{0,16},{8,24},{16,0},{24,8},{1,17},{9,25},{17,1},{25,9},{2,18},{10... | collective-permute-start | bytes 3932168 | tf_op jit(solution)/shard_map/ppermute | solution.py:25
  164.4 18.3 %copy-start.8 = (bf16[2,112,1280]{2,1,0:T(8,128)(2,1)S(1)}, bf16[2,112,1280]{2,1,0:T(8,128)(2,1)}, u32[]{:S(2)}) copy-start(bf16[2,112,1280]{2,1,0:T(8,128)(2,1)} %add_convert_fusion.5) | copy-start | bytes 1720324
  182.1 15.0 %collective-permute-start.19 = (bf16[4,128,1280]{2,1,0:T(8,128)(2,1)}, bf16[4,128,1280]{2,1,0:T(8,128)(2,1)}, u32[]{:S(2)}, u32[]{:S(2)}) collective-permute-start(bf16[4,128,1280]{2,1,0:T(8,128)(2,1)} %collective-permute-done.18.ns_y_ref.ns0_ref), channel_id=1, source_target_pairs={{0,1},{1,0},{2,3},{3,2},{4,5},{5,4},{6,7},{7,6},{8,9},{9,8},{10,11... | collective-permute-start | bytes 3932168 | tf_op jit(solution)/shard_map/ppermute | solution.py:25
  182.2 15.8 %collective-permute-start.21 = (bf16[4,128,1280]{2,1,0:T(8,128)(2,1)}, bf16[4,128,1280]{2,1,0:T(8,128)(2,1)}, u32[]{:S(2)}, u32[]{:S(2)}) collective-permute-start(bf16[4,128,1280]{2,1,0:T(8,128)(2,1)} %collective-permute-done.20.ns0_ref), channel_id=1, source_target_pairs={{0,1},{1,0},{2,3},{3,2},{4,5},{5,4},{6,7},{7,6},{8,9},{9,8},{10,11... | collective-permute-start | bytes 3932168 | tf_op jit(solution)/shard_map/ppermute | solution.py:25
  183.4 37.3 %collective-permute-start.11 = (bf16[112,1280]{1,0:T(8,128)(2,1)}, bf16[112,1280]{1,0:T(8,128)(2,1)}, u32[]{:S(2)}, u32[]{:S(2)}) collective-permute-start(bf16[112,1280]{1,0:T(8,128)(2,1)} %slice_bitcast_fusion.2), channel_id=1, source_target_pairs={{0,16},{8,24},{16,0},{24,8},{1,17},{9,25},{17,1},{25,9},{2,18},{10... | collective-permute-start | bytes 860168 | tf_op jit(solution)/shard_map/ppermute | solution.py:25
  188.8 31.9 %collective-permute-start.9 = (bf16[160,1792]{1,0:T(8,128)(2,1)}, bf16[160,1792]{1,0:T(8,128)(2,1)}, u32[]{:S(2)}, u32[]{:S(2)}) collective-permute-start(bf16[160,1792]{1,0:T(8,128)(2,1)} %slice_bitcast_fusion), channel_id=1, source_target_pairs={{0,8},{8,0},{16,24},{24,16},{1,9},{9,1},{17,25},{25,17},{2,10},{10... | collective-permute-start | bytes 1720328 | tf_op jit(solution)/shard_map/ppermute | solution.py:25
  192.1 35.0 %all-to-all-start.3 = ((bf16[4,128,1280]{2,1,0:T(8,128)(2,1)}), bf16[4,128,1280]{2,1,0:T(8,128)(2,1)S(1)}, u32[]{:S(2)}, u32[]{:S(2)}) async-start(bf16[4,128,1280]{2,1,0:T(8,128)(2,1)} %add_convert_fusion.1), calls=%async_computation.3 | async-start | bytes 2621440 | tf_op jit(solution)/shard_map/all_to_all | solution.py:35
  195.8 24.9 %collective-permute-start.16 = (bf16[256,1280]{1,0:T(8,128)(2,1)}, bf16[256,1280]{1,0:T(8,128)(2,1)}, u32[]{:S(2)}, u32[]{:S(2)}) collective-permute-start(bf16[256,1280]{1,0:T(8,128)(2,1)} %slice.52), channel_id=1, source_target_pairs={{0,8},{8,0},{16,24},{24,16},{1,9},{9,1},{17,25},{25,17},{2,10},{10... | collective-permute-start | bytes 1966088 | tf_op jit(solution)/shard_map/ppermute | solution.py:25
  197.1 23.7 %collective-permute-start.17 = (bf16[288,1280]{1,0:T(8,128)(2,1)}, bf16[288,1280]{1,0:T(8,128)(2,1)}, u32[]{:S(2)}, u32[]{:S(2)}) collective-permute-start(bf16[288,1280]{1,0:T(8,128)(2,1)} %slice.53), channel_id=1, source_target_pairs={{0,16},{8,24},{16,0},{24,8},{1,17},{9,25},{17,1},{25,9},{2,18},{10... | collective-permute-start | bytes 2211848 | tf_op jit(solution)/shard_map/ppermute | solution.py:25
  220.7 11.5 %collective-permute-start.22 = (bf16[544,1280]{1,0:T(8,128)(2,1)S(1)}, bf16[544,1280]{1,0:T(8,128)(2,1)}, u32[]{:S(2)}, u32[]{:S(2)}) collective-permute-start(bf16[544,1280]{1,0:T(8,128)(2,1)S(1)} %copy-done.3), channel_id=1, source_target_pairs={{0,1},{1,0},{2,3},{3,2},{4,5},{5,4},{6,7},{7,6},{8,9},{9,8},{10,11... | collective-permute-start | bytes 4177928 | tf_op jit(solution)/shard_map/ppermute | solution.py:25
  223.6 8.6 %collective-permute-start.23 = (bf16[256,1280]{1,0:T(8,128)(2,1)}, bf16[256,1280]{1,0:T(8,128)(2,1)}, u32[]{:S(2)}, u32[]{:S(2)}) collective-permute-start(bf16[256,1280]{1,0:T(8,128)(2,1)} %collective-permute-done.16.qx_ref), channel_id=1, source_target_pairs={{0,1},{1,0},{2,3},{3,2},{4,5},{5,4},{6,7},{7,6},{8,9},{9,8},{10,11... | collective-permute-start | bytes 1966088 | tf_op jit(solution)/shard_map/ppermute | solution.py:25
  224.1 8.1 %collective-permute-start.24 = (bf16[288,1280]{1,0:T(8,128)(2,1)}, bf16[288,1280]{1,0:T(8,128)(2,1)}, u32[]{:S(2)}, u32[]{:S(2)}) collective-permute-start(bf16[288,1280]{1,0:T(8,128)(2,1)} %collective-permute-done.17.by_ref), channel_id=1, source_target_pairs={{0,1},{1,0},{2,3},{3,2},{4,5},{5,4},{6,7},{7,6},{8,9},{9,8},{10,11... | collective-permute-start | bytes 2211848 | tf_op jit(solution)/shard_map/ppermute | solution.py:25
  227.1 41.4 %all-to-all-start.4 = ((bf16[4,40,3072]{2,1,0:T(8,128)(2,1)}), bf16[4,40,3072]{2,1,0:T(8,128)(2,1)}, u32[]{:S(2)}, u32[]{:S(2)}) async-start(bf16[4,40,3072]{2,1,0:T(8,128)(2,1)} %fusion.10), calls=%async_computation.4 | async-start | bytes 1966080 | tf_op jit(solution)/shard_map/all_to_all | solution.py:35
  240.7 24.8 %collective-permute-start.25 = (bf16[160,2560]{1,0:T(8,128)(2,1)}, bf16[160,2560]{1,0:T(8,128)(2,1)}, u32[]{:S(2)}, u32[]{:S(2)}) collective-permute-start(bf16[160,2560]{1,0:T(8,128)(2,1)} %get-tuple-element.135), channel_id=1, source_target_pairs={{0,16},{8,24},{16,0},{24,8},{1,17},{9,25},{17,1},{25,9},{2,18},{10... | collective-permute-start | bytes 2457608 | tf_op jit(solution)/shard_map/ppermute | solution.py:25
  241.7 23.8 %copy-start.14 = (bf16[160,2560]{1,0:T(8,128)(2,1)S(1)}, bf16[160,2560]{1,0:T(8,128)(2,1)}, u32[]{:S(2)}) copy-start(bf16[160,2560]{1,0:T(8,128)(2,1)} %get-tuple-element.134) | copy-start | bytes 2457604
  241.7 25.2 %collective-permute-start.26 = (bf16[160,2688]{1,0:T(8,128)(2,1)}, bf16[160,2688]{1,0:T(8,128)(2,1)S(1)}, u32[]{:S(2)}, u32[]{:S(2)}) collective-permute-start(bf16[160,2688]{1,0:T(8,128)(2,1)} %get-tuple-element.141), channel_id=1, source_target_pairs={{0,8},{8,0},{16,24},{24,16},{1,9},{9,1},{17,25},{25,17},{2,10},{10... | collective-permute-start | bytes 2580488 | tf_op jit(solution)/shard_map/ppermute | solution.py:25
  268.5 51.0 %all-to-all-start.5 = ((bf16[4,40,5248]{2,1,0:T(8,128)(2,1)}), bf16[4,40,5248]{2,1,0:T(8,128)(2,1)S(1)}, u32[]{:S(2)}, u32[]{:S(2)}) async-start(bf16[4,40,5248]{2,1,0:T(8,128)(2,1)} %bitcast.11), calls=%async_computation.5 | async-start | bytes 3358720 | tf_op jit(solution)/shard_map/all_to_all | solution.py:35
  273.6 38.8 %collective-permute-start.28 = (bf16[6720,128]{1,0:T(8,128)(2,1)}, bf16[6720,128]{1,0:T(8,128)(2,1)}, u32[]{:S(2)}, u32[]{:S(2)}) collective-permute-start(bf16[6720,128]{1,0:T(8,128)(2,1)} %get-tuple-element.147), channel_id=1, source_target_pairs={{0,8},{8,0},{16,24},{24,16},{1,9},{9,1},{17,25},{25,17},{2,10},{10... | collective-permute-start | bytes 5160968 | tf_op jit(solution)/shard_map/ppermute | solution.py:25
  274.8 38.5 %collective-permute-start.27 = (bf16[6720,128]{1,0:T(8,128)(2,1)}, bf16[6720,128]{1,0:T(8,128)(2,1)}, u32[]{:S(2)}, u32[]{:S(2)}) collective-permute-start(bf16[6720,128]{1,0:T(8,128)(2,1)} %get-tuple-element.146), channel_id=1, source_target_pairs={{0,16},{8,24},{16,0},{24,8},{1,17},{9,25},{17,1},{25,9},{2,18},{10... | collective-permute-start | bytes 5160968 | tf_op jit(solution)/shard_map/ppermute | solution.py:25
  (20 other events, 92.9 us)

commit v3 on v2

--- a/solution.py
+++ b/solution.py
@@ -297,9 +297,16 @@
 
 
 def routed_grads_kernel(
-    expert_count, slot, ids, x_ref, dg_ref, du_ref, hid_ref, row_gate_ref, dy_ref, ns0_ref, ns1_ref, early0_ref, early1_ref,
-    gate_ref, up_ref, down_ref, router_ref, sel_d_ref, sel_f_ref, send_ref, keep_ref, far_x, far_dy,
+    expert_count, slot, ids, row_gate_ref, ns0_ref, ns1_ref, early0_ref, early1_ref, router_ref, *refs,
 ):
+    late, (send_ref, keep_ref, far_x, far_dy), bufs, sems = refs[:10], refs[10:14], refs[14:24], refs[24]
+    copies = []
+    for i, (ref, buf) in enumerate(zip(late, bufs)):
+        source = ref.at[slot] if len(ref.shape) == 3 else ref
+        copies.append(pltpu.make_async_copy(source, buf, sems.at[i]))
+    for copy in copies:
+        copy.start()
+    gate_ref, up_ref, down_ref, sel_d_ref, x_ref, sel_f_ref, hid_ref, dg_ref, du_ref, dy_ref = bufs
     expert = ids[slot]
     sources, length, width = ns0_ref.shape
     rows = far_x.shape[0]
@@ -313,23 +320,28 @@
     x = far_x[...]
     row_gate = gates_of(x, router_ref[...], expert, expert_count)
     d_far = (far_dy[...].astype(F32) * row_gate).astype(BF)
-    g = dot_nn(x, gate_ref[0])
-    u = dot_nn(x, up_ref[0])
+    copies[0].wait()
+    g = dot_nn(x, gate_ref[...])
+    copies[1].wait()
+    u = dot_nn(x, up_ref[...])
     sig = jax.nn.sigmoid(g)
     act = g * sig
     hid = (act * u).astype(BF)
-    dh = dot_nt(d_far, down_ref[0])
+    copies[2].wait()
+    dh = dot_nt(d_far, down_ref[...])
     dg = (dh * u * sig * (1.0 + g * (1.0 - sig))).astype(BF)
     du = (dh * act).astype(BF)
+    for copy in copies[3:]:
+        copy.wait()
     x_t = dot_nt(sel_d_ref[...], x).astype(BF)
-    x_own = dot_nt(sel_d_ref[...], x_ref[0]).astype(BF)
+    x_own = dot_nt(sel_d_ref[...], x_ref[...]).astype(BF)
     hid_t = dot_nt(sel_f_ref[...], hid).astype(BF)
-    hid_own = dot_nt(sel_f_ref[...], hid_ref[0]).astype(BF)
-    d_own = (dy_ref[0].astype(F32) * row_gate_ref[0, :, :1]).astype(BF)
+    hid_own = dot_nt(sel_f_ref[...], hid_ref[...]).astype(BF)
+    d_own = (dy_ref[...].astype(F32) * row_gate_ref[0, :, :1]).astype(BF)
     start = 0
     for value in (
-        dot_nn(x_own, dg_ref[0]) + dot_nn(x_t, dg),
-        dot_nn(x_own, du_ref[0]) + dot_nn(x_t, du),
+        dot_nn(x_own, dg_ref[...]) + dot_nn(x_t, dg),
+        dot_nn(x_own, du_ref[...]) + dot_nn(x_t, du),
         dot_nn(hid_own, d_own) + dot_nn(hid_t, d_far),
     ):
         size = value.shape[0] // 2
@@ -342,25 +354,26 @@
 
 def routed_grads(slot, selectors, ids, own, far, weights, router, expert_count):
     gate, up, down = weights
-    _, rows, width = own[0].shape
+    x, dg, du, hid, row_gate, dy = own
+    _, rows, width = x.shape
     ff = gate.shape[2]
-    at = lambda v: pl.BlockSpec(
-        (1,) + v.shape[1:], lambda i, _: (slot, 0, 0), pipeline_mode=pl.Buffered(1)
-    )
     shape = (3 * width * ff // 4 // LANES, LANES)
-    rest = far + [router, *selectors]
-    rest_specs = [once(v.shape) for v in rest]
+    late = [gate, up, down, selectors[0], x, selectors[1], hid, dg, du, dy]
     return pl.pallas_call(
         functools.partial(routed_grads_kernel, expert_count, slot),
         grid_spec=pltpu.PrefetchScalarGridSpec(
             num_scalar_prefetch=1,
             grid=(1,),
-            in_specs=[at(v) for v in own]
-            + rest_specs[: len(far)]
-            + [at(v) for v in weights]
-            + rest_specs[len(far) :],
+            in_specs=[
+                pl.BlockSpec((1, rows, LANES), lambda i, _: (slot, 0, 0), pipeline_mode=pl.Buffered(1))
+            ]
+            + [once(v.shape) for v in far]
+            + [once(router.shape)]
+            + [pl.BlockSpec(memory_space=pl.ANY)] * len(late),
             out_specs=[once(shape)] * 2,
-            scratch_shapes=[pltpu.VMEM((rows, width), BF)] * 2,
+            scratch_shapes=[pltpu.VMEM((rows, width), BF)] * 2
+            + [pltpu.VMEM(v.shape[-2:], BF) for v in late]
+            + [pltpu.SemaphoreType.DMA((len(late),))],
         ),
         out_shape=[jax.ShapeDtypeStruct(shape, BF)] * 2,
         compiler_params=pltpu.CompilerParams(vmem_limit_bytes=VMEM_LIMIT),
@@ -370,7 +383,7 @@
             transcendentals=0,
         ),
         name="routed_grads",
-    )(ids, *own, *far, *weights, *rest[len(far) :])
+    )(ids, row_gate, *far, router, *late)
 
 
 def finish_kernel(slots, *refs):
@@ -496,12 +509,12 @@
     cos_ref, sin_ref, q_ref, k_ref, v_ref, wq_ref, wk_ref, wv_ref, wo_ref, *refs,
 ):
     parts = refs[0]
-    cat_ref, grad_ref, branch_ref, d_res_ref, acc_ref = refs[1:]
+    qk_ref, rest_ref, grad_ref, branch_ref, d_res_ref, acc_ref = refs[1:]
     i = pl.program_id(0)
     length, width = x_ref.shape
     step = wq_ref.shape[1]
     here = pl.multiple_of(i * step, step)
-    gains = slice(4 * length, 4 * length + 16)
+    gains = slice(2 * length, 2 * length + 16)
 
     @pl.when(i == 0)
     def _():
@@ -519,18 +532,18 @@
         probs = terms / jnp.sum(terms, 0, keepdims=True)
         d_logits = probs * (d_probs - jnp.sum(probs * d_probs, 0, keepdims=True))
         d_logits = jnp.where(row < expert_count, d_logits, 0.0).astype(BF)
-        cat_ref[4 * length + 16 :] = jnp.zeros((d_logits.shape[0], width), BF)
-        cat_ref[4 * length + 16 :, :length] = d_logits
+        rest_ref[2 * length + 16 :] = jnp.zeros((d_logits.shape[0], width), BF)
+        rest_ref[2 * length + 16 :, :length] = d_logits
         d_normed = shared_ref[...] + back + dot_tn(d_logits, router_t_ref[...])
         unit, scale = unit_of(residual_ref[...])
         c = d_normed * gain2_ref[...][None]
         gain_row = jnp.sum(d_normed * unit, 0, keepdims=True)
         which = lax.broadcasted_iota(jnp.int32, (16, width), 0)
-        cat_ref[gains] = jnp.where(which == 1, gain_row, 0.0).astype(BF)
+        rest_ref[gains] = jnp.where(which == 1, gain_row, 0.0).astype(BF)
         d_res = dy_ref[...].astype(F32) + scale * (c - unit * jnp.mean(c * unit, -1, keepdims=True))
         d_res_ref[...] = d_res
         branch_ref[...] = d_res.astype(BF)
-        cat_ref[3 * length : 4 * length] = d_res.astype(BF)
+        rest_ref[length : 2 * length] = d_res.astype(BF)
         acc_ref[...] = jnp.zeros_like(acc_ref)
 
     cosine, sine = cos_ref[...], -sin_ref[...]
@@ -547,8 +560,9 @@
         d_k.append(turn(dot_tn(d_scores, q) * att_scale, cosine, sine).astype(BF))
         d_v.append(dot_tn(probs.astype(BF), d_attended).astype(BF))
     d_q, d_k, d_v = (jnp.concatenate(v, 1) for v in (d_q, d_k, d_v))
-    for n, v in enumerate((d_q, d_k, d_v)):
-        cat_ref[n * length : (n + 1) * length, pl.ds(here, step)] = v
+    qk_ref[:length, pl.ds(here, step)] = d_q
+    qk_ref[length:, pl.ds(here, step)] = d_k
+    rest_ref[:length, pl.ds(here, step)] = d_v
     acc_ref[...] += dot_nt(d_q, wq_ref[...]) + dot_nt(d_k, wk_ref[...]) + dot_nt(d_v, wv_ref[...])
 
     @pl.when(i == pl.num_programs(0) - 1)
@@ -558,7 +572,7 @@
         c = d_normed * gain1_ref[...][None]
         gain_row = jnp.sum(d_normed * unit, 0, keepdims=True)
         which = lax.broadcasted_iota(jnp.int32, (16, width), 0)
-        cat_ref[gains] = jnp.where(which == 0, gain_row, cat_ref[gains].astype(F32)).astype(BF)
+        rest_ref[gains] = jnp.where(which == 0, gain_row, rest_ref[gains].astype(F32)).astype(BF)
         grad_ref[...] = d_res_ref[...] + scale * (c - unit * jnp.mean(c * unit, -1, keepdims=True))
 
 
@@ -581,7 +595,8 @@
         + [pl.BlockSpec((step, width), lambda i: (i, 0))]
         + [whole(parts.shape)],
         out_specs=[
-            whole((4 * length + 16 + router_t.shape[0], width)),
+            whole((2 * length, width)),
+            whole((2 * length + 16 + router_t.shape[0], width)),
             tall,
         ],
         scratch_shapes=[
@@ -590,7 +605,8 @@
             pltpu.VMEM((length, width), F32),
         ],
         out_shape=[
-            jax.ShapeDtypeStruct((4 * length + 16 + router_t.shape[0], width), BF),
+            jax.ShapeDtypeStruct((2 * length, width), BF),
+            jax.ShapeDtypeStruct((2 * length + 16 + router_t.shape[0], width), BF),
             jax.ShapeDtypeStruct((length, width), F32),
         ],
         compiler_params=pltpu.CompilerParams(vmem_limit_bytes=VMEM_LIMIT),
@@ -657,7 +673,7 @@
 
 
 def last_grads_kernel(
-    length, at_ns, z_ref, mine_ref, other_ref, qx_ref, qxo_ref, by_ref, byo_ref, a_ref, v_ref, o_ref,
+    length, at_ns, z_ref, mine_ref, other_ref, rest_ref, rest_other_ref, qx_ref, qxo_ref, by_ref, byo_ref, a_ref, v_ref, o_ref,
     ns_ref, cat_other_ref, ns_y_ref, ns_yo_ref, order_b_ref,
     a_send, a_keep, b_send, b_keep,
 ):
@@ -673,12 +689,11 @@
         at = slice(i * length, (i + 1) * length)
         tokens = join(mine_ref[at], other_ref[at], qx_ref[at], qxo_ref[at])
         put(dot_nn(a_ref[...], tokens), a_keep, a_send, slice(i * width, (i + 1) * width))
-        past = slice((2 + i) * length, (3 + i) * length)
-        tokens = join(mine_ref[past], other_ref[past], by_ref[at], byo_ref[at])
+        tokens = join(rest_ref[at], rest_other_ref[at], by_ref[at], byo_ref[at])
         left = (v_ref, o_ref)[i]
         put(dot_nn(left[...], tokens), b_keep, b_send, slice(i * width, (i + 1) * width))
-    start = 4 * length
-    refs = ((mine_ref, start), (other_ref, start), (by_ref, start - 2 * length), (byo_ref, start - 2 * length))
+    start = 2 * length
+    refs = ((rest_ref, start), (rest_other_ref, start), (by_ref, start), (byo_ref, start))
     gains = sum(ref[i : i + 16].astype(F32) for ref, i in refs).astype(BF)
     logits = jnp.concatenate([ref[i + 16 :, :length] for ref, i in refs], 1)
     ns = join(
@@ -747,13 +762,17 @@
     my_z = my_ex // 2
     first_x = partner(normed_first, "dp", 1)
     first_y = partner(jnp.stack([normed_first, attended]), "dp", 2)
-    ns = spread(after(normed_second, early, from_shared, first_x, first_y))
+    selectors = [(keep_rows(w, q), keep_rows(ff, q)) for q in (2, 1)]
+    order_f = rows_for(ff, (1, 3, 0, 2))
+    ns = spread(
+        after(normed_second, early, from_shared, first_x, first_y, selectors, order_a, order_b, order_d, order_f)
+    )
     from_other = over_core(from_shared)
     part_d, part_f = w // (2 * n_dp), ff // (2 * n_dp)
     su_send, su_keep, sd_send, sd_keep = call(
         functools.partial(shared_grads_kernel, ff, w), "shared_grads",
         [((2, part_d, 2 * ff), BF)] * 2 + [((2, part_f, w), BF)] * 2,
-        from_shared, from_other, order_d, rows_for(ff, (1, 3, 0, 2)),
+        from_shared, from_other, order_d, order_f,
     )
     early_other = over_core(early)
     early_x, early_y = partner(early, "dp", 1), partner(early, "dp", 2)
@@ -771,9 +790,8 @@
     ns_far, su_send, sd_send, early_x, early_y = after((ns, su_send, sd_send, early_x, early_y), back_sum)
     early_x_other, early_y_other = over_core(early_x), over_core(early_y)
     su_got, sd_got = partner(su_send, "dp", 2), partner(sd_send, "dp", 1)
-    ns_far = after(ns_far, su_got)
-    ns_x, ns_y = partner(ns_far, "dp", 1), partner(ns_far, "dp", 2)
     su, sd = plus(su_keep, su_got), plus(sd_keep, sd_got)
+    su_sum, sd_sum = su, sd
     su_last, sd_last = partner(su[1], "dp", 1), partner(sd[1], "dp", 2)
     su, sd = plus(su[0], su_last), plus(sd[0], sd_last)
 
@@ -784,25 +802,24 @@
     left_a, left_v, left_o = call(
         lefts_kernel, "lefts", [left_shape] * 3, lefts, lefts_other, order_a, order_b,
     )
+    ns_y = partner(after(ns_far, su_got, left_a), "dp", 2)
     combined_mine, combined_other = combine(after(hid, early_x_other, early_y_other), row_gate, pick, routed_down)
+    ns_x = partner(after(ns_far, combined_mine), "dp", 1)
     combined = plus(combined_mine, over_core(combined_other))
-    selectors = [(keep_rows(w, q), keep_rows(ff, q)) for q in (2, 1)]
-    back = after(back, combined, left_a, selectors)
+    back = after(back, combined, left_a, su_sum, sd_sum)
     combined = exchange_z(after(combined, back))
 
     high = -(-expert_count // 16) * 16
     router_t = jnp.pad(w_router.T, ((0, high - expert_count), (0, 0)))
-    d_cat, grad_inputs = backward(
+    d_qk, d_rest, grad_inputs = backward(
         tokens, cotangent, residual, normed_second, shared_back, router_t, gain1, gain2, cosine, sine,
         queries, key_rows, value_rows, w_query, w_key, w_value, w_out, back, expert_count,
     )
 
-    d_out = d_cat
-    qk_x, b_y = partner(d_out[: 2 * length], "dp", 1), partner(d_out[2 * length :], "dp", 2)
-    far_x = [ns_x, over_core(after(ns_x, d_cat)), early_x, early_x_other]
-
-    far_y = [ns_y, over_core(after(ns_y, d_cat)), early_y, early_y_other]
-    far = [far_x, far_y]
+    qk_x, b_y = partner(d_qk, "dp", 1), partner(d_rest, "dp", 2)
+    far_x = [ns_x, over_core(after(ns_x, d_qk)), early_x, early_x_other]
+
+    far = [far_x]
 
     def slot_grads(slot, last_dg):
         return routed_grads(
@@ -810,15 +827,16 @@
             far[slot % 2], [routed_gate, routed_up, routed_down], router_wide, expert_count,
         )
 
-    routed = [slot_grads(0, after(dg, d_cat, far_y[1]))]
-    d_cat, qk_x, b_y = after((d_cat, qk_x, b_y), routed[0], su_last, sd_last)
-
-    cat_other = over_core(d_cat)
+    routed = [slot_grads(0, after(dg, d_qk, ns_y))]
+    d_qk, d_rest, qk_x, b_y = after((d_qk, d_rest, qk_x, b_y), routed[0], su_last, sd_last)
+    qk_other, rest_other = over_core(d_qk), over_core(d_rest)
+    far_y = [ns_y, over_core(after(ns_y, routed[0])), early_y, early_y_other]
+    far.append(far_y)
     qk_x_other, b_y_other = over_core(qk_x), over_core(b_y)
     a_send, a_keep, b_send, b_keep = call(
         functools.partial(last_grads_kernel, length, 3 * ff), "last_grads",
         [((w // 8, 2 * w), BF)] * 2 + [((w // 8, 2 * w + LANES), BF)] * 2,
-        my_z[None], d_cat, cat_other, qk_x, qk_x_other, b_y, b_y_other, left_a, left_v, left_o,
+        my_z[None], d_qk, qk_other, d_rest, rest_other, qk_x, qk_x_other, b_y, b_y_other, left_a, left_v, left_o,
         normed_second, from_other, far_y[0], far_y[1], order_b, scalars=1,
     )
     a_got, b_got = partner(a_send, "dp", 2), partner(b_send, "dp", 1)

time: 331 us -> 326 us (0.985)
  Pallas kernels: 148 us -> 143 us
  local copies, waits for them, and re-layouts: 17.3 us -> 13.8 us
    pallas_call x2, Pallas kernels: 45.6 us -> 40.5 us  [routed_grads(): pl.pallas_call(functools.partial(routed_grads_kernel, expert_count, slot)...]
    ppermute x29 -> x30, starting transfers between devices: 22.1 us -> 21 us  [partner(): return lax.ppermute(v, axis, [(i, i ^ mask) for i in range(n)])]
    ppermute x29 -> x30, waiting for transfers between devices: 69.4 us -> 70.4 us  [partner(): return lax.ppermute(v, axis, [(i, i ^ mask) for i in range(n)])]
  transfers between devices with their start and end apart: 35 -> 36, of which waited for: 12 -> 12; matrix products, arithmetic and copies ran while one was open for 10% -> 9% of each run, Pallas kernels for 39% -> 38%
where the time goes in v3:
time: 326 us; the launch traced here: 320 us
  Pallas kernels  143 us (44%)
  waiting for transfers between devices  78.9 us (24%)
  starting transfers between devices  52 us (16%)
  other arithmetic  30.9 us (9%)
  local copies, waits for them, and re-layouts  13.8 us (4%)
    ppermute x30, waiting for transfers between devices, partner(): return lax.ppermute(v, axis, [(i, i ^ mask) for i in range(n)])  70.4 us
    pallas_call x2, Pallas kernels, routed_grads(): pl.pallas_call(functools.partial(routed_grads_kernel, expert_count, slot)...  40.5 us
    all_to_all x6, starting transfers between devices, exchange_z(): lax.all_to_all(s, 'expert', 0, 0, tiled=True, axis_index_groups=groups)  31 us
    pallas_call x4, Pallas kernels, call(): pl.pallas_call(kernel, in_specs=[pl.BlockSpec(memory_space=pltpu.SMEM)] *...  26.4 us
    pallas_call x1, Pallas kernels, experts(): pl.pallas_call(functools.partial(experts_kernel, expert_count), grid_spec...  22.1 us
    ppermute x30, starting transfers between devices, partner(): return lax.ppermute(v, axis, [(i, i ^ mask) for i in range(n)])  21 us
    pallas_call x1, Pallas kernels, backward(): pl.pallas_call(functools.partial(backward_kernel, expert_count), grid=(wi...  17.7 us
    convert_element_type x8, other arithmetic, plus(): return (a.astype(F32) + b.astype(F32)).astype(BF)  14.1 us
  transfers between devices with their start and end apart: 36, of which 12 were waited for; matrix products, arithmetic and copies ran while one was open for 9% of the time, Pallas kernels for 38%

profile of v3, /device:TPU:0, one launch (start us, length us, event | category | flops | bytes accessed | tf_op | source)
XLA Modules:
  0.0 319.8 jit_solution(127672218673256104)
XLA Ops:
  3.5 6.3 %all-to-all-start = ((bf16[4,144,1280]{2,1,0:T(8,128)(2,1)}), bf16[4,144,1280]{2,1,0:T(8,128)(2,1)S(1)}, u32[]{:S(2)}, u32[]{:S(2)}) async-start(bf16[4,144,1280]{2,1,0:T(8,128)(2,1)} %broadcast_in_dim.8), calls=%async_computation | async-start | bytes 2949120 | tf_op jit(solution)/shard_map/all_to_all | solution.py:35
  9.9 11.5 %attention.1 = (bf16[128,1280]{1,0:T(8,128)(2,1)}, bf16[128,1280]{1,0:T(8,128)(2,1)}, bf16[128,1280]{1,0:T(8,128)(2,1)}, bf16[128,1280]{1,0:T(8,128)(2,1)}, bf16...) custom-call(bf16[128,1280]{1,0:T(8,128)(2,1)} %x_ref.3, f32[1280]{0:T(1024)} %gain1_ref.3, ...), custom_call_target="tpu_custom_call" | custom-call | flops 1677721600 | bytes 13107200 | tf_op jit(solution)/shard_map/attention/pallas_call | solution.py:482
  21.4 1.6 collective-permute-start.1
  24.1 1.6 collective-permute-start.2
  28.1 1.5 fusion.order_d_ref
  29.6 2.2 fusion.1
  31.9 7.3 %shared.1 = (bf16[128,5248]{1,0:T(8,128)(2,1)}, f32[128,1280]{1,0:T(8,128)}, f32[128,1280]{1,0:T(8,128)}) custom-call(bf16[128,1280]{1,0:T(8,128)(2,1)} %get-tuple-element.93.ns_ref, bf16[128,1280]{1,0:T(8,128)(2,1)} %dy_ref.3, bf16[1280,896]{1,0:T(8,128)(2,1)} %gate_ref.2, bf16[1280,896]{1,0:T(8,128)(2,1)} %up_ref.2, bf16[896,1280]{1,0:T(8,128)(2,1)} %down_ref.3), custom_call_target="tpu_custom_call" | custom-call | flops 1 | bytes 1 | tf_op jit(solution)/shard_map/shared/pallas_call | solution.py:624
  40.4 1.5 fusion.7
  41.9 2.8 all-to-all-done.early_ref
  46.0 4.6 %all-to-all-start.1 = ((bf16[4,128,1280]{2,1,0:T(8,128)(2,1)}), bf16[4,128,1280]{2,1,0:T(8,128)(2,1)}, u32[]{:S(2)}, u32[]{:S(2)}) async-start(bf16[4,128,1280]{2,1,0:T(8,128)(2,1)} %broadcast_in_dim.9), calls=%async_computation.1 | async-start | bytes 2621440 | tf_op jit(solution)/shard_map/all_to_all | solution.py:35
  50.7 1.6 collective-permute-start.5
  52.3 1.5 collective-permute-start.4
  54.4 2.7 collective-permute-done.other_ref.cat_other_ref
  58.2 6.0 %shared_grads.1 = (bf16[2,160,1792]{2,1,0:T(8,128)(2,1)}, bf16[2,160,1792]{2,1,0:T(8,128)(2,1)}, bf16[2,112,1280]{2,1,0:T(8,128)(2,1)}, bf16[2,112,1280]{2,1,0:T(8,128)(2,1)}) custom-call(bf16[128,5248]{1,0:T(8,128)(2,1)} %get-tuple-element.89.cat_ref, bf16[128,5248]{1,0:T(8,128)(2,1)} %copy-done.3, bf16[640,1280]{1,0:T(8,128)(2,1)} %fusion.order_d_ref, ...), custom_call_target="tpu_custom_call" | custom-call | flops 1 | bytes 1 | tf_op jit(solution)/shard_map/shared_grads/pallas_call | solution.py:624
  64.2 10.8 %prepare.1 = (bf16[2,8,64,128]{3,2,1,0:T(8,128)(2,1)}, f32[2,512,896]{2,1,0:T(8,128)}, bf16[2,512,1280]{2,1,0:T(8,128)(2,1)}) custom-call(s32[2]{0:T(128)} %dynamic_slice.3.ids, bf16[4,144,1280]{2,1,0:T(8,128)(2,1)} %copy-done.2, bf16[4,144,1280]{2,1,0:T(8,128)(2,1)} %collective-permute-done.3.other_ref, bf16[2,896,1280]{2,1,0:T(8,128)(2,1)} %refs_2_.3), custom_call_target="tpu_custom_call" | custom-call | flops 1 | bytes 1 | tf_op jit(solution)/shard_map/prepare/pallas_call | solution.py:118
  74.9 10.5 %collective-permute-done.5.early0_ref = bf16[4,144,1280]{2,1,0:T(8,128)(2,1)} collective-permute-done((bf16[4,144,1280]{2,1,0:T(8,128)(2,1)S(1)}, bf16[4,144,1280]{2,1,0:T(8,128)(2,1)}, u32[]{:S(2)}, u32[]{:S(2)}) %collective-permute-start.5) | collective-permute-done | bytes 1474592 | tf_op jit(solution)/shard_map/ppermute | solution.py:25
  85.5 1.2 collective-permute-done.4.early0_ref
  87.8 2.2 collective-permute-done.6.ns1_ref
  91.1 22.1 %experts.1 = (bf16[4,144,1280]{2,1,0:T(8,128)(2,1)}, bf16[4,144,1280]{2,1,0:T(8,128)(2,1)}, bf16[2,512,896]{2,1,0:T(8,128)(2,1)}, bf16[2,512,896]{2,1,0:T(8,128)...) custom-call(s32[2]{0:T(128)} %dynamic_slice.3.ids, ...), custom_call_target="tpu_custom_call" | custom-call | flops 9395240960 | bytes 14680064 | tf_op jit(solution)/shard_map/experts/pallas_call | solution.py:210
  113.4 3.3 %collective-permute-done.7 = bf16[4,144,1280]{2,1,0:T(8,128)(2,1)S(1)} collective-permute-done((bf16[4,144,1280]{2,1,0:T(8,128)(2,1)}, bf16[4,144,1280]{2,1,0:T(8,128)(2,1)S(1)}, u32[]{:S(2)}, u32[]{:S(2)}) %collective-permute-start.7) | collective-permute-done | bytes 1474592 | tf_op jit(solution)/shard_map/ppermute | solution.py:25
  116.7 2.9 add_convert_fusion
  120.4 5.3 %all-to-all-start.2 = ((bf16[4,144,1280]{2,1,0:T(8,128)(2,1)}), bf16[4,144,1280]{2,1,0:T(8,128)(2,1)S(1)}, u32[]{:S(2)}, u32[]{:S(2)}) async-start(bf16[4,144,1280]{2,1,0:T(8,128)(2,1)} %add_convert_fusion), calls=%async_computation.2 | async-start | bytes 2949120 | tf_op jit(solution)/shard_map/all_to_all | solution.py:35
  125.8 1.6 collective-permute-start.10
  127.8 7.6 %combine.1 = (bf16[4,128,1280]{2,1,0:T(8,128)(2,1)}, bf16[4,128,1280]{2,1,0:T(8,128)(2,1)}) custom-call(bf16[2,512,896]{2,1,0:T(8,128)(2,1)} %get-tuple-element.107.hid_ref.refs_6_, f32[2,512,128]{2,1,0:T(8,128)} %get-tuple-element.108.row_gate_ref, bf16[2,8,64,128]{3,2,1,0:T(8,128)(2,1)} %get-tuple-element.94.pick_ref, bf16[2,896,1280]{2,1,0:T(8,128)(2,1)} %refs_2_.3), custom_call_target="tpu_custom_call" | custom-call | flops 5368709120 | bytes 6422528 | tf_op jit(solution)/shard_map/combine/pallas_call | solution.py:275
  136.6 4.3 %collective-permute-done.10 = bf16[2,112,1280]{2,1,0:T(8,128)(2,1)} collective-permute-done((bf16[2,112,1280]{2,1,0:T(8,128)(2,1)}, bf16[2,112,1280]{2,1,0:T(8,128)(2,1)}, u32[]{:S(2)}, u32[]{:S(2)}) %collective-permute-start.10) | collective-permute-done | bytes 573472 | tf_op jit(solution)/shard_map/ppermute | solution.py:25
  140.9 2.0 add_convert_fusion.5
  142.9 1.5 collective-permute-start.18
  144.4 10.0 %collective-permute-done.8 = bf16[2,160,1792]{2,1,0:T(8,128)(2,1)} collective-permute-done((bf16[2,160,1792]{2,1,0:T(8,128)(2,1)}, bf16[2,160,1792]{2,1,0:T(8,128)(2,1)}, u32[]{:S(2)}, u32[]{:S(2)}) %collective-permute-start.8) | collective-permute-done | bytes 1146912 | tf_op jit(solution)/shard_map/ppermute | solution.py:25
  154.4 2.5 add_convert_fusion.2
  156.9 4.7 %lefts.1 = (bf16[320,512]{1,0:T(8,128)(2,1)}, bf16[320,512]{1,0:T(8,128)(2,1)}, bf16[320,512]{1,0:T(8,128)(2,1)}) custom-call(bf16[5,128,1280]{2,1,0:T(8,128)(2,1)} %copy-done, bf16[5,128,1280]{2,1,0:T(8,128)(2,1)} %collective-permute-done.15.other_ref, bf16[320,1280]{1,0:T(8,128)(2,1)} %fusion.4.order_a_ref, bf16[320,1280]{1,0:T(8,128)(2,1)} %fusion.5.order_b_ref), custom_call_target="tpu_custom_call" | custom-call | flops 1 | bytes 1 | tf_op jit(solution)/shard_map/lefts/pallas_call | solution.py:624
  162.1 2.7 add_convert_fusion.1
  166.0 17.7 %backward.1 = (bf16[256,1280]{1,0:T(8,128)(2,1)}, bf16[288,1280]{1,0:T(8,128)(2,1)}, f32[128,1280]{1,0:T(8,128)}) custom-call(bf16[128,1280]{1,0:T(8,128)(2,1)} %x_ref.3, bf16[128,1280]{1,0:T(8,128)(2,1)} %dy_ref.3, f32[128,1280]{1,0:T(8,128)} %get-tuple-element.86.residual_ref, bf16[128,1280]{1,0:T(8,128)(2,1)} %get-tuple-element.93.ns_ref, ...), custom_call_target="tpu_custom_call" | custom-call | flops 1677721600 | bytes 13107200 | tf_op jit(solution)/shard_map/backward/pallas_call | solution.py:587
  184.8 1.6 collective-permute-start.11
  187.8 1.5 collective-permute-start.16
  189.3 5.3 %all-to-all-start.3 = ((bf16[4,128,1280]{2,1,0:T(8,128)(2,1)}), bf16[4,128,1280]{2,1,0:T(8,128)(2,1)S(1)}, u32[]{:S(2)}, u32[]{:S(2)}) async-start(bf16[4,128,1280]{2,1,0:T(8,128)(2,1)} %add_convert_fusion.1), calls=%async_computation.3 | async-start | bytes 2621440 | tf_op jit(solution)/shard_map/all_to_all | solution.py:35
  195.2 20.2 %routed_grads.2 = (bf16[6720,128]{1,0:T(8,128)(2,1)}, bf16[6720,128]{1,0:T(8,128)(2,1)}) custom-call(s32[2]{0:T(128)} %dynamic_slice.3.ids, f32[2,512,128]{2,1,0:T(8,128)} %get-tuple-element.108.row_gate_ref, bf16[4,128,1280]{2,1,0:T(8,128)(2,1)} %collective-permute-done.18.ns0_ref, bf16[4,128,1280]{2,1,0:T(8,128)(2,1)} %collective-permute-done.19.ns1_ref, ...), custom_call_target="tpu_custom_call" | custom-call | flops 9395240960 | bytes 24248320 | tf_op jit(solution)/shard_map/routed_grads/pallas_call | solution.py:362
  220.1 5.7 %all-to-all-done.3 = bf16[4,128,1280]{2,1,0:T(8,128)(2,1)S(1)} async-done(((bf16[4,128,1280]{2,1,0:T(8,128)(2,1)}), bf16[4,128,1280]{2,1,0:T(8,128)(2,1)S(1)}, u32[]{:S(2)}, u32[]{:S(2)}) %all-to-all-start.3) | async-done | bytes 1310752 | tf_op jit(solution)/shard_map/all_to_all | solution.py:35
  225.7 4.4 %all-to-all-start.4 = ((bf16[4,40,3072]{2,1,0:T(8,128)(2,1)}), bf16[4,40,3072]{2,1,0:T(8,128)(2,1)}, u32[]{:S(2)}, u32[]{:S(2)}) async-start(bf16[4,40,3072]{2,1,0:T(8,128)(2,1)} %fusion.10), calls=%async_computation.4 | async-start | bytes 1966080 | tf_op jit(solution)/shard_map/all_to_all | solution.py:35
  230.2 8.4 %last_grads.1 = (bf16[160,2560]{1,0:T(8,128)(2,1)}, bf16[160,2560]{1,0:T(8,128)(2,1)}, bf16[160,2688]{1,0:T(8,128)(2,1)}, bf16[160,2688]{1,0:T(8,128)(2,1)}) custom-call(s32[1]{0:T(128)} %bitcast.9.z_ref, bf16[256,1280]{1,0:T(8,128)(2,1)} %get-tuple-element.133.mine_ref, bf16[256,1280]{1,0:T(8,128)(2,1)} %collective-permute-done.21.other_ref, ...), custom_call_target="tpu_custom_call" | custom-call | flops 1 | bytes 1 | tf_op jit(solution)/shard_map/last_grads/pallas_call | solution.py:624
  239.6 20.3 %routed_grads.3 = (bf16[6720,128]{1,0:T(8,128)(2,1)}, bf16[6720,128]{1,0:T(8,128)(2,1)}) custom-call(s32[2]{0:T(128)} %dynamic_slice.3.ids, f32[2,512,128]{2,1,0:T(8,128)} %get-tuple-element.108.row_gate_ref, bf16[4,128,1280]{2,1,0:T(8,128)(2,1)} %collective-permute-done.20.ns_y_ref.ns0_ref, bf16[4,128,1280]{2,1,0:T(8,128)(2,1)} %collective-permute-done.25.ns_yo_ref.ns1_ref, ...), custom_call_target="tpu_custom_call" | custom-call | flops 9395240960 | bytes 24248320 | tf_op jit(solution)/shard_map/routed_grads/pallas_call | solution.py:362
  260.0 1.5 add_convert_fusion.4
  261.7 1.4 pad_maximum_fusion
  263.1 5.0 %all-to-all-start.5 = ((bf16[4,40,5248]{2,1,0:T(8,128)(2,1)}), bf16[4,40,5248]{2,1,0:T(8,128)(2,1)S(1)}, u32[]{:S(2)}, u32[]{:S(2)}) async-start(bf16[4,40,5248]{2,1,0:T(8,128)(2,1)} %bitcast.11), calls=%async_computation.5 | async-start | bytes 3358720 | tf_op jit(solution)/shard_map/all_to_all | solution.py:35
  268.1 1.5 collective-permute-start.29
  269.6 1.5 collective-permute-start.28
  271.1 34.7 %collective-permute-done.29.refs_3_ = bf16[6720,128]{1,0:T(8,128)(2,1)} collective-permute-done((bf16[6720,128]{1,0:T(8,128)(2,1)}, bf16[6720,128]{1,0:T(8,128)(2,1)}, u32[]{:S(2)}, u32[]{:S(2)}) %collective-permute-start.29) | collective-permute-done | bytes 1720352 | tf_op jit(solution)/shard_map/ppermute | solution.py:25
  307.0 6.2 %finish.1 = (f32[2,320,896]{2,1,0:T(8,128)}, f32[2,320,896]{2,1,0:T(8,128)}, f32[2,224,1280]{2,1,0:T(8,128)}) custom-call(bf16[6720,128]{1,0:T(8,128)(2,1)} %get-tuple-element.132.refs_0_, bf16[6720,128]{1,0:T(8,128)(2,1)} %collective-permute-done.28.refs_1_, bf16[6720,128]{1,0:T(8,128)(2,1)} %get-tuple-element.144.refs_2_, ...), custom_call_target="tpu_custom_call" | custom-call | tf_op jit(solution)/shard_map/finish/pallas_call | solution.py:407
  313.2 1.4 add_bitcast_fusion.1
  (152 shorter events, 32.2 us)
Async XLA Ops:
  3.5 41.2 %all-to-all-start = ((bf16[4,144,1280]{2,1,0:T(8,128)(2,1)}), bf16[4,144,1280]{2,1,0:T(8,128)(2,1)S(1)}, u32[]{:S(2)}, u32[]{:S(2)}) async-start(bf16[4,144,1280]{2,1,0:T(8,128)(2,1)} %broadcast_in_dim.8), calls=%async_computation | async-start | bytes 2949120 | tf_op jit(solution)/shard_map/all_to_all | solution.py:35
  9.9 15.9 %copy-start.27 = (s32[320]{0:T(512)S(1)}, s32[320]{0:T(512)}, u32[]{:S(2)}) copy-start(s32[320]{0:T(512)} %constant.97.clone) | copy-start | bytes 3844
  9.9 15.9 %copy-start.28 = (s32[320]{0:T(512)S(1)}, s32[320]{0:T(512)}, u32[]{:S(2)}) copy-start(s32[320]{0:T(512)} %constant.96.clone) | copy-start | bytes 3844
  9.9 15.9 %copy-start.29 = (s32[320]{0:T(512)S(1)}, s32[320]{0:T(512)}, u32[]{:S(2)}) copy-start(s32[320]{0:T(512)} %constant.95.clone) | copy-start | bytes 3844
  9.9 15.9 %copy-start.30 = (s32[320]{0:T(512)S(1)}, s32[320]{0:T(512)}, u32[]{:S(2)}) copy-start(s32[320]{0:T(512)} %constant.94.clone) | copy-start | bytes 3844
  21.4 20.4 %collective-permute-start.1 = (bf16[128,1280]{1,0:T(8,128)(2,1)}, bf16[128,1280]{1,0:T(8,128)(2,1)S(1)}, u32[]{:S(2)}, u32[]{:S(2)}) collective-permute-start(bf16[128,1280]{1,0:T(8,128)(2,1)} %get-tuple-element.91), channel_id=1, source_target_pairs={{0,8},{8,0},{16,24},{24,16},{1,9},{9,1},{17,25},{25,17},{2,10},{10... | collective-permute-start | bytes 983048 | tf_op jit(solution)/shard_map/ppermute | solution.py:25
  24.1 17.8 %collective-permute-start.2 = (bf16[2,128,1280]{2,1,0:T(8,128)(2,1)S(1)}, bf16[2,128,1280]{2,1,0:T(8,128)(2,1)S(1)}, u32[]{:S(2)}, u32[]{:S(2)}) collective-permute-start(bf16[2,128,1280]{2,1,0:T(8,128)(2,1)S(1)} %pad_maximum_fusion.2), channel_id=1, source_target_pairs={{0,16},{8,24},{16,0},{24,8},{1,17},{9,25},{17,1},{25,9},{2,18},{10... | collective-permute-start | bytes 1966088 | tf_op jit(solution)/shard_map/ppermute | solution.py:25
  46.0 7.8 %copy-start.32 = (s32[16]{0:T(128)S(1)}, s32[16]{0:T(128)}, u32[]{:S(2)}) copy-start(s32[16]{0:T(128)} %param.38) | copy-start | bytes 196
  46.0 40.8 %all-to-all-start.1 = ((bf16[4,128,1280]{2,1,0:T(8,128)(2,1)}), bf16[4,128,1280]{2,1,0:T(8,128)(2,1)}, u32[]{:S(2)}, u32[]{:S(2)}) async-start(bf16[4,128,1280]{2,1,0:T(8,128)(2,1)} %broadcast_in_dim.9), calls=%async_computation.1 | async-start | bytes 2621440 | tf_op jit(solution)/shard_map/all_to_all | solution.py:35
  50.6 13.6 %collective-permute-start.3 = (bf16[4,144,1280]{2,1,0:T(8,128)(2,1)S(1)}, bf16[4,144,1280]{2,1,0:T(8,128)(2,1)}, u32[]{:S(2)}, u32[]{:S(2)}) collective-permute-start(bf16[4,144,1280]{2,1,0:T(8,128)(2,1)S(1)} %all-to-all-done.early_ref), channel_id=1, source_target_pairs={{0,1},{1,0},{2,3},{3,2},{4,5},{5,4},{6,7},{7,6},{8,9},{9,8},{10,11... | collective-permute-start | bytes 4423688 | tf_op jit(solution)/shard_map/ppermute | solution.py:25
  50.7 34.8 %collective-permute-start.5 = (bf16[4,144,1280]{2,1,0:T(8,128)(2,1)S(1)}, bf16[4,144,1280]{2,1,0:T(8,128)(2,1)}, u32[]{:S(2)}, u32[]{:S(2)}) collective-permute-start(bf16[4,144,1280]{2,1,0:T(8,128)(2,1)S(1)} %all-to-all-done.early_ref), channel_id=1, source_target_pairs={{0,16},{8,24},{16,0},{24,8},{1,17},{9,25},{17,1},{25,9},{2,18},{10... | collective-permute-start | bytes 4423688 | tf_op jit(solution)/shard_map/ppermute | solution.py:25
  52.3 34.5 %collective-permute-start.4 = (bf16[4,144,1280]{2,1,0:T(8,128)(2,1)S(1)}, bf16[4,144,1280]{2,1,0:T(8,128)(2,1)}, u32[]{:S(2)}, u32[]{:S(2)}) collective-permute-start(bf16[4,144,1280]{2,1,0:T(8,128)(2,1)S(1)} %all-to-all-done.early_ref), channel_id=1, source_target_pairs={{0,8},{8,0},{16,24},{24,16},{1,9},{9,1},{17,25},{25,17},{2,10},{10... | collective-permute-start | bytes 4423688 | tf_op jit(solution)/shard_map/ppermute | solution.py:25
  53.8 3.3 %collective-permute-start = (bf16[128,5248]{1,0:T(8,128)(2,1)}, bf16[128,5248]{1,0:T(8,128)(2,1)S(1)}, u32[]{:S(2)}, u32[]{:S(2)}) collective-permute-start(bf16[128,5248]{1,0:T(8,128)(2,1)} %get-tuple-element.89.cat_ref), channel_id=1, source_target_pairs={{0,1},{1,0},{2,3},{3,2},{4,5},{5,4},{6,7},{7,6},{8,9},{9,8},{10,11... | collective-permute-start | bytes 4030472 | tf_op jit(solution)/shard_map/ppermute | solution.py:25
  64.2 22.6 %copy-start.20 = (bf16[1280,15]{0,1:T(8,128)(2,1)S(1)}, bf16[1280,15]{0,1:T(8,128)(2,1)}, u32[]{:S(2)}) copy-start(bf16[1280,15]{0,1:T(8,128)(2,1)} %param.45) | copy-start | bytes 115204
  86.7 3.2 %collective-permute-start.6 = (bf16[4,128,1280]{2,1,0:T(8,128)(2,1)}, bf16[4,128,1280]{2,1,0:T(8,128)(2,1)S(1)}, u32[]{:S(2)}, u32[]{:S(2)}) collective-permute-start(bf16[4,128,1280]{2,1,0:T(8,128)(2,1)} %all-to-all-done.1.ns0_ref), channel_id=1, source_target_pairs={{0,1},{1,0},{2,3},{3,2},{4,5},{5,4},{6,7},{7,6},{8,9},{9,8},{10,11... | collective-permute-start | bytes 3932168 | tf_op jit(solution)/shard_map/ppermute | solution.py:25
  113.2 3.5 %collective-permute-start.7 = (bf16[4,144,1280]{2,1,0:T(8,128)(2,1)}, bf16[4,144,1280]{2,1,0:T(8,128)(2,1)S(1)}, u32[]{:S(2)}, u32[]{:S(2)}) collective-permute-start(bf16[4,144,1280]{2,1,0:T(8,128)(2,1)} %get-tuple-element.100), channel_id=1, source_target_pairs={{0,1},{1,0},{2,3},{3,2},{4,5},{5,4},{6,7},{7,6},{8,9},{9,8},{10,11... | collective-permute-start | bytes 4423688 | tf_op jit(solution)/shard_map/ppermute | solution.py:25
  119.7 8.1 %collective-permute-start.12 = (bf16[4,144,1280]{2,1,0:T(8,128)(2,1)}, bf16[4,144,1280]{2,1,0:T(8,128)(2,1)}, u32[]{:S(2)}, u32[]{:S(2)}) collective-permute-start(bf16[4,144,1280]{2,1,0:T(8,128)(2,1)} %collective-permute-done.4.early0_ref), channel_id=1, source_target_pairs={{0,1},{1,0},{2,3},{3,2},{4,5},{5,4},{6,7},{7,6},{8,9},{9,8},{10,11... | collective-permute-start | bytes 4423688 | tf_op jit(solution)/shard_map/ppermute | solution.py:25
  119.8 8.0 %collective-permute-start.13 = (bf16[4,144,1280]{2,1,0:T(8,128)(2,1)}, bf16[4,144,1280]{2,1,0:T(8,128)(2,1)}, u32[]{:S(2)}, u32[]{:S(2)}) collective-permute-start(bf16[4,144,1280]{2,1,0:T(8,128)(2,1)} %collective-permute-done.5.early0_ref), channel_id=1, source_target_pairs={{0,1},{1,0},{2,3},{3,2},{4,5},{5,4},{6,7},{7,6},{8,9},{9,8},{10,11... | collective-permute-start | bytes 4423688 | tf_op jit(solution)/shard_map/ppermute | solution.py:25
  120.4 15.0 %copy-start = (bf16[5,128,1280]{2,1,0:T(8,128)(2,1)}, bf16[5,128,1280]{2,1,0:T(8,128)(2,1)S(1)}, u32[]{:S(2)}) copy-start(bf16[5,128,1280]{2,1,0:T(8,128)(2,1)S(1)} %pad_maximum_fusion.1.mine_ref) | copy-start | bytes 4915204
  120.4 44.4 %all-to-all-start.2 = ((bf16[4,144,1280]{2,1,0:T(8,128)(2,1)}), bf16[4,144,1280]{2,1,0:T(8,128)(2,1)S(1)}, u32[]{:S(2)}, u32[]{:S(2)}) async-start(bf16[4,144,1280]{2,1,0:T(8,128)(2,1)} %add_convert_fusion), calls=%async_computation.2 | async-start | bytes 2949120 | tf_op jit(solution)/shard_map/all_to_all | solution.py:35
  125.8 15.1 %collective-permute-start.10 = (bf16[2,112,1280]{2,1,0:T(8,128)(2,1)}, bf16[2,112,1280]{2,1,0:T(8,128)(2,1)}, u32[]{:S(2)}, u32[]{:S(2)}) collective-permute-start(bf16[2,112,1280]{2,1,0:T(8,128)(2,1)} %get-tuple-element.103), channel_id=1, source_target_pairs={{0,8},{8,0},{16,24},{24,16},{1,9},{9,1},{17,25},{25,17},{2,10},{10... | collective-permute-start | bytes 1720328 | tf_op jit(solution)/shard_map/ppermute | solution.py:25
  127.3 27.1 %collective-permute-start.8 = (bf16[2,160,1792]{2,1,0:T(8,128)(2,1)}, bf16[2,160,1792]{2,1,0:T(8,128)(2,1)}, u32[]{:S(2)}, u32[]{:S(2)}) collective-permute-start(bf16[2,160,1792]{2,1,0:T(8,128)(2,1)} %get-tuple-element.101), channel_id=1, source_target_pairs={{0,16},{8,24},{16,0},{24,8},{1,17},{9,25},{17,1},{25,9},{2,18},{10... | collective-permute-start | bytes 3440648 | tf_op jit(solution)/shard_map/ppermute | solution.py:25
  127.8 29.1 %collective-permute-start.15 = (bf16[5,128,1280]{2,1,0:T(8,128)(2,1)S(1)}, bf16[5,128,1280]{2,1,0:T(8,128)(2,1)}, u32[]{:S(2)}, u32[]{:S(2)}) collective-permute-start(bf16[5,128,1280]{2,1,0:T(8,128)(2,1)S(1)} %pad_maximum_fusion.1.mine_ref), channel_id=1, source_target_pairs={{0,1},{1,0},{2,3},{3,2},{4,5},{5,4},{6,7},{7,6},{8,9},{9,8},{10,11... | collective-permute-start | bytes 4915208 | tf_op jit(solution)/shard_map/ppermute | solution.py:25
  127.8 13.0 %copy-start.17 = (bf16[2,112,1280]{2,1,0:T(8,128)(2,1)S(1)}, bf16[2,112,1280]{2,1,0:T(8,128)(2,1)}, u32[]{:S(2)}) copy-start(bf16[2,112,1280]{2,1,0:T(8,128)(2,1)} %get-tuple-element.102) | copy-start | bytes 1720324
  135.4 19.0 %copy-start.11 = (bf16[2,160,1792]{2,1,0:T(8,128)(2,1)S(1)}, bf16[2,160,1792]{2,1,0:T(8,128)(2,1)}, u32[]{:S(2)}) copy-start(bf16[2,160,1792]{2,1,0:T(8,128)(2,1)} %get-tuple-element.90) | copy-start | bytes 3440644
  135.4 26.7 %collective-permute-start.14 = (bf16[4,128,1280]{2,1,0:T(8,128)(2,1)}, bf16[4,128,1280]{2,1,0:T(8,128)(2,1)}, u32[]{:S(2)}, u32[]{:S(2)}) collective-permute-start(bf16[4,128,1280]{2,1,0:T(8,128)(2,1)} %get-tuple-element.110), channel_id=1, source_target_pairs={{0,1},{1,0},{2,3},{3,2},{4,5},{5,4},{6,7},{7,6},{8,9},{9,8},{10,11... | collective-permute-start | bytes 3932168 | tf_op jit(solution)/shard_map/ppermute | solution.py:25
  142.9 40.9 %collective-permute-start.18 = (bf16[4,128,1280]{2,1,0:T(8,128)(2,1)}, bf16[4,128,1280]{2,1,0:T(8,128)(2,1)}, u32[]{:S(2)}, u32[]{:S(2)}) collective-permute-start(bf16[4,128,1280]{2,1,0:T(8,128)(2,1)} %all-to-all-done.1.ns0_ref), channel_id=1, source_target_pairs={{0,8},{8,0},{16,24},{24,16},{1,9},{9,1},{17,25},{25,17},{2,10},{10... | collective-permute-start | bytes 3932168 | tf_op jit(solution)/shard_map/ppermute | solution.py:25
  161.6 33.0 %collective-permute-start.20 = (bf16[4,128,1280]{2,1,0:T(8,128)(2,1)}, bf16[4,128,1280]{2,1,0:T(8,128)(2,1)}, u32[]{:S(2)}, u32[]{:S(2)}) collective-permute-start(bf16[4,128,1280]{2,1,0:T(8,128)(2,1)} %all-to-all-done.1.ns0_ref), channel_id=1, source_target_pairs={{0,16},{8,24},{16,0},{24,8},{1,17},{9,25},{17,1},{25,9},{2,18},{10... | collective-permute-start | bytes 3932168 | tf_op jit(solution)/shard_map/ppermute | solution.py:25
  166.0 20.4 %copy-start.5 = (bf16[2,160,1792]{2,1,0:T(8,128)(2,1)S(1)}, bf16[2,160,1792]{2,1,0:T(8,128)(2,1)}, u32[]{:S(2)}) copy-start(bf16[2,160,1792]{2,1,0:T(8,128)(2,1)} %add_convert_fusion.2) | copy-start | bytes 3440644
  183.7 11.4 %collective-permute-start.19 = (bf16[4,128,1280]{2,1,0:T(8,128)(2,1)}, bf16[4,128,1280]{2,1,0:T(8,128)(2,1)}, u32[]{:S(2)}, u32[]{:S(2)}) collective-permute-start(bf16[4,128,1280]{2,1,0:T(8,128)(2,1)} %collective-permute-done.18.ns0_ref), channel_id=1, source_target_pairs={{0,1},{1,0},{2,3},{3,2},{4,5},{5,4},{6,7},{7,6},{8,9},{9,8},{10,11... | collective-permute-start | bytes 3932168 | tf_op jit(solution)/shard_map/ppermute | solution.py:25
  184.8 30.6 %collective-permute-start.11 = (bf16[112,1280]{1,0:T(8,128)(2,1)S(1)}, bf16[112,1280]{1,0:T(8,128)(2,1)}, u32[]{:S(2)}, u32[]{:S(2)}) collective-permute-start(bf16[112,1280]{1,0:T(8,128)(2,1)S(1)} %slice_bitcast_fusion.2), channel_id=1, source_target_pairs={{0,16},{8,24},{16,0},{24,8},{1,17},{9,25},{17,1},{25,9},{2,18},{10... | collective-permute-start | bytes 860168 | tf_op jit(solution)/shard_map/ppermute | solution.py:25
  187.3 29.3 %collective-permute-start.9 = (bf16[160,1792]{1,0:T(8,128)(2,1)}, bf16[160,1792]{1,0:T(8,128)(2,1)}, u32[]{:S(2)}, u32[]{:S(2)}) collective-permute-start(bf16[160,1792]{1,0:T(8,128)(2,1)} %slice_bitcast_fusion), channel_id=1, source_target_pairs={{0,8},{8,0},{16,24},{24,16},{1,9},{9,1},{17,25},{25,17},{2,10},{10... | collective-permute-start | bytes 1720328 | tf_op jit(solution)/shard_map/ppermute | solution.py:25
  187.8 28.9 %collective-permute-start.16 = (bf16[256,1280]{1,0:T(8,128)(2,1)}, bf16[256,1280]{1,0:T(8,128)(2,1)}, u32[]{:S(2)}, u32[]{:S(2)}) collective-permute-start(bf16[256,1280]{1,0:T(8,128)(2,1)} %get-tuple-element.133.mine_ref), channel_id=1, source_target_pairs={{0,8},{8,0},{16,24},{24,16},{1,9},{9,1},{17,25},{25,17},{2,10},{10... | collective-permute-start | bytes 1966088 | tf_op jit(solution)/shard_map/ppermute | solution.py:25
  189.3 36.4 %all-to-all-start.3 = ((bf16[4,128,1280]{2,1,0:T(8,128)(2,1)}), bf16[4,128,1280]{2,1,0:T(8,128)(2,1)S(1)}, u32[]{:S(2)}, u32[]{:S(2)}) async-start(bf16[4,128,1280]{2,1,0:T(8,128)(2,1)} %add_convert_fusion.1), calls=%async_computation.3 | async-start | bytes 2621440 | tf_op jit(solution)/shard_map/all_to_all | solution.py:35
  194.6 22.1 %collective-permute-start.17 = (bf16[288,1280]{1,0:T(8,128)(2,1)}, bf16[288,1280]{1,0:T(8,128)(2,1)}, u32[]{:S(2)}, u32[]{:S(2)}) collective-permute-start(bf16[288,1280]{1,0:T(8,128)(2,1)} %get-tuple-element.134.rest_ref), channel_id=1, source_target_pairs={{0,16},{8,24},{16,0},{24,8},{1,17},{9,25},{17,1},{25,9},{2,18},{10... | collective-permute-start | bytes 2211848 | tf_op jit(solution)/shard_map/ppermute | solution.py:25
  195.2 20.3 %copy-start.7 = (bf16[2,112,1280]{2,1,0:T(8,128)(2,1)S(1)}, bf16[2,112,1280]{2,1,0:T(8,128)(2,1)}, u32[]{:S(2)}) copy-start(bf16[2,112,1280]{2,1,0:T(8,128)(2,1)} %add_convert_fusion.5) | copy-start | bytes 1720324
  215.4 14.8 %collective-permute-start.25 = (bf16[4,128,1280]{2,1,0:T(8,128)(2,1)}, bf16[4,128,1280]{2,1,0:T(8,128)(2,1)}, u32[]{:S(2)}, u32[]{:S(2)}) collective-permute-start(bf16[4,128,1280]{2,1,0:T(8,128)(2,1)} %collective-permute-done.20.ns_y_ref.ns0_ref), channel_id=1, source_target_pairs={{0,1},{1,0},{2,3},{3,2},{4,5},{5,4},{6,7},{7,6},{8,9},{9,8},{10,11... | collective-permute-start | bytes 3932168 | tf_op jit(solution)/shard_map/ppermute | solution.py:25
  216.7 13.4 %collective-permute-start.21 = (bf16[256,1280]{1,0:T(8,128)(2,1)}, bf16[256,1280]{1,0:T(8,128)(2,1)}, u32[]{:S(2)}, u32[]{:S(2)}) collective-permute-start(bf16[256,1280]{1,0:T(8,128)(2,1)} %get-tuple-element.133.mine_ref), channel_id=1, source_target_pairs={{0,1},{1,0},{2,3},{3,2},{4,5},{5,4},{6,7},{7,6},{8,9},{9,8},{10,11... | collective-permute-start | bytes 1966088 | tf_op jit(solution)/shard_map/ppermute | solution.py:25
  217.1 13.0 %collective-permute-start.23 = (bf16[256,1280]{1,0:T(8,128)(2,1)}, bf16[256,1280]{1,0:T(8,128)(2,1)}, u32[]{:S(2)}, u32[]{:S(2)}) collective-permute-start(bf16[256,1280]{1,0:T(8,128)(2,1)} %collective-permute-done.16.qx_ref), channel_id=1, source_target_pairs={{0,1},{1,0},{2,3},{3,2},{4,5},{5,4},{6,7},{7,6},{8,9},{9,8},{10,11... | collective-permute-start | bytes 1966088 | tf_op jit(solution)/shard_map/ppermute | solution.py:25
  217.3 12.9 %collective-permute-start.22 = (bf16[288,1280]{1,0:T(8,128)(2,1)}, bf16[288,1280]{1,0:T(8,128)(2,1)}, u32[]{:S(2)}, u32[]{:S(2)}) collective-permute-start(bf16[288,1280]{1,0:T(8,128)(2,1)} %get-tuple-element.134.rest_ref), channel_id=1, source_target_pairs={{0,1},{1,0},{2,3},{3,2},{4,5},{5,4},{6,7},{7,6},{8,9},{9,8},{10,11... | collective-permute-start | bytes 2211848 | tf_op jit(solution)/shard_map/ppermute | solution.py:25
  217.6 12.5 %collective-permute-start.24 = (bf16[288,1280]{1,0:T(8,128)(2,1)}, bf16[288,1280]{1,0:T(8,128)(2,1)}, u32[]{:S(2)}, u32[]{:S(2)}) collective-permute-start(bf16[288,1280]{1,0:T(8,128)(2,1)} %collective-permute-done.17.by_ref), channel_id=1, source_target_pairs={{0,1},{1,0},{2,3},{3,2},{4,5},{5,4},{6,7},{7,6},{8,9},{9,8},{10,11... | collective-permute-start | bytes 2211848 | tf_op jit(solution)/shard_map/ppermute | solution.py:25
  225.7 37.3 %all-to-all-start.4 = ((bf16[4,40,3072]{2,1,0:T(8,128)(2,1)}), bf16[4,40,3072]{2,1,0:T(8,128)(2,1)}, u32[]{:S(2)}, u32[]{:S(2)}) async-start(bf16[4,40,3072]{2,1,0:T(8,128)(2,1)} %fusion.10), calls=%async_computation.4 | async-start | bytes 1966080 | tf_op jit(solution)/shard_map/all_to_all | solution.py:35
  238.6 21.4 %collective-permute-start.26 = (bf16[160,2560]{1,0:T(8,128)(2,1)}, bf16[160,2560]{1,0:T(8,128)(2,1)}, u32[]{:S(2)}, u32[]{:S(2)}) collective-permute-start(bf16[160,2560]{1,0:T(8,128)(2,1)} %get-tuple-element.141), channel_id=1, source_target_pairs={{0,16},{8,24},{16,0},{24,8},{1,17},{9,25},{17,1},{25,9},{2,18},{10... | collective-permute-start | bytes 2457608 | tf_op jit(solution)/shard_map/ppermute | solution.py:25
  239.1 20.9 %copy-start.13 = (bf16[160,2560]{1,0:T(8,128)(2,1)S(1)}, bf16[160,2560]{1,0:T(8,128)(2,1)}, u32[]{:S(2)}) copy-start(bf16[160,2560]{1,0:T(8,128)(2,1)} %get-tuple-element.140) | copy-start | bytes 2457604
  239.1 22.3 %collective-permute-start.27 = (bf16[160,2688]{1,0:T(8,128)(2,1)}, bf16[160,2688]{1,0:T(8,128)(2,1)S(1)}, u32[]{:S(2)}, u32[]{:S(2)}) collective-permute-start(bf16[160,2688]{1,0:T(8,128)(2,1)} %get-tuple-element.147), channel_id=1, source_target_pairs={{0,8},{8,0},{16,24},{24,16},{1,9},{9,1},{17,25},{25,17},{2,10},{10... | collective-permute-start | bytes 2580488 | tf_op jit(solution)/shard_map/ppermute | solution.py:25
  263.1 50.2 %all-to-all-start.5 = ((bf16[4,40,5248]{2,1,0:T(8,128)(2,1)}), bf16[4,40,5248]{2,1,0:T(8,128)(2,1)S(1)}, u32[]{:S(2)}, u32[]{:S(2)}) async-start(bf16[4,40,5248]{2,1,0:T(8,128)(2,1)} %bitcast.11), calls=%async_computation.5 | async-start | bytes 3358720 | tf_op jit(solution)/shard_map/all_to_all | solution.py:35
  268.1 37.7 %collective-permute-start.29 = (bf16[6720,128]{1,0:T(8,128)(2,1)}, bf16[6720,128]{1,0:T(8,128)(2,1)}, u32[]{:S(2)}, u32[]{:S(2)}) collective-permute-start(bf16[6720,128]{1,0:T(8,128)(2,1)} %get-tuple-element.153), channel_id=1, source_target_pairs={{0,8},{8,0},{16,24},{24,16},{1,9},{9,1},{17,25},{25,17},{2,10},{10... | collective-permute-start | bytes 5160968 | tf_op jit(solution)/shard_map/ppermute | solution.py:25
  269.6 37.4 %collective-permute-start.28 = (bf16[6720,128]{1,0:T(8,128)(2,1)}, bf16[6720,128]{1,0:T(8,128)(2,1)}, u32[]{:S(2)}, u32[]{:S(2)}) collective-permute-start(bf16[6720,128]{1,0:T(8,128)(2,1)} %get-tuple-element.152), channel_id=1, source_target_pairs={{0,16},{8,24},{16,0},{24,8},{1,17},{9,25},{17,1},{25,9},{2,18},{10... | collective-permute-start | bytes 5160968 | tf_op jit(solution)/shard_map/ppermute | solution.py:25
  (21 other events, 83.3 us)

commit v4 on v3

--- a/solution.py
+++ b/solution.py
@@ -17,7 +17,7 @@
 BF = jnp.bfloat16
 F32 = jnp.float32
 VMEM_LIMIT = 60 * 2**20
-COST = 1
+COST = 4
 
 
 def partner(v, axis, mask):
@@ -386,13 +386,25 @@
     )(ids, row_gate, *far, router, *late)
 
 
-def finish_kernel(slots, *refs):
-    outs = refs[2 * slots :]
+def finish_kernel(slots, outs_count, *refs):
+    sources, outs = refs[: 2 * slots], refs[2 * slots : 2 * slots + outs_count]
+    bufs, sems = refs[2 * slots + outs_count : -1], refs[-1]
+    copies = [
+        pltpu.make_async_copy(ref, buf, sems.at[i]) for i, (ref, buf) in enumerate(zip(sources, bufs))
+    ]
+
+    @pl.when(pl.program_id(0) == 0)
+    def _():
+        for copy in copies:
+            copy.start()
+
     for s in range(slots):
-        keep, got = refs[2 * s], refs[2 * s + 1]
+        keep, got = bufs[2 * s], bufs[2 * s + 1]
 
         @pl.when(pl.program_id(0) == s)
         def _():
+            copies[2 * s].wait()
+            copies[2 * s + 1].wait()
             start = 0
             for out in outs:
                 size, columns = out.shape[1:]
@@ -404,15 +416,17 @@
 
 def finish(pieces, shapes):
     slots = len(pieces)
+    flat = [v for piece in pieces for v in piece]
     return pl.pallas_call(
-        functools.partial(finish_kernel, slots),
+        functools.partial(finish_kernel, slots, len(shapes)),
         grid=(slots,),
-        in_specs=[once(v.shape) for piece in pieces for v in piece],
+        in_specs=[pl.BlockSpec(memory_space=pl.ANY)] * len(flat),
         out_specs=[per_slot(*shape) for shape in shapes],
         out_shape=[jax.ShapeDtypeStruct((slots,) + shape, F32) for shape in shapes],
+        scratch_shapes=[pltpu.VMEM(v.shape, BF) for v in flat] + [pltpu.SemaphoreType.DMA((len(flat),))],
         compiler_params=pltpu.CompilerParams(vmem_limit_bytes=VMEM_LIMIT),
         name="finish",
-    )(*(v for piece in pieces for v in piece))
+    )(*flat)
 
 
 def rotary(length):
@@ -476,7 +490,7 @@
 
 def attention(x, gain1, gain2, cosine, sine, wq, wk, wv, wo):
     length, width = x.shape
-    step = 2 * HEAD_DIM
+    step = 5 * HEAD_DIM
     columns = lambda rows: pl.BlockSpec((rows, step), lambda i: (0, i))
     low = jax.ShapeDtypeStruct((length, width), BF)
     return pl.pallas_call(
@@ -581,7 +595,7 @@
     q, k, v, wq, wk, wv, wo, parts, expert_count,
 ):
     length, width = x.shape
-    step = 2 * HEAD_DIM
+    step = 5 * HEAD_DIM
     columns = lambda rows: pl.BlockSpec((rows, step), lambda i: (0, i))
     tall = whole((length, width))
     return pl.pallas_call(
@@ -673,8 +687,8 @@
 
 
 def last_grads_kernel(
-    length, at_ns, z_ref, mine_ref, other_ref, rest_ref, rest_other_ref, qx_ref, qxo_ref, by_ref, byo_ref, a_ref, v_ref, o_ref,
-    ns_ref, cat_other_ref, ns_y_ref, ns_yo_ref, order_b_ref,
+    length, z_ref, mine_ref, other_ref, rest_ref, rest_other_ref, qx_ref, qxo_ref, by_ref, byo_ref, a_ref, v_ref, o_ref,
+    ns_ref, ns_o_ref, ns_y_ref, ns_yo_ref, order_b_ref,
     a_send, a_keep, b_send, b_keep,
 ):
     width = mine_ref.shape[1]
@@ -697,7 +711,7 @@
     gains = sum(ref[i : i + 16].astype(F32) for ref, i in refs).astype(BF)
     logits = jnp.concatenate([ref[i + 16 :, :length] for ref, i in refs], 1)
     ns = join(
-        ns_ref[...], cat_other_ref[:, at_ns : at_ns + width], ns_y_ref[z_ref[0]], ns_yo_ref[z_ref[0]]
+        ns_ref[...], ns_o_ref[0], ns_y_ref[0], ns_yo_ref[0]
     )
     left_r = dot_nt(order_b_ref[...], ns).astype(BF)
     small = jnp.concatenate(
@@ -833,12 +847,23 @@
     far_y = [ns_y, over_core(after(ns_y, routed[0])), early_y, early_y_other]
     far.append(far_y)
     qk_x_other, b_y_other = over_core(qk_x), over_core(b_y)
-    a_send, a_keep, b_send, b_keep = call(
-        functools.partial(last_grads_kernel, length, 3 * ff), "last_grads",
-        [((w // 8, 2 * w), BF)] * 2 + [((w // 8, 2 * w + LANES), BF)] * 2,
-        my_z[None], d_qk, qk_other, d_rest, rest_other, qk_x, qk_x_other, b_y, b_y_other, left_a, left_v, left_o,
-        normed_second, from_other, far_y[0], far_y[1], order_b, scalars=1,
-    )
+    blocks = [d_qk, qk_other, d_rest, rest_other, qk_x, qk_x_other, b_y, b_y_other, left_a, left_v, left_o, normed_second]
+    out_a, out_b = (w // 8, 2 * w), (w // 8, 2 * w + LANES)
+    a_send, a_keep, b_send, b_keep = pl.pallas_call(
+        functools.partial(last_grads_kernel, length),
+        grid_spec=pltpu.PrefetchScalarGridSpec(
+            num_scalar_prefetch=1,
+            grid=(1,),
+            in_specs=[once(v.shape) for v in blocks]
+            + [pl.BlockSpec((1, length, w), lambda i, z: (z[0], 0, 0), pipeline_mode=pl.Buffered(1))] * 3
+            + [once(order_b.shape)],
+            out_specs=[once(shape) for shape in (out_a, out_a, out_b, out_b)],
+        ),
+        out_shape=[jax.ShapeDtypeStruct(shape, BF) for shape in (out_a, out_a, out_b, out_b)],
+        compiler_params=pltpu.CompilerParams(vmem_limit_bytes=VMEM_LIMIT),
+        cost_estimate=pl.CostEstimate(flops=1, bytes_accessed=1, transcendentals=0),
+        name="last_grads",
+    )(my_z[None], *blocks, ns_other, far_y[0], far_y[1], order_b)
     a_got, b_got = partner(a_send, "dp", 2), partner(b_send, "dp", 1)
 
     routed += [slot_grads(slot, after(dg, a_send)) for slot in range(1, slot_dev)]

time: 326 us -> 323 us (level)
  Pallas kernels: 143 us -> 139 us
    pallas_call x4 -> x3, Pallas kernels: 26.4 us -> 18.4 us  [call(): pl.pallas_call(kernel, in_specs=[pl.BlockSpec(memory_space=pltpu.SMEM)] *...]
    pallas_call x1 -> x2, Pallas kernels: 6.21 us -> 12.8 us  [the longest x1 7.63 us: shards(): pl.pallas_call(functools.partial(last_grads_kernel, length), grid_spec=pl...]
    unnamed x68 -> x72, local copies, waits for them, and re-layouts: 4.45 us -> 6.67 us
  transfers between devices with their start and end apart: 36 -> 36, of which waited for: 12 -> 12; matrix products, arithmetic and copies ran while one was open for 9% -> 8% of each run, Pallas kernels for 38% -> 37%
where the time goes in v4:
time: 323 us; the launch traced here: 317 us
  Pallas kernels  139 us (43%)
  waiting for transfers between devices  80.5 us (25%)
  starting transfers between devices  51.4 us (16%)
  other arithmetic  29 us (9%)
  local copies, waits for them, and re-layouts  15.1 us (5%)
    ppermute x30, waiting for transfers between devices, partner(): return lax.ppermute(v, axis, [(i, i ^ mask) for i in range(n)])  71.7 us
    pallas_call x2, Pallas kernels, routed_grads(): pl.pallas_call(functools.partial(routed_grads_kernel, expert_count, slot)...  40.4 us
    all_to_all x6, starting transfers between devices, exchange_z(): lax.all_to_all(s, 'expert', 0, 0, tiled=True, axis_index_groups=groups)  30.3 us
    pallas_call x1, Pallas kernels, experts(): pl.pallas_call(functools.partial(experts_kernel, expert_count), grid_spec...  22.2 us
    ppermute x30, starting transfers between devices, partner(): return lax.ppermute(v, axis, [(i, i ^ mask) for i in range(n)])  21.1 us
    pallas_call x3, Pallas kernels, call(): pl.pallas_call(kernel, in_specs=[pl.BlockSpec(memory_space=pltpu.SMEM)] *...  18.4 us
    pallas_call x1, Pallas kernels, backward(): pl.pallas_call(functools.partial(backward_kernel, expert_count), grid=(wi...  17 us
    convert_element_type x8, other arithmetic, plus(): return (a.astype(F32) + b.astype(F32)).astype(BF)  13 us
  transfers between devices with their start and end apart: 36, of which 12 were waited for; matrix products, arithmetic and copies ran while one was open for 8% of the time, Pallas kernels for 37%

profile of v4, /device:TPU:0, one launch (start us, length us, event | category | flops | bytes accessed | tf_op | source)
XLA Modules:
  0.0 316.8 jit_solution(142473278009441130)
XLA Ops:
  3.5 6.3 %all-to-all-start = ((bf16[4,144,1280]{2,1,0:T(8,128)(2,1)}), bf16[4,144,1280]{2,1,0:T(8,128)(2,1)S(1)}, u32[]{:S(2)}, u32[]{:S(2)}) async-start(bf16[4,144,1280]{2,1,0:T(8,128)(2,1)} %broadcast_in_dim.8), calls=%async_computation | async-start | bytes 2949120 | tf_op jit(solution)/shard_map/all_to_all | solution.py:35
  10.0 9.9 %attention.1 = (bf16[128,1280]{1,0:T(8,128)(2,1)}, bf16[128,1280]{1,0:T(8,128)(2,1)}, bf16[128,1280]{1,0:T(8,128)(2,1)}, bf16[128,1280]{1,0:T(8,128)(2,1)}, bf16...) custom-call(bf16[128,1280]{1,0:T(8,128)(2,1)} %x_ref.3, f32[1280]{0:T(1024)} %gain1_ref.3, ...), custom_call_target="tpu_custom_call" | custom-call | flops 6710886400 | bytes 52428800 | tf_op jit(solution)/shard_map/attention/pallas_call | solution.py:496
  19.9 1.5 collective-permute-start.1
  22.6 1.6 collective-permute-start.2
  24.4 1.5 fusion.order_d_ref
  25.9 1.5 fusion.4
  27.4 2.3 fusion.1
  29.7 7.3 %shared.1 = (bf16[128,5248]{1,0:T(8,128)(2,1)}, f32[128,1280]{1,0:T(8,128)}, f32[128,1280]{1,0:T(8,128)}) custom-call(bf16[128,1280]{1,0:T(8,128)(2,1)} %get-tuple-element.93.ns_ref, bf16[128,1280]{1,0:T(8,128)(2,1)} %dy_ref.3, bf16[1280,896]{1,0:T(8,128)(2,1)} %gate_ref.2, bf16[1280,896]{1,0:T(8,128)(2,1)} %up_ref.2, bf16[896,1280]{1,0:T(8,128)(2,1)} %down_ref.3), custom_call_target="tpu_custom_call" | custom-call | flops 1 | bytes 1 | tf_op jit(solution)/shard_map/shared/pallas_call | solution.py:638
  38.2 1.5 fusion.7
  39.7 5.1 %all-to-all-done.early_ref = bf16[4,144,1280]{2,1,0:T(8,128)(2,1)S(1)} async-done(((bf16[4,144,1280]{2,1,0:T(8,128)(2,1)}), bf16[4,144,1280]{2,1,0:T(8,128)(2,1)S(1)}, u32[]{:S(2)}, u32[]{:S(2)}) %all-to-all-start) | async-done | bytes 1474592 | tf_op jit(solution)/shard_map/all_to_all | solution.py:35
  46.0 4.9 %all-to-all-start.1 = ((bf16[4,128,1280]{2,1,0:T(8,128)(2,1)}), bf16[4,128,1280]{2,1,0:T(8,128)(2,1)}, u32[]{:S(2)}, u32[]{:S(2)}) async-start(bf16[4,128,1280]{2,1,0:T(8,128)(2,1)} %broadcast_in_dim.9), calls=%async_computation.1 | async-start | bytes 2621440 | tf_op jit(solution)/shard_map/all_to_all | solution.py:35
  51.1 1.6 collective-permute-start.5
  52.6 1.5 collective-permute-start.4
  54.7 2.8 collective-permute-done.other_ref
  57.6 6.1 %shared_grads.1 = (bf16[2,160,1792]{2,1,0:T(8,128)(2,1)}, bf16[2,160,1792]{2,1,0:T(8,128)(2,1)}, bf16[2,112,1280]{2,1,0:T(8,128)(2,1)}, bf16[2,112,1280]{2,1,0:T(8,128)(2,1)}) custom-call(bf16[128,5248]{1,0:T(8,128)(2,1)} %get-tuple-element.89.cat_ref, bf16[128,5248]{1,0:T(8,128)(2,1)} %collective-permute-done.other_ref, bf16[640,1280]{1,0:T(8,128)(2,1)} %fusion.order_d_ref, ...), custom_call_target="tpu_custom_call" | custom-call | flops 1 | bytes 1 | tf_op jit(solution)/shard_map/shared_grads/pallas_call | solution.py:638
  64.7 10.7 %prepare.1 = (bf16[2,8,64,128]{3,2,1,0:T(8,128)(2,1)}, f32[2,512,896]{2,1,0:T(8,128)}, bf16[2,512,1280]{2,1,0:T(8,128)(2,1)}) custom-call(s32[2]{0:T(128)} %dynamic_slice.3.ids, bf16[4,144,1280]{2,1,0:T(8,128)(2,1)} %copy-done.1, bf16[4,144,1280]{2,1,0:T(8,128)(2,1)} %copy-done.6, bf16[2,896,1280]{2,1,0:T(8,128)(2,1)} %refs_2_.3), custom_call_target="tpu_custom_call" | custom-call | flops 1 | bytes 1 | tf_op jit(solution)/shard_map/prepare/pallas_call | solution.py:118
  75.4 10.4 %collective-permute-done.5.early0_ref = bf16[4,144,1280]{2,1,0:T(8,128)(2,1)} collective-permute-done((bf16[4,144,1280]{2,1,0:T(8,128)(2,1)S(1)}, bf16[4,144,1280]{2,1,0:T(8,128)(2,1)}, u32[]{:S(2)}, u32[]{:S(2)}) %collective-permute-start.5) | collective-permute-done | bytes 1474592 | tf_op jit(solution)/shard_map/ppermute | solution.py:25
  88.1 2.2 collective-permute-done.6.ns1_ref.ns_o_ref
  91.5 22.2 %experts.1 = (bf16[4,144,1280]{2,1,0:T(8,128)(2,1)}, bf16[4,144,1280]{2,1,0:T(8,128)(2,1)}, bf16[2,512,896]{2,1,0:T(8,128)(2,1)}, bf16[2,512,896]{2,1,0:T(8,128)...) custom-call(s32[2]{0:T(128)} %dynamic_slice.3.ids, ...), custom_call_target="tpu_custom_call" | custom-call | flops 37580963840 | bytes 58720256 | tf_op jit(solution)/shard_map/experts/pallas_call | solution.py:210
  113.8 3.3 %collective-permute-done.7 = bf16[4,144,1280]{2,1,0:T(8,128)(2,1)S(1)} collective-permute-done((bf16[4,144,1280]{2,1,0:T(8,128)(2,1)}, bf16[4,144,1280]{2,1,0:T(8,128)(2,1)S(1)}, u32[]{:S(2)}, u32[]{:S(2)}) %collective-permute-start.7) | collective-permute-done | bytes 1474592 | tf_op jit(solution)/shard_map/ppermute | solution.py:25
  117.2 2.9 add_convert_fusion
  120.8 5.3 %all-to-all-start.2 = ((bf16[4,144,1280]{2,1,0:T(8,128)(2,1)}), bf16[4,144,1280]{2,1,0:T(8,128)(2,1)}, u32[]{:S(2)}, u32[]{:S(2)}) async-start(bf16[4,144,1280]{2,1,0:T(8,128)(2,1)} %add_convert_fusion), calls=%async_computation.2 | async-start | bytes 2949120 | tf_op jit(solution)/shard_map/all_to_all | solution.py:35
  126.1 1.6 collective-permute-start.10
  128.2 7.6 %combine.1 = (bf16[4,128,1280]{2,1,0:T(8,128)(2,1)}, bf16[4,128,1280]{2,1,0:T(8,128)(2,1)}) custom-call(bf16[2,512,896]{2,1,0:T(8,128)(2,1)} %get-tuple-element.107.hid_ref.refs_6_, f32[2,512,128]{2,1,0:T(8,128)} %get-tuple-element.108.row_gate_ref, bf16[2,8,64,128]{3,2,1,0:T(8,128)(2,1)} %get-tuple-element.94.pick_ref, bf16[2,896,1280]{2,1,0:T(8,128)(2,1)} %refs_2_.3), custom_call_target="tpu_custom_call" | custom-call | flops 21474836480 | bytes 25690112 | tf_op jit(solution)/shard_map/combine/pallas_call | solution.py:275
  137.0 4.2 %collective-permute-done.10 = bf16[2,112,1280]{2,1,0:T(8,128)(2,1)S(1)} collective-permute-done((bf16[2,112,1280]{2,1,0:T(8,128)(2,1)}, bf16[2,112,1280]{2,1,0:T(8,128)(2,1)S(1)}, u32[]{:S(2)}, u32[]{:S(2)}) %collective-permute-start.10) | collective-permute-done | bytes 573472 | tf_op jit(solution)/shard_map/ppermute | solution.py:25
  143.1 1.6 collective-permute-start.18
  144.7 9.9 %collective-permute-done.8 = bf16[2,160,1792]{2,1,0:T(8,128)(2,1)S(1)} collective-permute-done((bf16[2,160,1792]{2,1,0:T(8,128)(2,1)}, bf16[2,160,1792]{2,1,0:T(8,128)(2,1)S(1)}, u32[]{:S(2)}, u32[]{:S(2)}) %collective-permute-start.8) | collective-permute-done | bytes 1146912 | tf_op jit(solution)/shard_map/ppermute | solution.py:25
  155.7 1.6 add_convert_fusion.2
  157.2 5.0 %lefts.1 = (bf16[320,512]{1,0:T(8,128)(2,1)}, bf16[320,512]{1,0:T(8,128)(2,1)}, bf16[320,512]{1,0:T(8,128)(2,1)}) custom-call(bf16[5,128,1280]{2,1,0:T(8,128)(2,1)} %copy-done, bf16[5,128,1280]{2,1,0:T(8,128)(2,1)} %collective-permute-done.15.other_ref, bf16[320,1280]{1,0:T(8,128)(2,1)} %get-tuple-element.235.order_a_ref, ...), custom_call_target="tpu_custom_call" | custom-call | flops 1 | bytes 1 | tf_op jit(solution)/shard_map/lefts/pallas_call | solution.py:638
  162.7 3.1 add_convert_fusion.1
  165.9 17.0 %backward.1 = (bf16[256,1280]{1,0:T(8,128)(2,1)}, bf16[288,1280]{1,0:T(8,128)(2,1)}, f32[128,1280]{1,0:T(8,128)}) custom-call(bf16[128,1280]{1,0:T(8,128)(2,1)} %x_ref.3, bf16[128,1280]{1,0:T(8,128)(2,1)} %dy_ref.3, f32[128,1280]{1,0:T(8,128)} %get-tuple-element.86.residual_ref, bf16[128,1280]{1,0:T(8,128)(2,1)} %get-tuple-element.93.ns_ref, ...), custom_call_target="tpu_custom_call" | custom-call | flops 6710886400 | bytes 52428800 | tf_op jit(solution)/shard_map/backward/pallas_call | solution.py:601
  183.0 1.6 collective-permute-start.11
  186.0 1.5 collective-permute-start.16
  187.5 5.0 %all-to-all-start.3 = ((bf16[4,128,1280]{2,1,0:T(8,128)(2,1)}), bf16[4,128,1280]{2,1,0:T(8,128)(2,1)S(1)}, u32[]{:S(2)}, u32[]{:S(2)}) async-start(bf16[4,128,1280]{2,1,0:T(8,128)(2,1)} %add_convert_fusion.1), calls=%async_computation.3 | async-start | bytes 2621440 | tf_op jit(solution)/shard_map/all_to_all | solution.py:35
  192.6 1.6 collective-permute-done.20.ns_y_ref.ns0_ref
  195.2 20.0 %routed_grads.2 = (bf16[6720,128]{1,0:T(8,128)(2,1)}, bf16[6720,128]{1,0:T(8,128)(2,1)}) custom-call(s32[2]{0:T(128)} %dynamic_slice.3.ids, f32[2,512,128]{2,1,0:T(8,128)} %get-tuple-element.108.row_gate_ref, bf16[4,128,1280]{2,1,0:T(8,128)(2,1)} %collective-permute-done.18.ns0_ref, bf16[4,128,1280]{2,1,0:T(8,128)(2,1)} %collective-permute-done.19.ns1_ref, ...), custom_call_target="tpu_custom_call" | custom-call | flops 37580963840 | bytes 96993280 | tf_op jit(solution)/shard_map/routed_grads/pallas_call | solution.py:362
  219.9 3.8 %all-to-all-done.3 = bf16[4,128,1280]{2,1,0:T(8,128)(2,1)S(1)} async-done(((bf16[4,128,1280]{2,1,0:T(8,128)(2,1)}), bf16[4,128,1280]{2,1,0:T(8,128)(2,1)S(1)}, u32[]{:S(2)}, u32[]{:S(2)}) %all-to-all-start.3) | async-done | bytes 1310752 | tf_op jit(solution)/shard_map/all_to_all | solution.py:35
  223.7 3.8 %all-to-all-start.4 = ((bf16[4,40,3072]{2,1,0:T(8,128)(2,1)}), bf16[4,40,3072]{2,1,0:T(8,128)(2,1)S(1)}, u32[]{:S(2)}, u32[]{:S(2)}) async-start(bf16[4,40,3072]{2,1,0:T(8,128)(2,1)} %fusion.10), calls=%async_computation.4 | async-start | bytes 1966080 | tf_op jit(solution)/shard_map/all_to_all | solution.py:35
  227.5 7.6 %last_grads.1 = (bf16[160,2560]{1,0:T(8,128)(2,1)}, bf16[160,2560]{1,0:T(8,128)(2,1)}, bf16[160,2688]{1,0:T(8,128)(2,1)}, bf16[160,2688]{1,0:T(8,128)(2,1)}) custom-call(s32[1]{0:T(128)} %bitcast.9.z_ref, bf16[256,1280]{1,0:T(8,128)(2,1)} %get-tuple-element.133.mine_ref, bf16[256,1280]{1,0:T(8,128)(2,1)} %collective-permute-done.21.other_ref, ...), custom_call_target="tpu_custom_call" | custom-call | flops 1 | bytes 1 | tf_op jit(solution)/shard_map/last_grads/pallas_call | solution.py:852
  236.2 20.4 %routed_grads.3 = (bf16[6720,128]{1,0:T(8,128)(2,1)}, bf16[6720,128]{1,0:T(8,128)(2,1)}) custom-call(s32[2]{0:T(128)} %dynamic_slice.3.ids, f32[2,512,128]{2,1,0:T(8,128)} %get-tuple-element.108.row_gate_ref, bf16[4,128,1280]{2,1,0:T(8,128)(2,1)} %copy-done.8, bf16[4,128,1280]{2,1,0:T(8,128)(2,1)} %collective-permute-done.25.ns_yo_ref.ns1_ref, ...), custom_call_target="tpu_custom_call" | custom-call | flops 37580963840 | bytes 96993280 | tf_op jit(solution)/shard_map/routed_grads/pallas_call | solution.py:362
  256.6 1.7 add_convert_fusion.4
  258.5 1.4 pad_maximum_fusion
  260.9 5.0 %all-to-all-start.5 = ((bf16[4,40,5248]{2,1,0:T(8,128)(2,1)}), bf16[4,40,5248]{2,1,0:T(8,128)(2,1)S(1)}, u32[]{:S(2)}, u32[]{:S(2)}) async-start(bf16[4,40,5248]{2,1,0:T(8,128)(2,1)} %bitcast.11), calls=%async_computation.5 | async-start | bytes 3358720 | tf_op jit(solution)/shard_map/all_to_all | solution.py:35
  265.9 1.5 collective-permute-start.29
  267.4 1.5 collective-permute-start.28
  268.9 34.7 %collective-permute-done.29.refs_3_ = bf16[6720,128]{1,0:T(8,128)(2,1)} collective-permute-done((bf16[6720,128]{1,0:T(8,128)(2,1)}, bf16[6720,128]{1,0:T(8,128)(2,1)}, u32[]{:S(2)}, u32[]{:S(2)}) %collective-permute-start.29) | collective-permute-done | bytes 1720352 | tf_op jit(solution)/shard_map/ppermute | solution.py:25
  304.8 5.2 %finish.1 = (f32[2,320,896]{2,1,0:T(8,128)}, f32[2,320,896]{2,1,0:T(8,128)}, f32[2,224,1280]{2,1,0:T(8,128)}) custom-call(bf16[6720,128]{1,0:T(8,128)(2,1)} %get-tuple-element.132.refs_0_, bf16[6720,128]{1,0:T(8,128)(2,1)} %collective-permute-done.28.refs_1_, bf16[6720,128]{1,0:T(8,128)(2,1)} %get-tuple-element.144.refs_2_, ...), custom_call_target="tpu_custom_call" | custom-call | tf_op jit(solution)/shard_map/finish/pallas_call | solution.py:420
  310.1 1.4 add_bitcast_fusion.1
  (155 shorter events, 33.4 us)
Async XLA Ops:
  3.5 41.2 %all-to-all-start = ((bf16[4,144,1280]{2,1,0:T(8,128)(2,1)}), bf16[4,144,1280]{2,1,0:T(8,128)(2,1)S(1)}, u32[]{:S(2)}, u32[]{:S(2)}) async-start(bf16[4,144,1280]{2,1,0:T(8,128)(2,1)} %broadcast_in_dim.8), calls=%async_computation | async-start | bytes 2949120 | tf_op jit(solution)/shard_map/all_to_all | solution.py:35
  9.9 14.4 %copy-start.33 = (s32[448]{0:T(512)S(1)}, s32[448]{0:T(512)}, u32[]{:S(2)}) copy-start(s32[448]{0:T(512)} %constant.100.clone) | copy-start | bytes 5380
  9.9 14.4 %copy-start.24 = (s32[640]{0:T(1024)S(1)}, s32[640]{0:T(1024)}, u32[]{:S(2)}) copy-start(s32[640]{0:T(1024)} %constant.93.clone) | copy-start | bytes 7684
  9.9 14.4 %copy-start.25 = (s32[640]{0:T(1024)S(1)}, s32[640]{0:T(1024)}, u32[]{:S(2)}) copy-start(s32[640]{0:T(1024)} %constant.92.clone) | copy-start | bytes 7684
  9.9 14.4 %copy-start.26 = (s32[640]{0:T(1024)S(1)}, s32[640]{0:T(1024)}, u32[]{:S(2)}) copy-start(s32[640]{0:T(1024)} %constant.91.clone) | copy-start | bytes 7684
  9.9 14.4 %copy-start.27 = (s32[320]{0:T(512)S(1)}, s32[320]{0:T(512)}, u32[]{:S(2)}) copy-start(s32[320]{0:T(512)} %constant.97.clone) | copy-start | bytes 3844
  9.9 14.4 %copy-start.28 = (s32[320]{0:T(512)S(1)}, s32[320]{0:T(512)}, u32[]{:S(2)}) copy-start(s32[320]{0:T(512)} %constant.96.clone) | copy-start | bytes 3844
  9.9 14.4 %copy-start.29 = (s32[320]{0:T(512)S(1)}, s32[320]{0:T(512)}, u32[]{:S(2)}) copy-start(s32[320]{0:T(512)} %constant.95.clone) | copy-start | bytes 3844
  10.0 14.4 %copy-start.30 = (s32[320]{0:T(512)S(1)}, s32[320]{0:T(512)}, u32[]{:S(2)}) copy-start(s32[320]{0:T(512)} %constant.94.clone) | copy-start | bytes 3844
  19.9 19.8 %collective-permute-start.1 = (bf16[128,1280]{1,0:T(8,128)(2,1)}, bf16[128,1280]{1,0:T(8,128)(2,1)S(1)}, u32[]{:S(2)}, u32[]{:S(2)}) collective-permute-start(bf16[128,1280]{1,0:T(8,128)(2,1)} %get-tuple-element.91), channel_id=1, source_target_pairs={{0,8},{8,0},{16,24},{24,16},{1,9},{9,1},{17,25},{25,17},{2,10},{10... | collective-permute-start | bytes 983048 | tf_op jit(solution)/shard_map/ppermute | solution.py:25
  22.6 17.1 %collective-permute-start.2 = (bf16[2,128,1280]{2,1,0:T(8,128)(2,1)S(1)}, bf16[2,128,1280]{2,1,0:T(8,128)(2,1)S(1)}, u32[]{:S(2)}, u32[]{:S(2)}) collective-permute-start(bf16[2,128,1280]{2,1,0:T(8,128)(2,1)S(1)} %pad_maximum_fusion.2), channel_id=1, source_target_pairs={{0,16},{8,24},{16,0},{24,8},{1,17},{9,25},{17,1},{25,9},{2,18},{10... | collective-permute-start | bytes 1966088 | tf_op jit(solution)/shard_map/ppermute | solution.py:25
  46.0 41.1 %all-to-all-start.1 = ((bf16[4,128,1280]{2,1,0:T(8,128)(2,1)}), bf16[4,128,1280]{2,1,0:T(8,128)(2,1)}, u32[]{:S(2)}, u32[]{:S(2)}) async-start(bf16[4,128,1280]{2,1,0:T(8,128)(2,1)} %broadcast_in_dim.9), calls=%async_computation.1 | async-start | bytes 2621440 | tf_op jit(solution)/shard_map/all_to_all | solution.py:35
  51.0 12.6 %collective-permute-start.3 = (bf16[4,144,1280]{2,1,0:T(8,128)(2,1)S(1)}, bf16[4,144,1280]{2,1,0:T(8,128)(2,1)S(1)}, u32[]{:S(2)}, u32[]{:S(2)}) collective-permute-start(bf16[4,144,1280]{2,1,0:T(8,128)(2,1)S(1)} %all-to-all-done.early_ref), channel_id=1, source_target_pairs={{0,1},{1,0},{2,3},{3,2},{4,5},{5,4},{6,7},{7,6},{8,9},{9,8},{10,11... | collective-permute-start | bytes 4423688 | tf_op jit(solution)/shard_map/ppermute | solution.py:25
  51.1 34.8 %collective-permute-start.5 = (bf16[4,144,1280]{2,1,0:T(8,128)(2,1)S(1)}, bf16[4,144,1280]{2,1,0:T(8,128)(2,1)}, u32[]{:S(2)}, u32[]{:S(2)}) collective-permute-start(bf16[4,144,1280]{2,1,0:T(8,128)(2,1)S(1)} %all-to-all-done.early_ref), channel_id=1, source_target_pairs={{0,16},{8,24},{16,0},{24,8},{1,17},{9,25},{17,1},{25,9},{2,18},{10... | collective-permute-start | bytes 4423688 | tf_op jit(solution)/shard_map/ppermute | solution.py:25
  52.6 34.5 %collective-permute-start.4 = (bf16[4,144,1280]{2,1,0:T(8,128)(2,1)S(1)}, bf16[4,144,1280]{2,1,0:T(8,128)(2,1)}, u32[]{:S(2)}, u32[]{:S(2)}) collective-permute-start(bf16[4,144,1280]{2,1,0:T(8,128)(2,1)S(1)} %all-to-all-done.early_ref), channel_id=1, source_target_pairs={{0,8},{8,0},{16,24},{24,16},{1,9},{9,1},{17,25},{25,17},{2,10},{10... | collective-permute-start | bytes 4423688 | tf_op jit(solution)/shard_map/ppermute | solution.py:25
  54.1 3.4 %collective-permute-start = (bf16[128,5248]{1,0:T(8,128)(2,1)}, bf16[128,5248]{1,0:T(8,128)(2,1)}, u32[]{:S(2)}, u32[]{:S(2)}) collective-permute-start(bf16[128,5248]{1,0:T(8,128)(2,1)} %get-tuple-element.89.cat_ref), channel_id=1, source_target_pairs={{0,1},{1,0},{2,3},{3,2},{4,5},{5,4},{6,7},{7,6},{8,9},{9,8},{10,11... | collective-permute-start | bytes 4030472 | tf_op jit(solution)/shard_map/ppermute | solution.py:25
  63.6 23.5 %copy-start.22 = (bf16[1280,15]{0,1:T(8,128)(2,1)S(1)}, bf16[1280,15]{0,1:T(8,128)(2,1)}, u32[]{:S(2)}) copy-start(bf16[1280,15]{0,1:T(8,128)(2,1)} %param.45) | copy-start | bytes 115204
  87.1 3.2 %collective-permute-start.6 = (bf16[4,128,1280]{2,1,0:T(8,128)(2,1)}, bf16[4,128,1280]{2,1,0:T(8,128)(2,1)S(1)}, u32[]{:S(2)}, u32[]{:S(2)}) collective-permute-start(bf16[4,128,1280]{2,1,0:T(8,128)(2,1)} %all-to-all-done.1.ns0_ref), channel_id=1, source_target_pairs={{0,1},{1,0},{2,3},{3,2},{4,5},{5,4},{6,7},{7,6},{8,9},{9,8},{10,11... | collective-permute-start | bytes 3932168 | tf_op jit(solution)/shard_map/ppermute | solution.py:25
  113.6 3.5 %collective-permute-start.7 = (bf16[4,144,1280]{2,1,0:T(8,128)(2,1)}, bf16[4,144,1280]{2,1,0:T(8,128)(2,1)S(1)}, u32[]{:S(2)}, u32[]{:S(2)}) collective-permute-start(bf16[4,144,1280]{2,1,0:T(8,128)(2,1)} %get-tuple-element.100), channel_id=1, source_target_pairs={{0,1},{1,0},{2,3},{3,2},{4,5},{5,4},{6,7},{7,6},{8,9},{9,8},{10,11... | collective-permute-start | bytes 4423688 | tf_op jit(solution)/shard_map/ppermute | solution.py:25
  120.1 8.1 %collective-permute-start.12 = (bf16[4,144,1280]{2,1,0:T(8,128)(2,1)}, bf16[4,144,1280]{2,1,0:T(8,128)(2,1)}, u32[]{:S(2)}, u32[]{:S(2)}) collective-permute-start(bf16[4,144,1280]{2,1,0:T(8,128)(2,1)} %collective-permute-done.4.early0_ref), channel_id=1, source_target_pairs={{0,1},{1,0},{2,3},{3,2},{4,5},{5,4},{6,7},{7,6},{8,9},{9,8},{10,11... | collective-permute-start | bytes 4423688 | tf_op jit(solution)/shard_map/ppermute | solution.py:25
  120.2 7.9 %collective-permute-start.13 = (bf16[4,144,1280]{2,1,0:T(8,128)(2,1)}, bf16[4,144,1280]{2,1,0:T(8,128)(2,1)}, u32[]{:S(2)}, u32[]{:S(2)}) collective-permute-start(bf16[4,144,1280]{2,1,0:T(8,128)(2,1)} %collective-permute-done.5.early0_ref), channel_id=1, source_target_pairs={{0,1},{1,0},{2,3},{3,2},{4,5},{5,4},{6,7},{7,6},{8,9},{9,8},{10,11... | collective-permute-start | bytes 4423688 | tf_op jit(solution)/shard_map/ppermute | solution.py:25
  120.8 15.0 %copy-start = (bf16[5,128,1280]{2,1,0:T(8,128)(2,1)}, bf16[5,128,1280]{2,1,0:T(8,128)(2,1)S(1)}, u32[]{:S(2)}) copy-start(bf16[5,128,1280]{2,1,0:T(8,128)(2,1)S(1)} %pad_maximum_fusion.1.mine_ref) | copy-start | bytes 4915204
  120.8 45.0 %all-to-all-start.2 = ((bf16[4,144,1280]{2,1,0:T(8,128)(2,1)}), bf16[4,144,1280]{2,1,0:T(8,128)(2,1)}, u32[]{:S(2)}, u32[]{:S(2)}) async-start(bf16[4,144,1280]{2,1,0:T(8,128)(2,1)} %add_convert_fusion), calls=%async_computation.2 | async-start | bytes 2949120 | tf_op jit(solution)/shard_map/all_to_all | solution.py:35
  126.1 15.0 %collective-permute-start.10 = (bf16[2,112,1280]{2,1,0:T(8,128)(2,1)}, bf16[2,112,1280]{2,1,0:T(8,128)(2,1)S(1)}, u32[]{:S(2)}, u32[]{:S(2)}) collective-permute-start(bf16[2,112,1280]{2,1,0:T(8,128)(2,1)} %get-tuple-element.103), channel_id=1, source_target_pairs={{0,8},{8,0},{16,24},{24,16},{1,9},{9,1},{17,25},{25,17},{2,10},{10... | collective-permute-start | bytes 1720328 | tf_op jit(solution)/shard_map/ppermute | solution.py:25
  127.6 27.0 %collective-permute-start.8 = (bf16[2,160,1792]{2,1,0:T(8,128)(2,1)}, bf16[2,160,1792]{2,1,0:T(8,128)(2,1)S(1)}, u32[]{:S(2)}, u32[]{:S(2)}) collective-permute-start(bf16[2,160,1792]{2,1,0:T(8,128)(2,1)} %get-tuple-element.101), channel_id=1, source_target_pairs={{0,16},{8,24},{16,0},{24,8},{1,17},{9,25},{17,1},{25,9},{2,18},{10... | collective-permute-start | bytes 3440648 | tf_op jit(solution)/shard_map/ppermute | solution.py:25
  128.2 29.1 %collective-permute-start.15 = (bf16[5,128,1280]{2,1,0:T(8,128)(2,1)S(1)}, bf16[5,128,1280]{2,1,0:T(8,128)(2,1)}, u32[]{:S(2)}, u32[]{:S(2)}) collective-permute-start(bf16[5,128,1280]{2,1,0:T(8,128)(2,1)S(1)} %pad_maximum_fusion.1.mine_ref), channel_id=1, source_target_pairs={{0,1},{1,0},{2,3},{3,2},{4,5},{5,4},{6,7},{7,6},{8,9},{9,8},{10,11... | collective-permute-start | bytes 4915208 | tf_op jit(solution)/shard_map/ppermute | solution.py:25
  135.8 19.9 %copy-start.11 = (bf16[2,160,1792]{2,1,0:T(8,128)(2,1)S(1)}, bf16[2,160,1792]{2,1,0:T(8,128)(2,1)}, u32[]{:S(2)}) copy-start(bf16[2,160,1792]{2,1,0:T(8,128)(2,1)} %get-tuple-element.90) | copy-start | bytes 3440644
  135.8 26.9 %collective-permute-start.14 = (bf16[4,128,1280]{2,1,0:T(8,128)(2,1)}, bf16[4,128,1280]{2,1,0:T(8,128)(2,1)}, u32[]{:S(2)}, u32[]{:S(2)}) collective-permute-start(bf16[4,128,1280]{2,1,0:T(8,128)(2,1)} %get-tuple-element.110), channel_id=1, source_target_pairs={{0,1},{1,0},{2,3},{3,2},{4,5},{5,4},{6,7},{7,6},{8,9},{9,8},{10,11... | collective-permute-start | bytes 3932168 | tf_op jit(solution)/shard_map/ppermute | solution.py:25
  143.1 39.8 %collective-permute-start.18 = (bf16[4,128,1280]{2,1,0:T(8,128)(2,1)}, bf16[4,128,1280]{2,1,0:T(8,128)(2,1)}, u32[]{:S(2)}, u32[]{:S(2)}) collective-permute-start(bf16[4,128,1280]{2,1,0:T(8,128)(2,1)} %all-to-all-done.1.ns0_ref), channel_id=1, source_target_pairs={{0,8},{8,0},{16,24},{24,16},{1,9},{9,1},{17,25},{25,17},{2,10},{10... | collective-permute-start | bytes 3932168 | tf_op jit(solution)/shard_map/ppermute | solution.py:25
  157.2 27.4 %copy-start.2 = (bf16[2,160,1792]{2,1,0:T(8,128)(2,1)}, bf16[2,160,1792]{2,1,0:T(8,128)(2,1)S(1)}, u32[]{:S(2)}) copy-start(bf16[2,160,1792]{2,1,0:T(8,128)(2,1)S(1)} %add_convert_fusion.2) | copy-start | bytes 3440644
  162.2 31.9 %collective-permute-start.20 = (bf16[4,128,1280]{2,1,0:T(8,128)(2,1)}, bf16[4,128,1280]{2,1,0:T(8,128)(2,1)S(1)}, u32[]{:S(2)}, u32[]{:S(2)}) collective-permute-start(bf16[4,128,1280]{2,1,0:T(8,128)(2,1)} %all-to-all-done.1.ns0_ref), channel_id=1, source_target_pairs={{0,16},{8,24},{16,0},{24,8},{1,17},{9,25},{17,1},{25,9},{2,18},{10... | collective-permute-start | bytes 3932168 | tf_op jit(solution)/shard_map/ppermute | solution.py:25
  182.9 11.7 %collective-permute-start.19 = (bf16[4,128,1280]{2,1,0:T(8,128)(2,1)}, bf16[4,128,1280]{2,1,0:T(8,128)(2,1)}, u32[]{:S(2)}, u32[]{:S(2)}) collective-permute-start(bf16[4,128,1280]{2,1,0:T(8,128)(2,1)} %collective-permute-done.18.ns0_ref), channel_id=1, source_target_pairs={{0,1},{1,0},{2,3},{3,2},{4,5},{5,4},{6,7},{7,6},{8,9},{9,8},{10,11... | collective-permute-start | bytes 3932168 | tf_op jit(solution)/shard_map/ppermute | solution.py:25
  183.0 32.3 %collective-permute-start.11 = (bf16[112,1280]{1,0:T(8,128)(2,1)S(1)}, bf16[112,1280]{1,0:T(8,128)(2,1)}, u32[]{:S(2)}, u32[]{:S(2)}) collective-permute-start(bf16[112,1280]{1,0:T(8,128)(2,1)S(1)} %slice_bitcast_fusion.2), channel_id=1, source_target_pairs={{0,16},{8,24},{16,0},{24,8},{1,17},{9,25},{17,1},{25,9},{2,18},{10... | collective-permute-start | bytes 860168 | tf_op jit(solution)/shard_map/ppermute | solution.py:25
  185.5 31.0 %collective-permute-start.9 = (bf16[160,1792]{1,0:T(8,128)(2,1)}, bf16[160,1792]{1,0:T(8,128)(2,1)}, u32[]{:S(2)}, u32[]{:S(2)}) collective-permute-start(bf16[160,1792]{1,0:T(8,128)(2,1)} %slice_bitcast_fusion), channel_id=1, source_target_pairs={{0,8},{8,0},{16,24},{24,16},{1,9},{9,1},{17,25},{25,17},{2,10},{10... | collective-permute-start | bytes 1720328 | tf_op jit(solution)/shard_map/ppermute | solution.py:25
  186.0 30.5 %collective-permute-start.16 = (bf16[256,1280]{1,0:T(8,128)(2,1)}, bf16[256,1280]{1,0:T(8,128)(2,1)}, u32[]{:S(2)}, u32[]{:S(2)}) collective-permute-start(bf16[256,1280]{1,0:T(8,128)(2,1)} %get-tuple-element.133.mine_ref), channel_id=1, source_target_pairs={{0,8},{8,0},{16,24},{24,16},{1,9},{9,1},{17,25},{25,17},{2,10},{10... | collective-permute-start | bytes 1966088 | tf_op jit(solution)/shard_map/ppermute | solution.py:25
  187.5 36.2 %all-to-all-start.3 = ((bf16[4,128,1280]{2,1,0:T(8,128)(2,1)}), bf16[4,128,1280]{2,1,0:T(8,128)(2,1)S(1)}, u32[]{:S(2)}, u32[]{:S(2)}) async-start(bf16[4,128,1280]{2,1,0:T(8,128)(2,1)} %add_convert_fusion.1), calls=%async_computation.3 | async-start | bytes 2621440 | tf_op jit(solution)/shard_map/all_to_all | solution.py:35
  194.1 22.4 %collective-permute-start.17 = (bf16[288,1280]{1,0:T(8,128)(2,1)}, bf16[288,1280]{1,0:T(8,128)(2,1)}, u32[]{:S(2)}, u32[]{:S(2)}) collective-permute-start(bf16[288,1280]{1,0:T(8,128)(2,1)} %get-tuple-element.134.rest_ref), channel_id=1, source_target_pairs={{0,16},{8,24},{16,0},{24,8},{1,17},{9,25},{17,1},{25,9},{2,18},{10... | collective-permute-start | bytes 2211848 | tf_op jit(solution)/shard_map/ppermute | solution.py:25
  215.3 12.2 %collective-permute-start.25 = (bf16[4,128,1280]{2,1,0:T(8,128)(2,1)}, bf16[4,128,1280]{2,1,0:T(8,128)(2,1)}, u32[]{:S(2)}, u32[]{:S(2)}) collective-permute-start(bf16[4,128,1280]{2,1,0:T(8,128)(2,1)} %copy-done.8), channel_id=1, source_target_pairs={{0,1},{1,0},{2,3},{3,2},{4,5},{5,4},{6,7},{7,6},{8,9},{9,8},{10,11... | collective-permute-start | bytes 3932168 | tf_op jit(solution)/shard_map/ppermute | solution.py:25
  216.6 10.9 %collective-permute-start.21 = (bf16[256,1280]{1,0:T(8,128)(2,1)}, bf16[256,1280]{1,0:T(8,128)(2,1)}, u32[]{:S(2)}, u32[]{:S(2)}) collective-permute-start(bf16[256,1280]{1,0:T(8,128)(2,1)} %get-tuple-element.133.mine_ref), channel_id=1, source_target_pairs={{0,1},{1,0},{2,3},{3,2},{4,5},{5,4},{6,7},{7,6},{8,9},{9,8},{10,11... | collective-permute-start | bytes 1966088 | tf_op jit(solution)/shard_map/ppermute | solution.py:25
  217.0 10.4 %collective-permute-start.23 = (bf16[256,1280]{1,0:T(8,128)(2,1)}, bf16[256,1280]{1,0:T(8,128)(2,1)}, u32[]{:S(2)}, u32[]{:S(2)}) collective-permute-start(bf16[256,1280]{1,0:T(8,128)(2,1)} %collective-permute-done.16.qx_ref), channel_id=1, source_target_pairs={{0,1},{1,0},{2,3},{3,2},{4,5},{5,4},{6,7},{7,6},{8,9},{9,8},{10,11... | collective-permute-start | bytes 1966088 | tf_op jit(solution)/shard_map/ppermute | solution.py:25
  217.1 10.4 %collective-permute-start.22 = (bf16[288,1280]{1,0:T(8,128)(2,1)}, bf16[288,1280]{1,0:T(8,128)(2,1)}, u32[]{:S(2)}, u32[]{:S(2)}) collective-permute-start(bf16[288,1280]{1,0:T(8,128)(2,1)} %get-tuple-element.134.rest_ref), channel_id=1, source_target_pairs={{0,1},{1,0},{2,3},{3,2},{4,5},{5,4},{6,7},{7,6},{8,9},{9,8},{10,11... | collective-permute-start | bytes 2211848 | tf_op jit(solution)/shard_map/ppermute | solution.py:25
  217.6 9.9 %collective-permute-start.24 = (bf16[288,1280]{1,0:T(8,128)(2,1)}, bf16[288,1280]{1,0:T(8,128)(2,1)}, u32[]{:S(2)}, u32[]{:S(2)}) collective-permute-start(bf16[288,1280]{1,0:T(8,128)(2,1)} %collective-permute-done.17.by_ref), channel_id=1, source_target_pairs={{0,1},{1,0},{2,3},{3,2},{4,5},{5,4},{6,7},{7,6},{8,9},{9,8},{10,11... | collective-permute-start | bytes 2211848 | tf_op jit(solution)/shard_map/ppermute | solution.py:25
  223.7 36.2 %all-to-all-start.4 = ((bf16[4,40,3072]{2,1,0:T(8,128)(2,1)}), bf16[4,40,3072]{2,1,0:T(8,128)(2,1)S(1)}, u32[]{:S(2)}, u32[]{:S(2)}) async-start(bf16[4,40,3072]{2,1,0:T(8,128)(2,1)} %fusion.10), calls=%async_computation.4 | async-start | bytes 1966080 | tf_op jit(solution)/shard_map/all_to_all | solution.py:35
  235.2 21.5 %collective-permute-start.26 = (bf16[160,2560]{1,0:T(8,128)(2,1)}, bf16[160,2560]{1,0:T(8,128)(2,1)}, u32[]{:S(2)}, u32[]{:S(2)}) collective-permute-start(bf16[160,2560]{1,0:T(8,128)(2,1)} %get-tuple-element.141), channel_id=1, source_target_pairs={{0,16},{8,24},{16,0},{24,8},{1,17},{9,25},{17,1},{25,9},{2,18},{10... | collective-permute-start | bytes 2457608 | tf_op jit(solution)/shard_map/ppermute | solution.py:25
  235.7 22.6 %collective-permute-start.27 = (bf16[160,2688]{1,0:T(8,128)(2,1)}, bf16[160,2688]{1,0:T(8,128)(2,1)S(1)}, u32[]{:S(2)}, u32[]{:S(2)}) collective-permute-start(bf16[160,2688]{1,0:T(8,128)(2,1)} %get-tuple-element.147), channel_id=1, source_target_pairs={{0,8},{8,0},{16,24},{24,16},{1,9},{9,1},{17,25},{25,17},{2,10},{10... | collective-permute-start | bytes 2580488 | tf_op jit(solution)/shard_map/ppermute | solution.py:25
  260.9 49.2 %all-to-all-start.5 = ((bf16[4,40,5248]{2,1,0:T(8,128)(2,1)}), bf16[4,40,5248]{2,1,0:T(8,128)(2,1)S(1)}, u32[]{:S(2)}, u32[]{:S(2)}) async-start(bf16[4,40,5248]{2,1,0:T(8,128)(2,1)} %bitcast.11), calls=%async_computation.5 | async-start | bytes 3358720 | tf_op jit(solution)/shard_map/all_to_all | solution.py:35
  265.9 37.7 %collective-permute-start.29 = (bf16[6720,128]{1,0:T(8,128)(2,1)}, bf16[6720,128]{1,0:T(8,128)(2,1)}, u32[]{:S(2)}, u32[]{:S(2)}) collective-permute-start(bf16[6720,128]{1,0:T(8,128)(2,1)} %get-tuple-element.153), channel_id=1, source_target_pairs={{0,8},{8,0},{16,24},{24,16},{1,9},{9,1},{17,25},{25,17},{2,10},{10... | collective-permute-start | bytes 5160968 | tf_op jit(solution)/shard_map/ppermute | solution.py:25
  267.4 37.5 %collective-permute-start.28 = (bf16[6720,128]{1,0:T(8,128)(2,1)}, bf16[6720,128]{1,0:T(8,128)(2,1)}, u32[]{:S(2)}, u32[]{:S(2)}) collective-permute-start(bf16[6720,128]{1,0:T(8,128)(2,1)} %get-tuple-element.152), channel_id=1, source_target_pairs={{0,16},{8,24},{16,0},{24,8},{1,17},{9,25},{17,1},{25,9},{2,18},{10... | collective-permute-start | bytes 5160968 | tf_op jit(solution)/shard_map/ppermute | solution.py:25
  (23 other events, 115.9 us)
